TPU v7x, 32 devices: a whole 2x2x4 slice. The times are simulated.
32 devices in a mesh: rep: 4 (over y, x), fsdp: 8 (over z, core).
Axes of the slice: x: 2, y: 2, z: 4, core: 2. Of those that a mesh axis runs over, the one named last changes fastest.
Arguments:
- tokens: bfloat16 [2, 32, 512, 768], P(None, ('rep', 'fsdp')), may hold values from -6 to 6
- lengths: int32 [2, 32], P(None, ('rep', 'fsdp')), may hold values from 128 to 512, as said below
- boundary: int32 [2, 32], P(None, ('rep', 'fsdp')), may hold values from 1 to 511, as said below
- w_query: bfloat16 [768, 768], P('fsdp'), may hold values from -0.21875 to 0.21875
- b_query: bfloat16 [768], P('fsdp'), may hold values from -2.5 to 2.5
- w_key: bfloat16 [768, 768], P('fsdp'), may hold values from -0.21875 to 0.21875
- b_key: bfloat16 [768], P('fsdp'), may hold values from -2.5 to 2.5
- w_value: bfloat16 [768, 768], P('fsdp'), may hold values from -0.21875 to 0.21875
- b_value: bfloat16 [768], P('fsdp'), may hold values from -2.5 to 2.5
- w_out: bfloat16 [768, 768], P('fsdp'), may hold values from -1.75 to 1.75
- b_out: bfloat16 [768], P('fsdp'), may hold values from -2.5 to 2.5
- first_gain: bfloat16 [768], P('fsdp'), may hold values from 0.5 to 1.5
- first_shift: bfloat16 [768], P('fsdp'), may hold values from -2.5 to 2.5
- w_up: bfloat16 [768, 3072], P('fsdp'), may hold values from -0.21875 to 0.21875
- b_up: bfloat16 [3072], P('fsdp'), may hold values from -2.5 to 2.5
- w_down: bfloat16 [3072, 768], P('fsdp'), may hold values from -0.109375 to 0.109375
- b_down: bfloat16 [768], P('fsdp'), may hold values from -2.5 to 2.5
- second_gain: bfloat16 [768], P('fsdp'), may hold values from 0.5 to 1.5
- second_shift: bfloat16 [768], P('fsdp'), may hold values from -2.5 to 2.5
- rel_table: bfloat16 [512, 768], P('fsdp'), may hold values from -6 to 6
- type_table: bfloat16 [2, 768], P(None, 'fsdp'), may hold values from -3 to 3
- out_grad: bfloat16 [2, 32, 512, 768], P(None, ('rep', 'fsdp')), may hold values from -6 to 6
Outputs:
- layer_out: bfloat16 [2, 32, 512, 768], P(None, ('rep', 'fsdp'))
- tokens_grad: bfloat16 [2, 32, 512, 768], P(None, ('rep', 'fsdp'))
- grad_w_query: float32 [768, 768], P('fsdp')
- grad_b_query: float32 [768], P('fsdp')
- grad_w_key: float32 [768, 768], P('fsdp')
- grad_b_key: float32 [768], P('fsdp')
- grad_w_value: float32 [768, 768], P('fsdp')
- grad_b_value: float32 [768], P('fsdp')
- grad_w_out: float32 [768, 768], P('fsdp')
- grad_b_out: float32 [768], P('fsdp')
- grad_first_gain: float32 [768], P('fsdp')
- grad_first_shift: float32 [768], P('fsdp')
- grad_w_up: float32 [768, 3072], P('fsdp')
- grad_b_up: float32 [3072], P('fsdp')
- grad_w_down: float32 [3072, 768], P('fsdp')
- grad_b_down: float32 [768], P('fsdp')
- grad_second_gain: float32 [768], P('fsdp')
- grad_second_shift: float32 [768], P('fsdp')
- grad_rel_table: float32 [512, 768], P('fsdp')
- grad_type_table: float32 [2, 768], P(None, 'fsdp')
Inputs may be any that keep to these rules, and one draw needn't show every extreme that they name: `lengths`: each sequence's valid tokens come first; the largest entry is exactly 512 and the smallest exactly 128 in every draw. `boundary`: lies below its sequence's valid length; both ends of the range are reached in every draw.
All inputs are finite; a program needn't handle non-finite values.
Results may differ from a plain program's by a relative error of at most 0.03.
Values may be sent and summed in bfloat16 or wider, within the bound.
No kernel may reach another device: no remote copies, remote signals or barrier semaphores. Data moves between devices by JAX's collectives and lax.ppermute only.
A program may use at most 320 MiB of HBM per device.

v0:
```python
import math

import jax
import jax.numpy as jnp
import numpy as np
from jax import lax
from jax.sharding import PartitionSpec as P

HEADS = 12
HEAD_DIM = 64
BUCKETS = 256
MAX_POS = 512


NORM_EPS = 1e-07
MASKED = -1e30


def bucket_index(offset_of):
    middle = BUCKETS // 2
    sign_of = np.sign(offset_of)
    magnitude = np.where(
        (offset_of < middle) & (offset_of > -middle), middle - 1, np.abs(offset_of)
    )
    log_pos = (
        np.ceil(np.log(magnitude / middle) / np.log((MAX_POS - 1) / middle) * (middle - 1)) + middle
    )
    bucket = np.where(magnitude <= middle, offset_of, log_pos * sign_of)
    return np.clip(bucket + BUCKETS, 0, 2 * BUCKETS - 1)


def offset_tables(seq_len):
    offsets = np.arange(2 * seq_len)
    table_rows = np.arange(2 * BUCKETS)
    from_query = bucket_index(seq_len - 1 - offsets)
    from_key = bucket_index(offsets - seq_len + 1)
    pick_query = (from_query[:, None] == table_rows[None, :]).astype(np.float32)
    pick_key = (from_key[:, None] == table_rows[None, :]).astype(np.float32)
    return (pick_query, pick_key)


def realign(scores_block):
    leading = scores_block.shape[:-2]
    row_count = scores_block.shape[-2]
    columns = scores_block.shape[-1]
    flattened = scores_block.reshape(leading + (row_count * columns,))
    flattened = flattened[..., row_count - 1 : row_count - 1 + row_count * (columns - 1)]
    return flattened.reshape(leading + (row_count, columns - 1))[..., :row_count]


def realign_back(gradient):
    row_count = gradient.shape[-2]
    wide_shape = gradient.shape[:-1] + (2 * row_count,)
    unused, pull_back = jax.vjp(realign, jnp.zeros(wide_shape, gradient.dtype))
    return pull_back(gradient)[0]


def normalize(values):
    centred = values - jnp.mean(values, -1, keepdims=True)
    inverse = lax.rsqrt(jnp.mean(centred * centred, -1, keepdims=True) + NORM_EPS)
    return (centred * inverse, inverse)


def normalize_back(grad_normed, normed, inverse):
    return inverse * (
        grad_normed
        - jnp.mean(grad_normed, -1, keepdims=True)
        - normed * jnp.mean(grad_normed * normed, -1, keepdims=True)
    )


def gelu_slope(values):
    cumulative = 0.5 * (1.0 + lax.erf(values * (1.0 / math.sqrt(2.0))))
    density = jnp.exp(-0.5 * values * values) * (1.0 / math.sqrt(2.0 * math.pi))
    return cumulative + values * density


def project(left_side, weight):
    return jnp.dot(left_side, weight, preferred_element_type=jnp.float32)


def outer_sum(left_side, right_side):
    return lax.dot_general(
        left_side, right_side, (((0,), (0,)), ((), ())), preferred_element_type=jnp.float32
    )


def back_project(gradient, weight):
    return lax.dot_general(
        gradient, weight, (((1,), (1,)), ((), ())), preferred_element_type=jnp.float32
    )


def exact_outer(left_side, right_side):
    return lax.dot_general(
        left_side,
        right_side,
        (((0,), (0,)), ((), ())),
        precision=lax.Precision.HIGHEST,
        preferred_element_type=jnp.float32,
    )


def exact_back(gradient, weight):
    return lax.dot_general(
        gradient,
        weight,
        (((1,), (1,)), ((), ())),
        precision=lax.Precision.HIGHEST,
        preferred_element_type=jnp.float32,
    )


def to_heads(values, seq_count):
    return values.reshape(seq_count, -1, HEADS, HEAD_DIM).transpose(0, 2, 1, 3)


def from_heads(values):
    seq_count, head_count, seq_len, head_dim = values.shape
    return values.transpose(0, 2, 1, 3).reshape(seq_count * seq_len, head_count * head_dim)


def table_heads(values):
    return values.reshape(values.shape[0], HEADS, HEAD_DIM).transpose(1, 0, 2)


def table_flat(values):
    return values.transpose(1, 0, 2).reshape(values.shape[1], -1)


def head_scores(query_seq, key_seq, key_table, query_table, key_valid):
    direct = jnp.einsum("hid,hjd->hij", query_seq, key_seq, preferred_element_type=jnp.float32)
    from_query = realign(
        jnp.einsum("hid,hkd->hik", query_seq, key_table, preferred_element_type=jnp.float32)
    )
    from_key = jnp.swapaxes(
        realign(
            jnp.einsum("hjd,hkd->hjk", key_seq, query_table, preferred_element_type=jnp.float32)
        ),
        -1,
        -2,
    )
    scaling = 1.0 / math.sqrt(3 * query_seq.shape[-1])
    return jnp.where(key_valid[None, None, :], (direct + from_query + from_key) * scaling, MASKED)


def attend(queries, key_heads, value_heads, key_table, query_table, lengths):
    positions = jnp.arange(queries.shape[2])

    def one_sequence(per_sequence):
        query_seq, key_seq, value_seq, length_one = per_sequence
        key_valid = positions < length_one
        query_valid = key_valid.astype(jnp.float32)[None, :, None]
        scores = head_scores(query_seq, key_seq, key_table, query_table, key_valid)
        row_peak = jnp.max(scores, -1, keepdims=True)
        exponent = jnp.exp(scores - row_peak)
        row_total = jnp.sum(exponent, -1, keepdims=True)
        probs_low = (exponent / row_total * query_valid).astype(jnp.bfloat16)
        context = jnp.einsum(
            "hij,hjd->hid", probs_low, value_seq, preferred_element_type=jnp.float32
        )
        return (context.astype(jnp.bfloat16), (row_peak + jnp.log(row_total))[..., 0])

    return lax.map(one_sequence, (queries, key_heads, value_heads, lengths))


def attend_back(
    queries, key_heads, value_heads, key_table, query_table, lengths, log_total, grad_context
):
    positions = jnp.arange(queries.shape[2])

    def one_sequence(running, per_sequence):
        query_seq, key_seq, value_seq, length_one, total_seq, grad_seq = per_sequence
        key_valid = positions < length_one
        query_valid = key_valid.astype(jnp.float32)[None, :, None]
        scores = head_scores(query_seq, key_seq, key_table, query_table, key_valid)
        soft_probs = jnp.exp(scores - total_seq[..., None])
        probs_low = (soft_probs * query_valid).astype(jnp.bfloat16)
        grad_value = jnp.einsum(
            "hij,hid->hjd", probs_low, grad_seq, preferred_element_type=jnp.float32
        )
        grad_soft = (
            jnp.einsum("hid,hjd->hij", grad_seq, value_seq, preferred_element_type=jnp.float32)
            * query_valid
        )
        scaling = 1.0 / math.sqrt(3 * query_seq.shape[-1])
        grad_raw = (
            soft_probs * (grad_soft - jnp.sum(grad_soft * soft_probs, -1, keepdims=True)) * scaling
        ).astype(jnp.bfloat16)
        grad_near = realign_back(grad_raw)
        grad_far = realign_back(jnp.swapaxes(grad_raw, -1, -2))
        grad_query = jnp.einsum(
            "hij,hjd->hid", grad_raw, key_seq, preferred_element_type=jnp.float32
        ) + jnp.einsum("hik,hkd->hid", grad_near, key_table, preferred_element_type=jnp.float32)
        grad_key = jnp.einsum(
            "hij,hid->hjd", grad_raw, query_seq, preferred_element_type=jnp.float32
        ) + jnp.einsum("hjk,hkd->hjd", grad_far, query_table, preferred_element_type=jnp.float32)
        grad_key_rows = jnp.einsum(
            "hik,hid->hkd", grad_near, query_seq, preferred_element_type=jnp.float32
        )
        grad_query_rows = jnp.einsum(
            "hjk,hjd->hkd", grad_far, key_seq, preferred_element_type=jnp.float32
        )
        return (
            (running[0] + grad_key_rows, running[1] + grad_query_rows),
            (grad_query, grad_key, grad_value),
        )

    empty_grad = jnp.zeros(key_table.shape, jnp.float32)
    offset_sums, per_token = lax.scan(
        one_sequence,
        (empty_grad, empty_grad),
        (queries, key_heads, value_heads, lengths, log_total, grad_context),
    )
    return (per_token[0], per_token[1], per_token[2], offset_sums[0], offset_sums[1])


def forward_pass(weights, tokens, lengths, boundary, pick_query, pick_key):
    (
        w_query,
        b_query,
        w_key,
        b_key,
        w_value,
        b_value,
        w_out,
        b_out,
        first_gain,
        first_shift,
        w_up,
        b_up,
        w_down,
        b_down,
        second_gain,
        second_shift,
        rel_table,
        type_table,
    ) = weights
    seq_count, seq_len, features = tokens.shape
    row_count = seq_count * seq_len
    positions = jnp.arange(seq_len)
    second_part = (positions[None, :] >= boundary[:, None]).reshape(row_count, 1)
    type_rows = type_table.astype(jnp.float32)
    summed = tokens.reshape(row_count, features).astype(jnp.float32) + jnp.where(
        second_part, type_rows[1], type_rows[0]
    )
    summed_low = summed.astype(jnp.bfloat16)
    queries = to_heads(
        (project(summed_low, w_query) + b_query.astype(jnp.float32)).astype(jnp.bfloat16), seq_count
    )
    key_heads = to_heads(
        (project(summed_low, w_key) + b_key.astype(jnp.float32)).astype(jnp.bfloat16), seq_count
    )
    value_heads = to_heads(
        (project(summed_low, w_value) + b_value.astype(jnp.float32)).astype(jnp.bfloat16), seq_count
    )
    pos_key = (project(rel_table, w_key) + b_key.astype(jnp.float32)).astype(jnp.bfloat16)
    pos_query = (project(rel_table, w_query) + b_query.astype(jnp.float32)).astype(jnp.bfloat16)
    key_table = table_heads(project(pick_query, pos_key).astype(jnp.bfloat16))
    query_table = table_heads(project(pick_key, pos_query).astype(jnp.bfloat16))
    context, log_total = attend(queries, key_heads, value_heads, key_table, query_table, lengths)
    context_low = from_heads(context)
    attended = project(context_low, w_out) + b_out.astype(jnp.float32)
    first_normed, first_inverse = normalize(summed + attended)
    hidden = first_normed * first_gain.astype(jnp.float32) + first_shift.astype(jnp.float32)
    hidden_low = hidden.astype(jnp.bfloat16)
    raised = project(hidden_low, w_up) + b_up.astype(jnp.float32)
    active_low = jax.nn.gelu(raised, approximate=False).astype(jnp.bfloat16)
    second_normed, second_inverse = normalize(
        hidden + project(active_low, w_down) + b_down.astype(jnp.float32)
    )
    layer_part = (
        second_normed * second_gain.astype(jnp.float32) + second_shift.astype(jnp.float32)
    ).astype(jnp.bfloat16)
    stored = (
        second_part,
        summed_low,
        queries,
        key_heads,
        value_heads,
        key_table,
        query_table,
        log_total,
        context_low,
        first_normed,
        first_inverse,
        hidden_low,
        raised,
        active_low,
        second_normed,
        second_inverse,
    )
    return (stored, layer_part.reshape(seq_count, seq_len, features))


def backward_pass(weights, stored, out_grad, lengths, pick_query, pick_key):
    (
        w_query,
        b_query,
        w_key,
        b_key,
        w_value,
        b_value,
        w_out,
        b_out,
        first_gain,
        first_shift,
        w_up,
        b_up,
        w_down,
        b_down,
        second_gain,
        second_shift,
        rel_table,
        type_table,
    ) = weights
    (
        second_part,
        summed_low,
        queries,
        key_heads,
        value_heads,
        key_table,
        query_table,
        log_total,
        context_low,
        first_normed,
        first_inverse,
        hidden_low,
        raised,
        active_low,
        second_normed,
        second_inverse,
    ) = stored
    seq_count, seq_len, features = out_grad.shape
    row_count = seq_count * seq_len
    grad_output = out_grad.reshape(row_count, features).astype(jnp.float32)
    grad_second_gain = jnp.sum(grad_output * second_normed, 0)
    grad_second_shift = jnp.sum(grad_output, 0)
    grad_mixed = normalize_back(
        grad_output * second_gain.astype(jnp.float32), second_normed, second_inverse
    )
    grad_ffn = grad_mixed.astype(jnp.bfloat16)
    grad_w_down = outer_sum(active_low, grad_ffn)
    grad_b_down = jnp.sum(grad_ffn.astype(jnp.float32), 0)
    grad_raised = (back_project(grad_ffn, w_down) * gelu_slope(raised)).astype(jnp.bfloat16)
    grad_w_up = outer_sum(hidden_low, grad_raised)
    grad_b_up = jnp.sum(grad_raised.astype(jnp.float32), 0)
    grad_hidden = back_project(grad_raised, w_up) + grad_mixed
    grad_first_gain = jnp.sum(grad_hidden * first_normed, 0)
    grad_first_shift = jnp.sum(grad_hidden, 0)
    grad_first = normalize_back(
        grad_hidden * first_gain.astype(jnp.float32), first_normed, first_inverse
    )
    grad_attended = grad_first.astype(jnp.bfloat16)
    grad_w_out = outer_sum(context_low, grad_attended)
    grad_b_out = jnp.sum(grad_attended.astype(jnp.float32), 0)
    grad_context = to_heads(back_project(grad_attended, w_out).astype(jnp.bfloat16), seq_count)
    grad_queries, grad_keys, grad_values, grad_key_table, grad_query_table = attend_back(
        queries, key_heads, value_heads, key_table, query_table, lengths, log_total, grad_context
    )
    grad_queries = from_heads(grad_queries.astype(jnp.bfloat16))
    grad_keys = from_heads(grad_keys.astype(jnp.bfloat16))
    grad_values = from_heads(grad_values.astype(jnp.bfloat16))
    grad_pos_key = outer_sum(pick_query, table_flat(grad_key_table).astype(jnp.bfloat16))
    grad_pos_query = outer_sum(pick_key, table_flat(grad_query_table).astype(jnp.bfloat16))
    rel_wide = rel_table.astype(jnp.float32)
    grad_w_query = outer_sum(summed_low, grad_queries) + exact_outer(rel_wide, grad_pos_query)
    grad_b_query = jnp.sum(grad_queries.astype(jnp.float32), 0) + jnp.sum(grad_pos_query, 0)
    grad_w_key = outer_sum(summed_low, grad_keys) + exact_outer(rel_wide, grad_pos_key)
    grad_b_key = jnp.sum(grad_keys.astype(jnp.float32), 0) + jnp.sum(grad_pos_key, 0)
    grad_w_value = outer_sum(summed_low, grad_values)
    grad_b_value = jnp.sum(grad_values.astype(jnp.float32), 0)
    grad_rel_table = exact_back(grad_pos_key, w_key.astype(jnp.float32)) + exact_back(
        grad_pos_query, w_query.astype(jnp.float32)
    )
    grad_summed = (
        back_project(grad_queries, w_query)
        + back_project(grad_keys, w_key)
        + back_project(grad_values, w_value)
        + grad_first
    )
    grad_type_table = jnp.stack(
        [
            jnp.sum(jnp.where(second_part, 0.0, grad_summed), 0),
            jnp.sum(jnp.where(second_part, grad_summed, 0.0), 0),
        ]
    )
    gradients = (
        grad_w_query,
        grad_b_query,
        grad_w_key,
        grad_b_key,
        grad_w_value,
        grad_b_value,
        grad_w_out,
        grad_b_out,
        grad_first_gain,
        grad_first_shift,
        grad_w_up,
        grad_b_up,
        grad_w_down,
        grad_b_down,
        grad_second_gain,
        grad_second_shift,
        grad_rel_table,
        grad_type_table,
    )
    return (gradients, grad_summed.astype(jnp.bfloat16).reshape(seq_count, seq_len, features))


def per_device(
    tokens,
    lengths,
    boundary,
    w_query,
    b_query,
    w_key,
    b_key,
    w_value,
    b_value,
    w_out,
    b_out,
    first_gain,
    first_shift,
    w_up,
    b_up,
    w_down,
    b_down,
    second_gain,
    second_shift,
    rel_table,
    type_table,
    out_grad,
):
    micro_count = tokens.shape[0]
    pick_c, pick_p = offset_tables(tokens.shape[2])
    pick_query = jnp.asarray(pick_c, jnp.bfloat16)
    pick_key = jnp.asarray(pick_p, jnp.bfloat16)
    layer_parts = []
    token_grads = []
    totals = None
    for micro_index in range(micro_count):
        gathered = (
            lax.all_gather(w_query, "fsdp", axis=0, tiled=True),
            lax.all_gather(b_query, "fsdp", axis=0, tiled=True),
            lax.all_gather(w_key, "fsdp", axis=0, tiled=True),
            lax.all_gather(b_key, "fsdp", axis=0, tiled=True),
            lax.all_gather(w_value, "fsdp", axis=0, tiled=True),
            lax.all_gather(b_value, "fsdp", axis=0, tiled=True),
            lax.all_gather(w_out, "fsdp", axis=0, tiled=True),
            lax.all_gather(b_out, "fsdp", axis=0, tiled=True),
            lax.all_gather(first_gain, "fsdp", axis=0, tiled=True),
            lax.all_gather(first_shift, "fsdp", axis=0, tiled=True),
            lax.all_gather(w_up, "fsdp", axis=0, tiled=True),
            lax.all_gather(b_up, "fsdp", axis=0, tiled=True),
            lax.all_gather(w_down, "fsdp", axis=0, tiled=True),
            lax.all_gather(b_down, "fsdp", axis=0, tiled=True),
            lax.all_gather(second_gain, "fsdp", axis=0, tiled=True),
            lax.all_gather(second_shift, "fsdp", axis=0, tiled=True),
            lax.all_gather(rel_table, "fsdp", axis=0, tiled=True),
            lax.all_gather(type_table, "fsdp", axis=1, tiled=True),
        )
        stored, layer_part = forward_pass(
            gathered,
            tokens[micro_index],
            lengths[micro_index],
            boundary[micro_index],
            pick_query,
            pick_key,
        )
        layer_parts.append(layer_part)
        regathered = (
            lax.all_gather(w_query, "fsdp", axis=0, tiled=True),
            lax.all_gather(b_query, "fsdp", axis=0, tiled=True),
            lax.all_gather(w_key, "fsdp", axis=0, tiled=True),
            lax.all_gather(b_key, "fsdp", axis=0, tiled=True),
            lax.all_gather(w_value, "fsdp", axis=0, tiled=True),
            lax.all_gather(b_value, "fsdp", axis=0, tiled=True),
            lax.all_gather(w_out, "fsdp", axis=0, tiled=True),
            lax.all_gather(b_out, "fsdp", axis=0, tiled=True),
            lax.all_gather(first_gain, "fsdp", axis=0, tiled=True),
            lax.all_gather(first_shift, "fsdp", axis=0, tiled=True),
            lax.all_gather(w_up, "fsdp", axis=0, tiled=True),
            lax.all_gather(b_up, "fsdp", axis=0, tiled=True),
            lax.all_gather(w_down, "fsdp", axis=0, tiled=True),
            lax.all_gather(b_down, "fsdp", axis=0, tiled=True),
            lax.all_gather(second_gain, "fsdp", axis=0, tiled=True),
            lax.all_gather(second_shift, "fsdp", axis=0, tiled=True),
            lax.all_gather(rel_table, "fsdp", axis=0, tiled=True),
            lax.all_gather(type_table, "fsdp", axis=1, tiled=True),
        )
        gradients, token_grad = backward_pass(
            regathered, stored, out_grad[micro_index], lengths[micro_index], pick_query, pick_key
        )
        token_grads.append(token_grad)
        shares = (
            lax.psum_scatter(
                gradients[0].astype(jnp.bfloat16), "fsdp", scatter_dimension=0, tiled=True
            ).astype(jnp.float32),
            lax.psum_scatter(
                gradients[1].astype(jnp.bfloat16), "fsdp", scatter_dimension=0, tiled=True
            ).astype(jnp.float32),
            lax.psum_scatter(
                gradients[2].astype(jnp.bfloat16), "fsdp", scatter_dimension=0, tiled=True
            ).astype(jnp.float32),
            lax.psum_scatter(
                gradients[3].astype(jnp.bfloat16), "fsdp", scatter_dimension=0, tiled=True
            ).astype(jnp.float32),
            lax.psum_scatter(
                gradients[4].astype(jnp.bfloat16), "fsdp", scatter_dimension=0, tiled=True
            ).astype(jnp.float32),
            lax.psum_scatter(
                gradients[5].astype(jnp.bfloat16), "fsdp", scatter_dimension=0, tiled=True
            ).astype(jnp.float32),
            lax.psum_scatter(
                gradients[6].astype(jnp.bfloat16), "fsdp", scatter_dimension=0, tiled=True
            ).astype(jnp.float32),
            lax.psum_scatter(
                gradients[7].astype(jnp.bfloat16), "fsdp", scatter_dimension=0, tiled=True
            ).astype(jnp.float32),
            lax.psum_scatter(
                gradients[8].astype(jnp.bfloat16), "fsdp", scatter_dimension=0, tiled=True
            ).astype(jnp.float32),
            lax.psum_scatter(
                gradients[9].astype(jnp.bfloat16), "fsdp", scatter_dimension=0, tiled=True
            ).astype(jnp.float32),
            lax.psum_scatter(
                gradients[10].astype(jnp.bfloat16), "fsdp", scatter_dimension=0, tiled=True
            ).astype(jnp.float32),
            lax.psum_scatter(
                gradients[11].astype(jnp.bfloat16), "fsdp", scatter_dimension=0, tiled=True
            ).astype(jnp.float32),
            lax.psum_scatter(
                gradients[12].astype(jnp.bfloat16), "fsdp", scatter_dimension=0, tiled=True
            ).astype(jnp.float32),
            lax.psum_scatter(
                gradients[13].astype(jnp.bfloat16), "fsdp", scatter_dimension=0, tiled=True
            ).astype(jnp.float32),
            lax.psum_scatter(
                gradients[14].astype(jnp.bfloat16), "fsdp", scatter_dimension=0, tiled=True
            ).astype(jnp.float32),
            lax.psum_scatter(
                gradients[15].astype(jnp.bfloat16), "fsdp", scatter_dimension=0, tiled=True
            ).astype(jnp.float32),
            lax.psum_scatter(
                gradients[16].astype(jnp.bfloat16), "fsdp", scatter_dimension=0, tiled=True
            ).astype(jnp.float32),
            lax.psum_scatter(
                gradients[17].astype(jnp.bfloat16), "fsdp", scatter_dimension=1, tiled=True
            ).astype(jnp.float32),
        )
        totals = (
            shares
            if totals is None
            else tuple([held + added for held, added in zip(totals, shares)])
        )
    shared = (
        lax.psum(totals[0].astype(jnp.bfloat16), "rep").astype(jnp.float32),
        lax.psum(totals[1].astype(jnp.bfloat16), "rep").astype(jnp.float32),
        lax.psum(totals[2].astype(jnp.bfloat16), "rep").astype(jnp.float32),
        lax.psum(totals[3].astype(jnp.bfloat16), "rep").astype(jnp.float32),
        lax.psum(totals[4].astype(jnp.bfloat16), "rep").astype(jnp.float32),
        lax.psum(totals[5].astype(jnp.bfloat16), "rep").astype(jnp.float32),
        lax.psum(totals[6].astype(jnp.bfloat16), "rep").astype(jnp.float32),
        lax.psum(totals[7].astype(jnp.bfloat16), "rep").astype(jnp.float32),
        lax.psum(totals[8].astype(jnp.bfloat16), "rep").astype(jnp.float32),
        lax.psum(totals[9].astype(jnp.bfloat16), "rep").astype(jnp.float32),
        lax.psum(totals[10].astype(jnp.bfloat16), "rep").astype(jnp.float32),
        lax.psum(totals[11].astype(jnp.bfloat16), "rep").astype(jnp.float32),
        lax.psum(totals[12].astype(jnp.bfloat16), "rep").astype(jnp.float32),
        lax.psum(totals[13].astype(jnp.bfloat16), "rep").astype(jnp.float32),
        lax.psum(totals[14].astype(jnp.bfloat16), "rep").astype(jnp.float32),
        lax.psum(totals[15].astype(jnp.bfloat16), "rep").astype(jnp.float32),
        lax.psum(totals[16].astype(jnp.bfloat16), "rep").astype(jnp.float32),
        lax.psum(totals[17].astype(jnp.bfloat16), "rep").astype(jnp.float32),
    )
    return (
        jnp.stack(layer_parts),
        jnp.stack(token_grads),
        shared[0],
        shared[1],
        shared[2],
        shared[3],
        shared[4],
        shared[5],
        shared[6],
        shared[7],
        shared[8],
        shared[9],
        shared[10],
        shared[11],
        shared[12],
        shared[13],
        shared[14],
        shared[15],
        shared[16],
        shared[17],
    )


def solution(mesh):
    placed = (
        P(None, ("rep", "fsdp"), None, None),
        P(None, ("rep", "fsdp")),
        P(None, ("rep", "fsdp")),
        P("fsdp", None),
        P("fsdp"),
        P("fsdp", None),
        P("fsdp"),
        P("fsdp", None),
        P("fsdp"),
        P("fsdp", None),
        P("fsdp"),
        P("fsdp"),
        P("fsdp"),
        P("fsdp", None),
        P("fsdp"),
        P("fsdp", None),
        P("fsdp"),
        P("fsdp"),
        P("fsdp"),
        P("fsdp", None),
        P(None, "fsdp"),
        P(None, ("rep", "fsdp"), None, None),
    )
    return jax.shard_map(
        per_device,
        mesh=mesh,
        in_specs=placed,
        out_specs=(
            P(None, ("rep", "fsdp"), None, None),
            P(None, ("rep", "fsdp"), None, None),
            P("fsdp", None),
            P("fsdp"),
            P("fsdp", None),
            P("fsdp"),
            P("fsdp", None),
            P("fsdp"),
            P("fsdp", None),
            P("fsdp"),
            P("fsdp"),
            P("fsdp"),
            P("fsdp", None),
            P("fsdp"),
            P("fsdp", None),
            P("fsdp"),
            P("fsdp"),
            P("fsdp"),
            P("fsdp", None),
            P(None, "fsdp"),
        ),
        check_vma=False,
    )
```

profile of v0, /device:TPU:0, one launch (start us, length us, event | category | flops | bytes accessed | tf_op | source)
XLA Modules:
  0.0 1801.8 jit_solution(14692895624631176474)
XLA Ops:
  21.8 30.6 %all-reduce.38 = (bf16[768]{0:T(1024)(128)(2,1)S(1)}, bf16[768]{0:T(1024)(128)(2,1)S(1)}, bf16[768]{0:T(1024)(128)(2,1)S(1)}, bf16[768]{0:T(1024)(128)(2,1)S(1)}...) all-reduce(bf16[768]{0:T(1024)(128)(2,1)S(1)} %dynamic-update-slice, ...), channel_id=1, replica_groups=mesh['rep'=4,'fsdp'=8] {'fsdp'}, use_global_device_ids=true, to_apply=%add.10 | all-reduce | flops 6144 | bytes 24576
  128.7 27.2 %pad.50 = f32[16,512,1024]{2,1,0:T(8,128)} pad(f32[12,512,1024]{2,1,0:T(8,128)S(1)} %fusion.195, f32[]{:T(128)} %constant.152.clone.1), padding=0_4x0_0x0_0 | pad | bytes 58720260
  155.8 28.3 %copy.161 = f32[2,8,512,1024]{3,1,2,0:T(8,128)S(1)} copy(f32[2,8,512,1024]{3,2,1,0:T(8,128)} %bitcast.356) | data formatting | bytes 67108864
  198.1 41.8 %reshape.599 = f32[12,512,1023]{2,1,0:T(8,128)} reshape(f32[12,523776]{1,0:T(8,128)} %slice.106) | data formatting | bytes 50282496 | tf_op jit(solution)/shard_map/while/body/eval_jaxpr/reshape | solution.py:48
  279.5 28.3 %copy.159 = f32[2,8,512,1024]{3,1,2,0:T(8,128)S(1)} copy(f32[2,8,512,1024]{3,2,1,0:T(8,128)} %bitcast.357) | data formatting | bytes 67108864
  321.8 41.8 %reshape.590 = f32[12,512,1023]{2,1,0:T(8,128)} reshape(f32[12,523776]{1,0:T(8,128)} %slice.102) | data formatting | bytes 50282496 | tf_op jit(solution)/shard_map/while/body/eval_jaxpr/reshape | solution.py:48
  406.4 28.3 %copy.162 = f32[2,8,512,1024]{3,1,2,0:T(8,128)S(1)} copy(f32[2,8,512,1024]{3,2,1,0:T(8,128)} %bitcast.358) | data formatting | bytes 67108864
  448.7 41.9 %reshape.601 = f32[12,512,1023]{2,1,0:T(8,128)} reshape(f32[12,523776]{1,0:T(8,128)} %slice.108) | data formatting | bytes 50282496 | tf_op jit(solution)/shard_map/while/body/eval_jaxpr/reshape | solution.py:48
  528.6 28.3 %copy.160 = f32[2,8,512,1024]{3,1,2,0:T(8,128)S(1)} copy(f32[2,8,512,1024]{3,2,1,0:T(8,128)} %bitcast.355) | data formatting | bytes 67108864
  570.9 41.9 %reshape.593 = f32[12,512,1023]{2,1,0:T(8,128)} reshape(f32[12,523776]{1,0:T(8,128)} %slice.104) | data formatting | bytes 50282496 | tf_op jit(solution)/shard_map/while/body/eval_jaxpr/reshape | solution.py:48
  641.2 31.2 %fusion.36 = (bf16[512,3072]{1,0:T(8,128)(2,1)}, bf16[512,3072]{1,0:T(8,128)(2,1)}, f32[512,3072]{1,0:T(8,128)}) fusion(f32[3072]{0:T(1024)S(1)} %bitcast.430, f32[512,3072]{1,0:T(8,128)S(1)} %fusion.171, bf16[768,3072]{1,0:T(8,128)(2,1)S(1)} %copy-done.162, f32[512,768]{1,0:T(8,128)S(1)} %get-tuple-element.272, f32[768]{0:T(1024)S(1)} %copy-done.133, ...), kind=kOutput, calls=%fused_computation.50 | convolution fusion | flops 2625503232 | bytes 25188352 | tf_op jit(solution)/shard_map/dot_general | solution.py:79
  717.6 16.7 multiply_convert_fusion.1
  752.0 35.2 %reshape.613 = bf16[12,523776]{1,0:T(8,128)(2,1)} reshape(bf16[12,512,1023]{2,1,0:T(8,128)(2,1)} %pad.36.clone) | data formatting | bytes 25141248 | tf_op jit(solution)/shard_map/while/body/eval_jaxpr/transpose(jvp())/reshape | solution.py:48
  797.9 25.7 %copy.165 = bf16[2,8,512,1024]{3,2,1,0:T(8,128)(2,1)S(1)} copy(bf16[2,8,512,1024]{3,1,2,0:T(8,128)(2,1)S(1)} %bitcast.365) | data formatting | bytes 33554432
  831.2 16.5 multiply_convert_fusion.3
  865.4 34.7 %reshape.605 = bf16[12,523776]{1,0:T(8,128)(2,1)} reshape(bf16[12,512,1023]{2,1,0:T(8,128)(2,1)} %pad.32.clone) | data formatting | bytes 25141248 | tf_op jit(solution)/shard_map/while/body/eval_jaxpr/transpose(jvp())/reshape | solution.py:48
  911.0 25.7 %copy.163 = bf16[2,8,512,1024]{3,2,1,0:T(8,128)(2,1)S(1)} copy(bf16[2,8,512,1024]{3,1,2,0:T(8,128)(2,1)S(1)} %bitcast.366) | data formatting | bytes 33554432
  952.0 34.7 %reshape.616 = bf16[12,523776]{1,0:T(8,128)(2,1)} reshape(bf16[12,512,1023]{2,1,0:T(8,128)(2,1)} %pad.38) | data formatting | bytes 25141248 | tf_op jit(solution)/shard_map/while/body/eval_jaxpr/transpose(jvp())/reshape | solution.py:48
  997.4 25.7 %copy.166 = bf16[2,8,512,1024]{3,2,1,0:T(8,128)(2,1)S(1)} copy(bf16[2,8,512,1024]{3,1,2,0:T(8,128)(2,1)S(1)} %bitcast.367) | data formatting | bytes 33554432
  1045.0 34.9 %reshape.608 = bf16[12,523776]{1,0:T(8,128)(2,1)} reshape(bf16[12,512,1023]{2,1,0:T(8,128)(2,1)} %pad.34) | data formatting | bytes 25141248 | tf_op jit(solution)/shard_map/while/body/eval_jaxpr/transpose(jvp())/reshape | solution.py:48
  1090.6 25.7 %copy.164 = bf16[2,8,512,1024]{3,2,1,0:T(8,128)(2,1)S(1)} copy(bf16[2,8,512,1024]{3,1,2,0:T(8,128)(2,1)S(1)} %bitcast.368) | data formatting | bytes 33554432
  1303.4 28.6 %all-reduce.37 = (bf16[768]{0:T(1024)(128)(2,1)S(1)}, bf16[768]{0:T(1024)(128)(2,1)S(1)}, bf16[768]{0:T(1024)(128)(2,1)S(1)}, bf16[768]{0:T(1024)(128)(2,1)S(1)}...) all-reduce(bf16[768]{0:T(1024)(128)(2,1)S(1)} %copy-done.118, ...), channel_id=1, replica_groups=mesh['rep'=4,'fsdp'=8] {'fsdp'}, use_global_device_ids=true, to_apply=%add.16 | all-reduce | flops 20736 | bytes 82944
  1338.0 24.2 %reduce-scatter.25.cloned.1.call-done = bf16[96,768]{1,0:T(8,128)(2,1)} async-done(((bf16[768,768]{1,0:T(8,128)(2,1)}), bf16[96,768]{1,0:T(8,128)(2,1)}) %reduce-scatter.25.cloned.1.call-update) | async-done | bytes 147472 | tf_op jit(solution)/shard_map/reduce_scatter | solution.py:504
  1363.9 32.1 %reduce-scatter.23.cloned.1.call-done = bf16[96,768]{1,0:T(8,128)(2,1)} async-done(((bf16[768,768]{1,0:T(8,128)(2,1)}), bf16[96,768]{1,0:T(8,128)(2,1)}) %reduce-scatter.23.cloned.1.call-update) | async-done | bytes 147472 | tf_op jit(solution)/shard_map/reduce_scatter | solution.py:498
  1396.0 33.7 %reduce-scatter.21.cloned.1.call-done = bf16[96,768]{1,0:T(8,128)(2,1)} async-done(((bf16[768,768]{1,0:T(8,128)(2,1)}), bf16[96,768]{1,0:T(8,128)(2,1)}) %reduce-scatter.21.cloned.1.call-update) | async-done | bytes 147472 | tf_op jit(solution)/shard_map/reduce_scatter | solution.py:498
  1431.4 53.7 %reduce-scatter.37.cloned.1.call-done = bf16[96,3072]{1,0:T(8,128)(2,1)} async-done(((bf16[768,3072]{1,0:T(8,128)(2,1)}), bf16[96,3072]{1,0:T(8,128)(2,1)}) %reduce-scatter.37.cloned.1.call-update) | async-done | bytes 589840 | tf_op jit(solution)/shard_map/reduce_scatter | solution.py:528
  1485.2 55.5 %reduce-scatter.39.cloned.1.call-done = bf16[96,3072]{1,0:T(8,128)(2,1)} async-done(((bf16[768,3072]{1,0:T(8,128)(2,1)}), bf16[96,3072]{1,0:T(8,128)(2,1)}) %reduce-scatter.39.cloned.1.call-update) | async-done | bytes 589840 | tf_op jit(solution)/shard_map/reduce_scatter | solution.py:528
  1542.9 53.4 %reduce-scatter.43.cloned.1.call-done = bf16[384,768]{1,0:T(8,128)(2,1)} async-done(((bf16[3072,768]{1,0:T(8,128)(2,1)}), bf16[384,768]{1,0:T(8,128)(2,1)}) %reduce-scatter.43.cloned.1.call-update) | async-done | bytes 589840 | tf_op jit(solution)/shard_map/reduce_scatter | solution.py:534
  1596.4 55.5 %reduce-scatter.41.cloned.1.call-done = bf16[384,768]{1,0:T(8,128)(2,1)} async-done(((bf16[3072,768]{1,0:T(8,128)(2,1)}), bf16[384,768]{1,0:T(8,128)(2,1)}) %reduce-scatter.41.cloned.1.call-update) | async-done | bytes 589840 | tf_op jit(solution)/shard_map/reduce_scatter | solution.py:534
  1658.6 24.7 %reduce-scatter.51.cloned.1.call-done = bf16[96,2]{1,0:T(8,128)(2,1)} async-done(((bf16[768,2]{1,0:T(8,128)(2,1)}), bf16[96,2]{1,0:T(8,128)(2,1)}) %reduce-scatter.51.cloned.1.call-update) | async-done | bytes 400
  1684.1 30.6 %reduce-scatter.49.cloned.1.call-done = bf16[96,2]{1,0:T(8,128)(2,1)} async-done(((bf16[768,2]{1,0:T(8,128)(2,1)}), bf16[96,2]{1,0:T(8,128)(2,1)}) %reduce-scatter.49.cloned.1.call-update) | async-done | bytes 400
  1731.4 54.0 %all-reduce.43.cloned.1.call-done = (bf16[96,768]{1,0:T(8,128)(2,1)}, bf16[96,768]{1,0:T(8,128)(2,1)}, bf16[96,768]{1,0:T(8,128)(2,1)}, bf16[96,768]{1,0:T(8,128...) async-done(((bf16[96,768]{1,0:T(8,128)(2,1)}, bf16[96,768]{1,0:T(8,128)(2,1)}, bf16[96,768]{1,0:T(8,128)(2,1)}, ...) | async-done | bytes 1867792 | tf_op jit(solution)/shard_map/psum | solution.py:559
  (686 shorter events, 691.6 us)
Async XLA Ops:
  7.3 86.1 %all-gather.11.cloned.1.call-start = ((), (), s32[]{:S(2)}) async-start(), calls=%async_computation.17 | async-start | bytes 1327104 | tf_op jit(solution)/shard_map/all_gather | solution.py:447
  8.1 89.2 %all-gather.13.cloned.1.call-start = ((), (), s32[]{:S(2)}) async-start(), calls=%async_computation.18 | async-start | bytes 1327104 | tf_op jit(solution)/shard_map/all_gather | solution.py:449
  8.8 100.6 %all-gather.9.cloned.1.call-start = ((), (), s32[]{:S(2)}) async-start(), calls=%async_computation.16 | async-start | bytes 1327104 | tf_op jit(solution)/shard_map/all_gather | solution.py:445
  9.6 498.9 %all-gather.15.cloned.1.call-start = ((), (), s32[]{:S(2)}) async-start(), calls=%async_computation.19 | async-start | bytes 1327104 | tf_op jit(solution)/shard_map/all_gather | solution.py:451
  10.1 621.9 %all-gather.17.cloned.1.call-start = ((), (), s32[]{:S(2)}) async-start(), calls=%async_computation.20 | async-start | bytes 5308416 | tf_op jit(solution)/shard_map/all_gather | solution.py:455
  10.7 661.7 %all-gather.19.cloned.1.call-start = ((), (), s32[]{:S(2)}) async-start(), calls=%async_computation.21 | async-start | bytes 5308416 | tf_op jit(solution)/shard_map/all_gather | solution.py:457
  11.3 1321.7 %reduce-scatter.47.cloned.1.call-start = ((), (), s32[]{:S(2)}) async-start(), calls=%async_computation.35 | async-start | bytes 884736 | tf_op jit(solution)/shard_map/reduce_scatter | solution.py:546
  511.2 196.2 %copy-start.98 = (f32[512]{0:T(512)}, f32[512]{0:T(512)S(1)}, u32[]{:S(2)}) copy-start(f32[512]{0:T(512)S(1)} %broadcast_multiply_fusion.9) | copy-start | bytes 6148
  512.4 195.0 %copy-start.121 = (f32[512]{0:T(512)}, f32[512]{0:T(512)S(1)}, u32[]{:S(2)}) copy-start(f32[512]{0:T(512)S(1)} %add_rsqrt_fusion.1) | copy-start | bytes 6148
  831.2 199.5 %copy-start.30 = (f32[768,512]{0,1:T(8,128)}, f32[768,512]{0,1:T(8,128)S(1)}, u32[]{:S(2)}) copy-start(f32[768,512]{0,1:T(8,128)S(1)} %get-tuple-element.294) | copy-start | bytes 4718596
  1036.0 297.0 %reduce-scatter.45.cloned.1.call-start = ((), (), s32[]{:S(2)}) async-start(), calls=%async_computation.34 | async-start | bytes 884736 | tf_op jit(solution)/shard_map/reduce_scatter | solution.py:546
  1131.7 202.9 %reduce-scatter.33.cloned.1.call-start = ((), (), s32[]{:S(2)}) async-start(), calls=%async_computation.28 | async-start | bytes 1327104 | tf_op jit(solution)/shard_map/reduce_scatter | solution.py:516
  1134.8 199.8 %reduce-scatter.35.cloned.1.call-start = ((), (), s32[]{:S(2)}) async-start(), calls=%async_computation.29 | async-start | bytes 1327104 | tf_op jit(solution)/shard_map/reduce_scatter | solution.py:516
  1138.5 197.9 %reduce-scatter.31.cloned.1.call-start = ((), (), s32[]{:S(2)}) async-start(), calls=%async_computation.27 | async-start | bytes 1327104 | tf_op jit(solution)/shard_map/reduce_scatter | solution.py:510
  1149.7 186.6 %reduce-scatter.29.cloned.1.call-start = ((), (), s32[]{:S(2)}) async-start(), calls=%async_computation.26 | async-start | bytes 1327104 | tf_op jit(solution)/shard_map/reduce_scatter | solution.py:510
  1160.4 177.7 %reduce-scatter.27.cloned.1.call-start = ((), (), s32[]{:S(2)}) async-start(), calls=%async_computation.25 | async-start | bytes 1327104 | tf_op jit(solution)/shard_map/reduce_scatter | solution.py:504
  1184.8 177.5 %reduce-scatter.25.cloned.1.call-start = ((), (), s32[]{:S(2)}) async-start(), calls=%async_computation.24 | async-start | bytes 1327104 | tf_op jit(solution)/shard_map/reduce_scatter | solution.py:504
  1208.4 187.6 %reduce-scatter.23.cloned.1.call-start = ((), (), s32[]{:S(2)}) async-start(), calls=%async_computation.23 | async-start | bytes 1327104 | tf_op jit(solution)/shard_map/reduce_scatter | solution.py:498
  1231.9 197.9 %reduce-scatter.21.cloned.1.call-start = ((), (), s32[]{:S(2)}) async-start(), calls=%async_computation.22 | async-start | bytes 1327104 | tf_op jit(solution)/shard_map/reduce_scatter | solution.py:498
  1254.3 230.9 %reduce-scatter.37.cloned.1.call-start = ((), (), s32[]{:S(2)}) async-start(), calls=%async_computation.30 | async-start | bytes 5308416 | tf_op jit(solution)/shard_map/reduce_scatter | solution.py:528
  1260.9 279.8 %reduce-scatter.39.cloned.1.call-start = ((), (), s32[]{:S(2)}) async-start(), calls=%async_computation.31 | async-start | bytes 5308416 | tf_op jit(solution)/shard_map/reduce_scatter | solution.py:528
  1268.9 327.5 %reduce-scatter.43.cloned.1.call-start = ((), (), s32[]{:S(2)}) async-start(), calls=%async_computation.33 | async-start | bytes 5308416 | tf_op jit(solution)/shard_map/reduce_scatter | solution.py:534
  1277.0 374.8 %reduce-scatter.41.cloned.1.call-start = ((), (), s32[]{:S(2)}) async-start(), calls=%async_computation.32 | async-start | bytes 5308416 | tf_op jit(solution)/shard_map/reduce_scatter | solution.py:534
  1285.1 398.2 %reduce-scatter.51.cloned.1.call-start = ((), (), s32[]{:S(2)}) async-start(), calls=%async_computation.37 | async-start | bytes 221184
  1303.0 411.8 %reduce-scatter.49.cloned.1.call-start = ((), (), s32[]{:S(2)}) async-start(), calls=%async_computation.36 | async-start | bytes 221184
  1332.9 452.6 %all-reduce.43.cloned.1.call-start = ((), (), s32[]{:S(2)}) async-start(), calls=%async_computation.38 | async-start | bytes 3735552 | tf_op jit(solution)/shard_map/psum | solution.py:559
  1542.9 111.9 %copy-start.5 = (f32[512,768]{1,0:T(8,128)S(1)}, f32[512,768]{1,0:T(8,128)}, u32[]{:S(2)}) copy-start(f32[512,768]{1,0:T(8,128)} %copy-done.4) | copy-start | bytes 4718596
  1542.9 111.9 %copy-start.89 = (f32[768]{0:T(1024)S(1)}, f32[768]{0:T(1024)}, u32[]{:S(2)}) copy-start(f32[768]{0:T(1024)} %convert_element_type.674) | copy-start | bytes 9220
  1542.9 111.9 %copy-start.91 = (f32[512]{0:T(512)S(1)}, f32[512]{0:T(512)}, u32[]{:S(2)}) copy-start(f32[512]{0:T(512)} %copy-done.90) | copy-start | bytes 6148
  1542.9 111.9 %copy-start.93 = (f32[512]{0:T(512)S(1)}, f32[512]{0:T(512)}, u32[]{:S(2)}) copy-start(f32[512]{0:T(512)} %copy-done.92) | copy-start | bytes 6148
  1542.9 111.9 %copy-start.95 = (f32[512]{0:T(512)S(1)}, f32[512]{0:T(512)}, u32[]{:S(2)}) copy-start(f32[512]{0:T(512)} %copy-done.94) | copy-start | bytes 6148
  1542.9 111.9 %copy-start.97 = (f32[512]{0:T(512)S(1)}, f32[512]{0:T(512)}, u32[]{:S(2)}) copy-start(f32[512]{0:T(512)} %copy-done.96) | copy-start | bytes 6148
  (188 other events, 1968.5 us)
Sparse Core Ops, SparseCore 0:
  9.8 25.7 all-gather.10
  37.2 22.2 all-gather.12
  61.1 23.1 all-gather.8
  85.8 22.3 all-gather.14
  109.7 51.4 all-gather.16
  162.7 50.5 all-gather.18
  1036.1 30.7 reduce-scatter.46
  1131.8 30.7 reduce-scatter.44
  1165.0 31.1 reduce-scatter.32
  1198.3 30.8 reduce-scatter.34
  1231.4 30.9 reduce-scatter.30
  1264.6 30.9 reduce-scatter.28
  1297.8 31.4 reduce-scatter.26
  1331.5 30.7 reduce-scatter.24
  1364.9 31.0 reduce-scatter.22
  1398.8 30.9 reduce-scatter.20
  1431.9 53.2 reduce-scatter.36
  1487.3 53.3 reduce-scatter.38
  1543.0 53.3 reduce-scatter.42
  1598.5 53.3 reduce-scatter.40
  1654.7 28.6 reduce-scatter.50
  1686.2 28.4 reduce-scatter.48
  1719.9 65.4 all-reduce.42
where the time goes:
time: 1810 us; the launch traced here: 1800 us
  local copies, waits for them, and re-layouts  844 us (47%)
  waiting for transfers between devices  422 us (23%)
  matrix products  351 us (19%)
  blocking collectives  106 us (6%)
  other arithmetic  57.1 us (3%)
  between operations  18.9 us (1%)
    unnamed x434, local copies, waits for them, and re-layouts  365 us
    reshape x8, local copies, waits for them, and re-layouts, realign(): flattened.reshape(leading + (row_count, columns - 1))[..., :row_count]  307 us
    reduce_scatter x2, waiting for transfers between devices, per_device(): lax.psum_scatter(gradients[10].astype(jnp.bfloat16), 'fsdp', scatter_dime...  109 us
    reduce_scatter x2, waiting for transfers between devices, per_device(): lax.psum_scatter(gradients[12].astype(jnp.bfloat16), 'fsdp', scatter_dime...  109 us
    dot_general x14, matrix products, project(): return jnp.dot(left_side, weight, preferred_element_type=jnp.float32)  70.9 us
    reduce_scatter x2, waiting for transfers between devices, per_device(): lax.psum_scatter(gradients[0].astype(jnp.bfloat16), 'fsdp', scatter_dimen...  65.9 us
    unnamed x25, waiting for transfers between devices  59.3 us
    unnamed x2, blocking collectives  59.2 us
  transfers between devices with their start and end apart: 23, of which 10 were waited for; matrix products, arithmetic and copies ran while one was open for 47% of the time, Pallas kernels for 0%

commit v1 on v0

v1 whole, which is shorter than its diff:
```python
import math

import jax
import jax.numpy as jnp
import numpy as np
from jax import lax
from jax.experimental import pallas as pl
from jax.experimental.pallas import tpu as pltpu
from jax.sharding import PartitionSpec as P

BUCKETS = 256
MAX_POS = 512
NORM_EPS = 1e-07

HEAD_DIM=64
MASKED=-1e30
f32=jnp.float32; bf=jnp.bfloat16
BLK=128
LOG2E=math.log2(math.e)

def nn(a,b): return lax.dot_general(a,b,(((1,),(0,)),((),())),preferred_element_type=f32)
def nt(a,b): return lax.dot_general(a,b,(((1,),(1,)),((),())),preferred_element_type=f32)

def eye(rows, flip=False):
    r=lax.broadcasted_iota(jnp.int32,(rows,rows),0)
    c=lax.broadcasted_iota(jnp.int32,(rows,rows),1)
    return jnp.where((r+c==rows-1) if flip else (r==c),1.0,0.0).astype(bf)

def attn_fwd_kernel(len_ref,q_ref,k_ref,v_ref,pkr_ref,pq_ref,ctxT_ref,p_ref,linv_ref,c_scr,s_scr):
    S=q_ref.shape[0]
    nb=S//BLK
    W=S+BLK
    m=pl.program_id(1)
    length=len_ref[m]
    scale=LOG2E/math.sqrt(3*HEAD_DIM)
    q=q_ref[...]; k=k_ref[...]
    pq=pq_ref[...]
    vT=v_ref[...].T
    ident=eye(BLK)
    lane_s=lax.broadcasted_iota(jnp.int32,(S,2*HEAD_DIM),1)
    row_s=lax.broadcasted_iota(jnp.int32,(S,2*HEAD_DIM),0)
    lane_t=lax.broadcasted_iota(jnp.int32,(2*S,2*HEAD_DIM),1)
    bias=jnp.where(row_s<length,0.0,MASKED).astype(bf)
    zero=jnp.zeros((),bf)
    pos=lax.broadcasted_iota(jnp.int32,(1,S),1)
    for h in range(2):
        mine=(lane_s<HEAD_DIM) if h==0 else (lane_s>=HEAD_DIM)
        mine_t=(lane_t<HEAD_DIM) if h==0 else (lane_t>=HEAD_DIM)
        spare=HEAD_DIM if h==0 else 0
        qh=jnp.where(mine,q,zero)
        kb=jnp.where(mine,k,jnp.where(lane_s==spare,bias,zero))
        pqh=jnp.where(mine_t,pq,jnp.where(lane_t==spare,jnp.ones((),bf),zero))
        for b in range(nb):
            st=(nb-1-b)*BLK
            c=nt(qh[b*BLK:(b+1)*BLK],pkr_ref[st:st+W,:]).astype(bf)
            c_scr[b*BLK:(b+1)*BLK,:]=pltpu.roll(c,S+1,1,stride=1,stride_axis=0)[:,:S]
        top=None
        for b in range(nb):
            st=(nb-1-b)*BLK
            js=slice(b*BLK,(b+1)*BLK)
            d=nt(kb[js],pqh[st:st+W]).astype(bf)
            d=pltpu.roll(d,S+1,1,stride=1,stride_axis=0)[:,:S]
            lhs=jnp.concatenate([k[js],ident],axis=1)
            rhs=jnp.concatenate([qh,c_scr[:,js]],axis=1)
            s=nt(lhs,rhs)+d.astype(f32)
            s_scr[js,:]=s
            t=jnp.max(s,axis=0,keepdims=True)
            top=t if top is None else jnp.maximum(top,t)
        top=top*scale
        tot=None
        for b in range(nb):
            js=slice(b*BLK,(b+1)*BLK)
            p=jnp.exp2(s_scr[js,:]*scale-top)
            t=jnp.sum(p,axis=0,keepdims=True)
            tot=t if tot is None else tot+t
            p_ref[0,h,js,:]=p.astype(bf)
        linv=jnp.where(pos<length,1.0/tot,0.0)
        linv_ref[0,0,h:h+1,:]=linv
        ctx=nn(vT[h*HEAD_DIM:(h+1)*HEAD_DIM,:],p_ref[0,h])*linv
        ctxT_ref[h*HEAD_DIM:(h+1)*HEAD_DIM,:]=ctx.astype(bf)

def attn_fwd(qkv,pkr,pq,lengths,heads):
    M=lengths.shape[0]; D=heads*HEAD_DIM
    S=pq.shape[0]//2
    NP=heads//2; L=2*HEAD_DIM
    grid=(NP,M)
    return pl.pallas_call(
        attn_fwd_kernel,
        grid_spec=pltpu.PrefetchScalarGridSpec(
            num_scalar_prefetch=1,grid=grid,
            in_specs=[
                pl.BlockSpec((S,L),lambda p,m,_:(m,p)),
                pl.BlockSpec((S,L),lambda p,m,_:(m,NP+p)),
                pl.BlockSpec((S,L),lambda p,m,_:(m,2*NP+p)),
                pl.BlockSpec((2*S,L),lambda p,m,_:(0,p)),
                pl.BlockSpec((2*S,L),lambda p,m,_:(0,p)),
            ],
            out_specs=[
                pl.BlockSpec((L,S),lambda p,m,_:(p,m)),
                pl.BlockSpec((1,2,S,S),lambda p,m,_:(m,p,0,0)),
                pl.BlockSpec((1,1,2,S),lambda p,m,_:(m,p,0,0)),
            ],
            scratch_shapes=[pltpu.VMEM((S,S),bf),pltpu.VMEM((S,S),f32)],
        ),
        out_shape=[jax.ShapeDtypeStruct((D,M*S),bf),jax.ShapeDtypeStruct((M,heads,S,S),bf),jax.ShapeDtypeStruct((M,NP,2,S),f32)],
        compiler_params=pltpu.CompilerParams(vmem_limit_bytes=40*1024*1024),
        cost_estimate=pl.CostEstimate(flops=int(2*M*heads*S*S*64*12),bytes_accessed=int(M*heads*S*S*2),transcendentals=M*heads*S*S),
    )(lengths,qkv,qkv,qkv,pkr,pq)

def attn_bwd_kernel(q_ref,k_ref,v_ref,dcT_ref,ctxT_ref,p_ref,linv_ref,pk_ref,pq_ref,dq_ref,dk_ref,dv_ref,ko_ref,qo_ref,ds_scr):
    S=q_ref.shape[0]
    nb=S//BLK
    W=S+BLK
    m=pl.program_id(1)
    scale=1.0/math.sqrt(3*HEAD_DIM)
    zero=jnp.zeros((),bf)
    ident=eye(BLK); flip=eye(BLK,True)
    q=q_ref[...]
    def reverse(x):
        return jnp.concatenate([nn(flip,x[(nb-1-b)*BLK:(nb-b)*BLK]).astype(bf) for b in range(nb)],axis=0)
    kr=reverse(k_ref[...]); vr=reverse(v_ref[...])
    qT=q.T; krT=kr.T
    lane_s=lax.broadcasted_iota(jnp.int32,(S,2*HEAD_DIM),1)
    lane_t=lax.broadcasted_iota(jnp.int32,(2*S,2*HEAD_DIM),1)
    pad=jnp.zeros((BLK,BLK),bf)
    @pl.when(m==0)
    def _():
        ko_ref[...]=jnp.zeros_like(ko_ref)
        qo_ref[...]=jnp.zeros_like(qo_ref)
    dq=[None]*nb; dk=[None]*nb; dv=None
    zrow=jnp.zeros((HEAD_DIM,S),bf)
    for h in range(2):
        hs=slice(h*HEAD_DIM,(h+1)*HEAD_DIM)
        mine=(lane_s<HEAD_DIM) if h==0 else (lane_s>=HEAD_DIM)
        mine_t=(lane_t<HEAD_DIM) if h==0 else (lane_t>=HEAD_DIM)
        qh=jnp.where(mine,q,zero); krh=jnp.where(mine,kr,zero)
        pkh=jnp.where(mine_t,pk_ref[...],zero); pqh=jnp.where(mine_t,pq_ref[...],zero)
        linv=linv_ref[0,0,h:h+1,:]
        dc=dcT_ref[hs,:].astype(f32)*linv
        delta=jnp.sum(dc*ctxT_ref[hs,:].astype(f32),axis=0,keepdims=True)*scale
        dcl=dc.astype(bf); dcs=(dc*scale).astype(bf)
        def wide(x): return jnp.concatenate([x,zrow] if h==0 else [zrow,x],axis=0)
        t=nt(p_ref[0,h],wide(dcl))
        dv=t if dv is None else dv+t
        dcw=wide(dcs)
        for b in range(nb):
            js=slice(b*BLK,(b+1)*BLK)
            dp=nn(vr[js],dcw)
            p=nn(flip,p_ref[0,h,(nb-1-b)*BLK:(nb-b)*BLK,:])
            ds=(p*(dp-delta)).astype(bf)
            ds_scr[js,:]=ds
            far=pltpu.roll(jnp.concatenate([ds,pad],axis=1),0,1,stride=1,stride_axis=0)
            st=b*BLK
            t=nn(ds,qh)+nn(far,pqh[st:st+W])
            dk[b]=t if dk[b] is None else dk[b]+t
            qo_ref[hs,st:st+W]+=nn(krT[hs,js],far)
        for b in range(nb):
            js=slice(b*BLK,(b+1)*BLK)
            ds=nt(ident,ds_scr[:,js]).astype(bf)
            near=pltpu.roll(jnp.concatenate([ds,pad],axis=1),0,1,stride=1,stride_axis=0)
            st=b*BLK
            t=nn(ds,krh)+nn(near,pkh[st:st+W])
            dq[b]=t if dq[b] is None else dq[b]+t
            ko_ref[hs,st:st+W]+=nn(qT[hs,js],near)
    dv_ref[...]=dv.astype(bf)
    for b in range(nb):
        dq_ref[b*BLK:(b+1)*BLK,:]=dq[b].astype(bf)
        dk_ref[(nb-1-b)*BLK:(nb-b)*BLK,:]=nn(flip,dk[b].astype(bf)).astype(bf)

def attn_bwd(qkv,dcT,ctxT,p,linv,pk,pq):
    M,heads,S,_=p.shape; D=heads*HEAD_DIM
    NP=heads//2; L=2*HEAD_DIM
    tok=lambda off: pl.BlockSpec((S,L),lambda p,m:(m,off+p))
    colT=pl.BlockSpec((L,S),lambda p,m:(p,m))
    tab=pl.BlockSpec((2*S,L),lambda p,m:(0,p))
    return pl.pallas_call(
        attn_bwd_kernel,
        grid=(NP,M),
        in_specs=[tok(0),tok(NP),tok(2*NP),colT,colT,
            pl.BlockSpec((1,2,S,S),lambda p,m:(m,p,0,0)),
            pl.BlockSpec((1,1,2,S),lambda p,m:(m,p,0,0)),
            tab,tab],
        out_specs=[tok(0),tok(0),tok(0),pl.BlockSpec((L,2*S),lambda p,m:(p,0)),pl.BlockSpec((L,2*S),lambda p,m:(p,0))],
        out_shape=[jax.ShapeDtypeStruct((M*S,D),bf)]*3+[jax.ShapeDtypeStruct((D,2*S),f32)]*2,
        scratch_shapes=[pltpu.VMEM((S,S),bf)],
        compiler_params=pltpu.CompilerParams(vmem_limit_bytes=40*1024*1024),
        cost_estimate=pl.CostEstimate(flops=int(2*M*heads*S*S*64*24),bytes_accessed=int(M*heads*S*S*2),transcendentals=0),
    )(qkv,qkv,qkv,dcT,ctxT,p,linv,pk,pq)


def bucket_index(offset_of):
    middle = BUCKETS // 2
    sign_of = np.sign(offset_of)
    magnitude = np.where(
        (offset_of < middle) & (offset_of > -middle), middle - 1, np.abs(offset_of)
    )
    log_pos = (
        np.ceil(np.log(magnitude / middle) / np.log((MAX_POS - 1) / middle) * (middle - 1)) + middle
    )
    bucket = np.where(magnitude <= middle, offset_of, log_pos * sign_of)
    return np.clip(bucket + BUCKETS, 0, 2 * BUCKETS - 1)


def pick_rows(offsets):
    return (bucket_index(offsets)[:, None] == np.arange(2 * BUCKETS)[None, :]).astype(np.float32)


def tn(a, b):
    return lax.dot_general(a, b, (((0,), (0,)), ((), ())), preferred_element_type=f32)


def normalize(values):
    centred = values - jnp.mean(values, -1, keepdims=True)
    inverse = lax.rsqrt(jnp.mean(centred * centred, -1, keepdims=True) + NORM_EPS)
    return centred * inverse, inverse


def normalize_back(grad, normed, inverse):
    return inverse * (
        grad
        - jnp.mean(grad, -1, keepdims=True)
        - normed * jnp.mean(grad * normed, -1, keepdims=True)
    )


def gelu_slope(values):
    cumulative = 0.5 * (1.0 + lax.erf(values * (1.0 / math.sqrt(2.0))))
    density = jnp.exp(-0.5 * values * values) * (1.0 / math.sqrt(2.0 * math.pi))
    return cumulative + values * density


def per_device(
    tokens, lengths, boundary,
    w_query, b_query, w_key, b_key, w_value, b_value, w_out, b_out,
    first_gain, first_shift, w_up, b_up, w_down, b_down,
    second_gain, second_shift, rel_table, type_table, out_grad,
):
    micros, seqs, seq_len, features = tokens.shape
    rows = micros * seqs * seq_len
    heads = features // HEAD_DIM
    gather = lambda a: lax.all_gather(a, "fsdp", axis=0, tiled=True)
    vectors = (b_query, b_key, b_value, b_out, first_gain, first_shift, b_up, b_down,
               second_gain, second_shift, type_table[0], type_table[1])
    sizes = [v.shape[0] for v in vectors]
    packed = gather(jnp.concatenate(vectors)[None, :])
    ends = np.cumsum([0] + sizes)
    wide = [packed[:, a:b].reshape(-1).astype(f32) for a, b in zip(ends[:-1], ends[1:])]
    (v_query, v_key, v_value, v_out, g_first, s_first, v_up, v_down, g_second, s_second,
     type_zero, type_one) = wide
    w_qkv = gather(jnp.concatenate([w_query, w_key, w_value], axis=1))
    rel = gather(rel_table)
    w_o = gather(w_out)
    w_u = gather(w_up)
    w_d = gather(w_down)

    offsets = np.clip(np.arange(2 * seq_len) - (seq_len - 1), 1 - seq_len, seq_len - 1)
    pick = jnp.asarray(pick_rows(offsets), bf)
    pick_back = jnp.asarray(pick_rows(-offsets), bf)

    positions = jnp.arange(seq_len)
    second_part = (positions[None, None, :] >= boundary[:, :, None]).reshape(rows, 1)
    summed = tokens.reshape(rows, features).astype(f32) + jnp.where(second_part, type_one, type_zero)
    summed_low = summed.astype(bf)
    v_qkv = jnp.concatenate([v_query, v_key, v_value])
    qkv = (nn(summed_low, w_qkv) + v_qkv).astype(bf)
    pos = (nn(rel, w_qkv[:, : 2 * features]) + v_qkv[: 2 * features]).astype(bf)
    pos_query, pos_key = pos[:, :features], pos[:, features:]
    key_rows = nn(pick, pos_key).astype(bf)
    key_rows_back = nn(pick_back, pos_key).astype(bf)
    query_rows = nn(pick, pos_query).astype(bf)
    flat_lengths = lengths.reshape(-1)
    context_t, probs, inverse_total = attn_fwd(qkv, key_rows_back, query_rows, flat_lengths, heads)
    attended = tn(context_t, w_o) + v_out
    first_normed, first_inverse = normalize(summed + attended)
    hidden = first_normed * g_first + s_first
    hidden_low = hidden.astype(bf)
    raised = nn(hidden_low, w_u) + v_up
    active = jax.nn.gelu(raised, approximate=False).astype(bf)
    second_normed, second_inverse = normalize(hidden + nn(active, w_d) + v_down)
    layer_out = (second_normed * g_second + s_second).astype(bf).reshape(tokens.shape)

    grad_output = out_grad.reshape(rows, features).astype(f32)
    d_second_gain = jnp.sum(grad_output * second_normed, 0)
    d_second_shift = jnp.sum(grad_output, 0)
    grad_mixed = normalize_back(grad_output * g_second, second_normed, second_inverse)
    grad_ffn = grad_mixed.astype(bf)
    d_w_down = tn(active, grad_ffn)
    d_b_down = jnp.sum(grad_ffn.astype(f32), 0)
    grad_raised = (nt(grad_ffn, w_d) * gelu_slope(raised)).astype(bf)
    d_w_up = tn(hidden_low, grad_raised)
    d_b_up = jnp.sum(grad_raised.astype(f32), 0)
    grad_hidden = nt(grad_raised, w_u) + grad_mixed
    d_first_gain = jnp.sum(grad_hidden * first_normed, 0)
    d_first_shift = jnp.sum(grad_hidden, 0)
    grad_first = normalize_back(grad_hidden * g_first, first_normed, first_inverse)
    grad_attended = grad_first.astype(bf)
    d_w_out = nn(context_t, grad_attended)
    d_b_out = jnp.sum(grad_attended.astype(f32), 0)
    grad_context_t = nt(w_o, grad_attended).astype(bf)
    d_query, d_key, d_value, key_off, query_off = attn_bwd(
        qkv, grad_context_t, context_t, probs, inverse_total, key_rows, query_rows
    )
    grad_pos_key = lax.dot_general(
        pick, key_off.astype(bf), (((0,), (1,)), ((), ())), preferred_element_type=f32)
    grad_pos_query = lax.dot_general(
        pick, query_off.astype(bf), (((0,), (1,)), ((), ())), preferred_element_type=f32)
    low_pos_key = grad_pos_key.astype(bf)
    low_pos_query = grad_pos_query.astype(bf)
    d_w_query = tn(summed_low, d_query) + tn(rel, low_pos_query)
    d_w_key = tn(summed_low, d_key) + tn(rel, low_pos_key)
    d_w_value = tn(summed_low, d_value)
    d_b_query = jnp.sum(d_query.astype(f32), 0) + jnp.sum(grad_pos_query, 0)
    d_b_key = jnp.sum(d_key.astype(f32), 0) + jnp.sum(grad_pos_key, 0)
    d_b_value = jnp.sum(d_value.astype(f32), 0)
    w_q, w_k, w_v = w_qkv[:, :features], w_qkv[:, features : 2 * features], w_qkv[:, 2 * features :]
    d_rel = nt(low_pos_key, w_k) + nt(low_pos_query, w_q)
    grad_summed = nt(d_query, w_q) + nt(d_key, w_k) + nt(d_value, w_v) + grad_first
    whole = jnp.sum(grad_summed, 0)
    d_type_one = jnp.sum(jnp.where(second_part, grad_summed, 0.0), 0)
    tokens_grad = grad_summed.astype(bf).reshape(tokens.shape)

    share = lambda a: lax.psum_scatter(a.astype(bf), "fsdp", scatter_dimension=0, tiled=True)
    s_down, s_up, s_out = share(d_w_down), share(d_w_up), share(d_w_out)
    s_q, s_k, s_v, s_rel = share(d_w_query), share(d_w_key), share(d_w_value), share(d_rel)
    small = (d_b_query, d_b_key, d_b_value, d_b_out, d_first_gain, d_first_shift, d_b_up, d_b_down,
             d_second_gain, d_second_shift, whole - d_type_one, d_type_one)
    devices = lax.axis_size("fsdp")
    small = jnp.concatenate([a.reshape(devices, -1) for a in small], axis=1)
    small = lax.psum(small, ("rep", "fsdp"))
    small = lax.dynamic_index_in_dim(small, lax.axis_index("fsdp"), 0, keepdims=False)
    (d_b_query, d_b_key, d_b_value, d_b_out, d_first_gain, d_first_shift, d_b_up, d_b_down,
     d_second_gain, d_second_shift, d_type_zero, d_type_one) = [
        small[a:b] for a, b in zip(ends[:-1], ends[1:])]
    total = lambda a: lax.psum(a, "rep").astype(f32)
    return (
        layer_out, tokens_grad,
        total(s_q), d_b_query, total(s_k), d_b_key, total(s_v), d_b_value, total(s_out), d_b_out,
        d_first_gain, d_first_shift, total(s_up), d_b_up, total(s_down), d_b_down,
        d_second_gain, d_second_shift, total(s_rel), jnp.stack([d_type_zero, d_type_one]),
    )


def solution(mesh):
    seq = P(None, ("rep", "fsdp"), None, None)
    flat = P(None, ("rep", "fsdp"))
    mat, vec = P("fsdp", None), P("fsdp")
    weights = (mat, vec, mat, vec, mat, vec, mat, vec, vec, vec, mat, vec, mat, vec, vec, vec, mat,
               P(None, "fsdp"))
    return jax.shard_map(
        per_device,
        mesh=mesh,
        in_specs=(seq, flat, flat) + weights + (seq,),
        out_specs=(seq, seq) + weights,
        check_vma=False,
    )
```

time: 1810 us -> 683 us (0.38)
  local copies, waits for them, and re-layouts: 844 us -> 20.3 us
  matrix products: 351 us -> 144 us
  waiting for transfers between devices: 422 us -> 264 us
  Pallas kernels: 0 us -> 113 us
  other arithmetic: 57.1 us -> 27.9 us
  blocking collectives: 106 us -> 86.9 us
    unnamed x434 -> x84, local copies, waits for them, and re-layouts: 365 us -> 9.7 us
    reshape x8, local copies, waits for them, and re-layouts: 307 us -> 0.51 us  [per_device(): small = jnp.concatenate([a.reshape(devices, -1) for a in small], axis=1)]
    dot_general x72 -> x26, matrix products: 318 us -> 144 us  [the longest x8 63 us: nn(): lax.dot_general(a, b, (((1,), (0,)), ((), ())), preferred_element_type=f32)]
    pallas_call x0 -> x2, Pallas kernels: none -> 113 us  [the longest x1 76.4 us: attn_bwd(): pl.pallas_call(attn_bwd_kernel, grid=(NP, M), in_specs=[tok(0), tok(NP),...]
    pad x8 -> x0, local copies, waits for them, and re-layouts: 78.9 us -> none  [the longest x4 42.9 us: realign(): flattened[..., row_count - 1:row_count - 1 + row_count * (columns - 1)]]
    slice x9 -> x2, local copies, waits for them, and re-layouts: 78.5 us -> 1.29 us  [per_device(): small[a:b]]
    reduce_scatter x14 -> x7, waiting for transfers between devices: 308 us -> 231 us  [per_device(): lax.psum_scatter(a.astype(bf), 'fsdp', scatter_dimension=0, tiled=True)]
    unnamed x25 -> x12, waiting for transfers between devices: 59.3 us -> 2.05 us
  transfers between devices with their start and end apart: 23 -> 12, of which waited for: 10 -> 8; matrix products, arithmetic and copies ran while one was open for 47% -> 19% of each run, Pallas kernels for 0% -> 5%
where the time goes in v1:
time: 683 us; the launch traced here: 673 us
  waiting for transfers between devices  264 us (39%)
  matrix products  144 us (21%)
  Pallas kernels  113 us (17%)
  blocking collectives  86.9 us (13%)
  other arithmetic  27.9 us (4%)
  local copies, waits for them, and re-layouts  20.3 us (3%)
  between operations  15.9 us (2%)
    reduce_scatter x7, waiting for transfers between devices, per_device(): lax.psum_scatter(a.astype(bf), 'fsdp', scatter_dimension=0, tiled=True)  231 us
    pallas_call x1, Pallas kernels, attn_bwd(): pl.pallas_call(attn_bwd_kernel, grid=(NP, M), in_specs=[tok(0), tok(NP),...  76.4 us
    dot_general x8, matrix products, nn(): lax.dot_general(a, b, (((1,), (0,)), ((), ())), preferred_element_type=f32)  63 us
    dot_general x8, matrix products, tn(): lax.dot_general(a, b, (((0,), (0,)), ((), ())), preferred_element_type=f32)  39.8 us
    dot_general x8, matrix products, nt(): lax.dot_general(a, b, (((1,), (1,)), ((), ())), preferred_element_type=f32)  39.2 us
    psum x1, blocking collectives, per_device(): small = lax.psum(small, ('rep', 'fsdp'))  38.2 us
    pallas_call x1, Pallas kernels, attn_fwd(): pl.pallas_call(attn_fwd_kernel, grid_spec=pltpu.PrefetchScalarGridSpec(nu...  36.5 us
    unnamed x1, blocking collectives  31.6 us
  transfers between devices with their start and end apart: 12, of which 8 were waited for; matrix products, arithmetic and copies ran while one was open for 19% of the time, Pallas kernels for 5%

profile of v1, /device:TPU:0, one launch (start us, length us, event | category | flops | bytes accessed | tf_op | source)
XLA Modules:
  0.0 673.4 jit_solution(17890625892091533988)
XLA Ops:
  14.0 6.8 %concatenate.15 = bf16[1440]{0:T(1024)(128)(2,1)S(1)} concatenate(bf16[96]{0:T(256)(128)(2,1)} %param.28, bf16[96]{0:T(256)(128)(2,1)} %param.30, bf16[96]{0:T(256)(128)(2,1)} %param.32, bf16[96]{0:T(256)(128)(2,1)} %param.34, bf16[96]{0:T(256)(128)(2,1)} %param.35, bf16[96]{0:T(256)(128)(2,1)} %param.36, bf16[384]{0:T(512)(128)(2,1)} %param.38, bf16[96]{0:T(256)(128)(2,1)} %param.40, ...), dimensions={0} | concatenate | bytes 5760 | tf_op jit(solution)/shard_map/concatenate | solution.py:245
  21.1 31.6 %all-reduce = bf16[11520]{0:T(1024)(128)(2,1)S(1)} all-reduce(bf16[11520]{0:T(1024)(128)(2,1)S(1)} %dynamic-update-slice), channel_id=2, replica_groups=mesh['rep'=4,'fsdp'=8] {'fsdp'}, use_global_device_ids=true, to_apply=%add | all-reduce | flops 11520 | bytes 46080
  54.1 17.1 %all_gather.20 = bf16[512,768]{1,0:T(8,128)(2,1)S(1)} all-gather(bf16[64,768]{1,0:T(8,128)(2,1)} %param.43), channel_id=1, replica_groups=mesh['rep'=4,'fsdp'=8] {'fsdp'}, dimensions={0}, use_global_device_ids=true | all-gather | bytes 884736 | tf_op jit(solution)/shard_map/all_gather | solution.py:241
  72.9 3.0 fusion.23
  75.9 3.3 fusion.26
  84.9 4.0 add_convert_fusion.q_ref.k_ref.v_ref
  89.0 36.5 %shard_map.386 = (bf16[768,1024]{1,0:T(8,128)(2,1)S(1)}, bf16[2,12,512,512]{3,2,1,0:T(8,128)(2,1)}, f32[2,6,2,512]{3,2,1,0:T(2,128)S(1)}) custom-call(s32[2]{0:T(128)S(1)} %bitcast.108, bf16[1024,2304]{1,0:T(8,128)(2,1)S(1)} %add_convert_fusion.q_ref.k_ref.v_ref, bf16[1024,2304]{1,0:T(8,128)(2,1)S(1)} %add_convert_fusion.q_ref.k_ref.v_ref, ...), custom_call_target="tpu_custom_call" | custom-call | flops 9663676416 | bytes 12582912 | tf_op jit(solution)/shard_map/pallas_call | solution.py:87
  127.6 5.6 fusion.62
  135.6 37.4 %fusion.2 = (bf16[1024,3072]{1,0:T(8,128)(2,1)}, f32[1024,3072]{1,0:T(8,128)}) fusion(f32[3072]{0:T(1024)S(1)} %reshape.273, bf16[768,3072]{1,0:T(8,128)(2,1)} %all-gather.10.cloned.1.call-done, f32[1024,768]{1,0:T(8,128)} %get-tuple-element.124, f32[768]{0:T(1024)S(1)} %reshape.272, f32[768]{0:T(1024)S(1)} %reshape.271, f32[1024]{0:T(1024)S(1)} %add_rsqrt_fusion.1, ...), kind=kOutput, calls=%fused_computation.4 | convolution fusion | flops 5043388416 | bytes 26765312 | tf_op jit(solution)/shard_map/dot_general | solution.py:21
  173.0 11.3 %all-gather.12.cloned.1.call-done = bf16[3072,768]{1,0:T(8,128)(2,1)} async-done(((bf16[384,768]{1,0:T(8,128)(2,1)}), bf16[3072,768]{1,0:T(8,128)(2,1)}) %all-gather.12.cloned.1.call-update) | async-done | bytes 4718608 | tf_op jit(solution)/shard_map/all_gather | solution.py:241
  184.3 9.3 %fusion.63 = (f32[1024]{0:T(1024)S(1)}, f32[1024,768]{1,0:T(8,128)S(1)}) fusion(f32[768]{0:T(1024)S(1)} %reshape.274, bf16[1024,3072]{1,0:T(8,128)(2,1)} %get-tuple-element.125, bf16[3072,768]{1,0:T(8,128)(2,1)} %all-gather.12.cloned.1.call-done, f32[768]{0:T(1024)S(1)} %reshape.272, f32[768]{0:T(1024)S(1)} %reshape.271, f32[1024]{0:T(1024)S(1)} %add_rsqrt_fusion.1, ...), kind=kOutput, calls=%fused_computation.146 | convolution fusion | flops 4837342208 | bytes 17323008 | tf_op jit(solution)/shard_map/dot_general | solution.py:21
  195.4 2.7 convert_reduce_fusion.2
  198.2 13.3 %convert_reduce_fusion = (f32[3072]{0:T(1024)S(1)}, bf16[1024,3072]{1,0:T(8,128)(2,1)S(1)}) fusion(f32[1024,3072]{1,0:T(8,128)} %get-tuple-element.126, f32[3072]{0:T(1024)S(1)} %reshape.273, bf16[3072,768]{1,0:T(8,128)(2,1)S(1)} %copy-done.31, f32[1024,768]{1,0:T(8,128)S(1)} %get-tuple-element.94), kind=kOutput, calls=%fused_computation.11 | convolution fusion | flops 4873516032 | bytes 26763264 | tf_op jit(solution)/shard_map/dot_general | solution.py:22
  211.5 10.1 %multiply_reduce_fusion = (f32[768]{0:T(1024)S(1)}, f32[1024]{0:T(1024)S(1)}, f32[1024]{0:T(1024)S(1)}, f32[768]{0:T(1024)S(1)}, f32[1024,768]{1,0:T(8,128)S(1)}) fusion(f32[1024,768]{1,0:T(8,128)} %get-tuple-element.124, f32[1024]{0:T(1024)S(1)} %add_rsqrt_fusion.1, f32[1024]{0:T(1024)S(1)} %broadcast_multiply_fusion.4, f32[768]{0:T(1024)S(1)} %reshape.271, ...), kind=kOutput, calls=%fused_computation.45 | convolution fusion | flops 4839698432 | bytes 20472832 | tf_op jit(solution)/shard_map/dot_general | solution.py:22
  227.8 76.4 %shard_map.387 = (bf16[1024,768]{1,0:T(8,128)(2,1)S(1)}, bf16[1024,768]{1,0:T(8,128)(2,1)S(1)}, bf16[1024,768]{1,0:T(8,128)(2,1)S(1)}, f32[768,1024]{1,0:T(8,128)S(1)}, f32[768,1024]{1,0:T(8,128)}) custom-call(bf16[1024,2304]{1,0:T(8,128)(2,1)} %copy-done.7, bf16[1024,2304]{1,0:T(8,128)(2,1)} %copy-done.7, bf16[1024,2304]{1,0:T(8,128)(2,1)} %copy-done.7, ...), custom_call_target="tpu_custom_call" | custom-call | flops 19327352832 | bytes 12582912 | tf_op jit(solution)/shard_map/pallas_call | solution.py:176
  310.7 3.5 fusion.67
  316.1 4.8 convolution_convert_fusion.6
  321.2 3.0 fusion.66
  326.2 3.9 convolution_convert_fusion.7
  330.1 9.7 %convolution_convert_fusion = bf16[3072,768]{1,0:T(8,128)(2,1)} fusion(bf16[1024,3072]{1,0:T(8,128)(2,1)} %get-tuple-element.125, f32[1024,768]{1,0:T(8,128)} %copy-done.14), kind=kOutput, calls=%fused_computation.28 | convolution fusion | flops 4834983936 | bytes 14155776 | tf_op jit(solution)/shard_map/dot_general | solution.py:209
  339.9 10.5 %convolution_convert_fusion.1 = bf16[768,3072]{1,0:T(8,128)(2,1)} fusion(bf16[1024,3072]{1,0:T(8,128)(2,1)} %copy-done.37, f32[1024,768]{1,0:T(8,128)} %get-tuple-element.124, f32[768]{0:T(1024)S(1)} %reshape.272, f32[768]{0:T(1024)S(1)} %reshape.271, f32[1024]{0:T(1024)S(1)} %add_rsqrt_fusion.1, f32[1024]{0:T(1024)S(1)} %broadcast_multiply_fusion.4), kind=kOutput, calls=%fused_computation.29 | convolution fusion | flops 4838129664 | bytes 14170112 | tf_op jit(solution)/shard_map/dot_general | solution.py:209
  351.1 4.8 fusion.41
  356.0 18.9 %reduce-scatter.10.cloned.1.call-done = bf16[96,768]{1,0:T(8,128)(2,1)} async-done(((bf16[768,768]{1,0:T(8,128)(2,1)}), bf16[96,768]{1,0:T(8,128)(2,1)}) %reduce-scatter.10.cloned.1.call-update) | async-done | bytes 147472 | tf_op jit(solution)/shard_map/reduce_scatter | solution.py:322
  374.9 33.3 %reduce-scatter.14.cloned.1.call-done = bf16[96,768]{1,0:T(8,128)(2,1)} async-done(((bf16[768,768]{1,0:T(8,128)(2,1)}), bf16[96,768]{1,0:T(8,128)(2,1)}) %reduce-scatter.14.cloned.1.call-update) | async-done | bytes 147472 | tf_op jit(solution)/shard_map/reduce_scatter | solution.py:322
  408.2 34.0 %reduce-scatter.8.cloned.1.call-done = bf16[96,768]{1,0:T(8,128)(2,1)} async-done(((bf16[768,768]{1,0:T(8,128)(2,1)}), bf16[96,768]{1,0:T(8,128)(2,1)}) %reduce-scatter.8.cloned.1.call-update) | async-done | bytes 147472 | tf_op jit(solution)/shard_map/reduce_scatter | solution.py:322
  442.2 33.6 %reduce-scatter.12.cloned.1.call-done = bf16[96,768]{1,0:T(8,128)(2,1)} async-done(((bf16[768,768]{1,0:T(8,128)(2,1)}), bf16[96,768]{1,0:T(8,128)(2,1)}) %reduce-scatter.12.cloned.1.call-update) | async-done | bytes 147472 | tf_op jit(solution)/shard_map/reduce_scatter | solution.py:322
  475.8 55.5 %reduce-scatter.18.cloned.1.call-done = bf16[384,768]{1,0:T(8,128)(2,1)} async-done(((bf16[3072,768]{1,0:T(8,128)(2,1)}), bf16[384,768]{1,0:T(8,128)(2,1)}) %reduce-scatter.18.cloned.1.call-update) | async-done | bytes 589840 | tf_op jit(solution)/shard_map/reduce_scatter | solution.py:322
  531.4 55.8 %reduce-scatter.16.cloned.1.call-done = bf16[96,3072]{1,0:T(8,128)(2,1)} async-done(((bf16[768,3072]{1,0:T(8,128)(2,1)}), bf16[96,3072]{1,0:T(8,128)(2,1)}) %reduce-scatter.16.cloned.1.call-update) | async-done | bytes 589840 | tf_op jit(solution)/shard_map/reduce_scatter | solution.py:322
  587.2 2.8 fusion.44
  590.4 4.2 select_reduce_fusion
  598.1 38.2 %psum.57 = f32[8,1440]{1,0:T(8,128)S(1)} all-reduce(f32[8,1440]{1,0:T(8,128)S(1)} %concatenate.19), channel_id=1, replica_groups=mesh['rep'=4,'fsdp'=8] {'rep','fsdp'}, use_global_device_ids=true, to_apply=%region_24.25 | all-reduce | flops 11520 | bytes 92160 | tf_op jit(solution)/shard_map/psum | solution.py:329
  638.2 19.9 %all-reduce.4.cloned.1.call-done = (bf16[96,768]{1,0:T(8,128)(2,1)}, bf16[96,768]{1,0:T(8,128)(2,1)}, bf16[96,768]{1,0:T(8,128)(2,1)}, bf16[96,768]{1,0:T(8,128)...) async-done(((bf16[96,768]{1,0:T(8,128)(2,1)}, bf16[96,768]{1,0:T(8,128)(2,1)}, bf16[96,768]{1,0:T(8,128)(2,1)}, ...) | async-done | bytes 1867792 | tf_op jit(solution)/shard_map/psum | solution.py:334
  (185 shorter events, 52.7 us)
Async XLA Ops:
  7.2 64.4 %copy-start.8 = (bf16[2,1,512,768]{3,2,1,0:T(8,128)(2,1)S(1)}, bf16[2,1,512,768]{3,2,1,0:T(8,128)(2,1)}, u32[]{:S(2)}) copy-start(bf16[2,1,512,768]{3,2,1,0:T(8,128)(2,1)} %param.45) | copy-start | bytes 4718596
  7.2 68.7 %all-gather.6.cloned.1.call-start = ((), (), s32[]{:S(2)}) async-start(), calls=%async_computation.7 | async-start | bytes 3981312 | tf_op jit(solution)/shard_map/all_gather | solution.py:241
  9.2 118.3 %all-gather.8.cloned.1.call-start = ((), (), s32[]{:S(2)}) async-start(), calls=%async_computation.8 | async-start | bytes 1327104 | tf_op jit(solution)/shard_map/all_gather | solution.py:241
  10.0 125.6 %all-gather.10.cloned.1.call-start = ((), (), s32[]{:S(2)}) async-start(), calls=%async_computation.9 | async-start | bytes 5308416 | tf_op jit(solution)/shard_map/all_gather | solution.py:241
  10.7 173.6 %all-gather.12.cloned.1.call-start = ((), (), s32[]{:S(2)}) async-start(), calls=%async_computation.10 | async-start | bytes 5308416 | tf_op jit(solution)/shard_map/all_gather | solution.py:241
  11.3 344.7 %reduce-scatter.20.cloned.1.call-start = ((), (), s32[]{:S(2)}) async-start(), calls=%async_computation.17 | async-start | bytes 884736 | tf_op jit(solution)/shard_map/reduce_scatter | solution.py:322
  54.1 73.5 %copy-start.29 = (pred[1024]{0:T(1024)(128)(4,1)}, pred[1024]{0:T(1024)(128)(4,1)S(1)}, u32[]{:S(2)}) copy-start(pred[1024]{0:T(1024)(128)(4,1)S(1)} %ge.25) | copy-start | bytes 3076
  71.2 8.0 %copy-start.11 = (bf16[512,768]{1,0:T(8,128)(2,1)}, bf16[512,768]{1,0:T(8,128)(2,1)S(1)}, u32[]{:S(2)}) copy-start(bf16[512,768]{1,0:T(8,128)(2,1)S(1)} %all_gather.20) | copy-start | bytes 2359300
  80.3 8.7 %copy-start.2 = (bf16[1024,768]{1,0:T(8,128)(2,1)}, bf16[1024,768]{1,0:T(8,128)(2,1)S(1)}, u32[]{:S(2)}) copy-start(bf16[1024,768]{1,0:T(8,128)(2,1)S(1)} %fusion.36.pq_ref) | copy-start | bytes 4718596
  84.9 4.0 copy-start.1
  127.5 5.7 copy-start.5
  195.4 16.1 %slice-start = ((s8[4718592]{0:T(1024)(128)(4,1)}), s8[4194304]{0:T(1024)(128)(4,1)S(1)}, s32[]{:S(2)}) async-start(s8[4718592]{0:T(1024)(128)(4,1)} %bitcast.114), calls=%async_computation.19 | async-start | bytes 8388608
  198.2 13.3 %copy-start.14 = (f32[1024,768]{1,0:T(8,128)}, f32[1024,768]{1,0:T(8,128)S(1)}, u32[]{:S(2)}) copy-start(f32[1024,768]{1,0:T(8,128)S(1)} %get-tuple-element.94) | copy-start | bytes 9437188
  198.2 13.3 %slice-start.1 = ((s8[4718592]{0:T(1024)(128)(4,1)}), s8[524288]{0:T(1024)(128)(4,1)S(1)}, s32[]{:S(2)}) async-start(s8[4718592]{0:T(1024)(128)(4,1)} %bitcast.114), calls=%async_computation.20 | async-start | bytes 1048576
  211.5 10.2 %copy-start.37 = (bf16[1024,3072]{1,0:T(8,128)(2,1)}, bf16[1024,3072]{1,0:T(8,128)(2,1)S(1)}, u32[]{:S(2)}) copy-start(bf16[1024,3072]{1,0:T(8,128)(2,1)S(1)} %get-tuple-element.136) | copy-start | bytes 18874372
  227.8 76.4 %copy-start.34 = (bf16[1024,512]{1,0:T(8,128)(2,1)S(1)}, bf16[1024,512]{1,0:T(8,128)(2,1)}, u32[]{:S(2)}) copy-start(bf16[1024,512]{1,0:T(8,128)(2,1)} %constant.91.clone) | copy-start | bytes 3145732
  304.2 3.8 copy-start
  305.3 3.6 copy-start.19
  310.6 64.2 %reduce-scatter.10.cloned.1.call-start = ((), (), s32[]{:S(2)}) async-start(), calls=%async_computation.12 | async-start | bytes 1327104 | tf_op jit(solution)/shard_map/reduce_scatter | solution.py:322
  310.7 3.5 copy-start.12
  310.7 3.5 copy-start.20
  316.1 92.1 %reduce-scatter.14.cloned.1.call-start = ((), (), s32[]{:S(2)}) async-start(), calls=%async_computation.14 | async-start | bytes 1327104 | tf_op jit(solution)/shard_map/reduce_scatter | solution.py:322
  321.0 121.3 %reduce-scatter.8.cloned.1.call-start = ((), (), s32[]{:S(2)}) async-start(), calls=%async_computation.11 | async-start | bytes 1327104 | tf_op jit(solution)/shard_map/reduce_scatter | solution.py:322
  326.2 149.7 %reduce-scatter.12.cloned.1.call-start = ((), (), s32[]{:S(2)}) async-start(), calls=%async_computation.13 | async-start | bytes 1327104 | tf_op jit(solution)/shard_map/reduce_scatter | solution.py:322
  330.1 201.3 %reduce-scatter.18.cloned.1.call-start = ((), (), s32[]{:S(2)}) async-start(), calls=%async_computation.16 | async-start | bytes 5308416 | tf_op jit(solution)/shard_map/reduce_scatter | solution.py:322
  339.8 247.3 %reduce-scatter.16.cloned.1.call-start = ((), (), s32[]{:S(2)}) async-start(), calls=%async_computation.15 | async-start | bytes 5308416 | tf_op jit(solution)/shard_map/reduce_scatter | solution.py:322
  350.4 307.7 %all-reduce.4.cloned.1.call-start = ((), (), s32[]{:S(2)}) async-start(), calls=%async_computation.18 | async-start | bytes 3735552 | tf_op jit(solution)/shard_map/psum | solution.py:334
  658.1 4.4 copy-start.26
  658.1 5.1 copy-start.25
  658.1 5.9 copy-start.24
  658.1 6.6 copy-start.23
  658.1 7.4 %copy-start.27 = (bf16[64,768]{1,0:T(8,128)(2,1)S(1)}, bf16[64,768]{1,0:T(8,128)(2,1)}, u32[]{:S(2)}) copy-start(bf16[64,768]{1,0:T(8,128)(2,1)} %get-tuple-element.92) | copy-start | bytes 294916
  (20 other events, 50.0 us)
Sparse Core Ops, SparseCore 0:
  10.2 44.8 all-gather.5
  56.8 22.4 all-gather.7
  80.9 51.3 all-gather.9
  133.8 50.5 all-gather.11
  310.8 30.3 reduce-scatter.19
  344.0 30.8 reduce-scatter.9
  377.3 30.8 reduce-scatter.13
  411.2 31.0 reduce-scatter.7
  444.6 31.1 reduce-scatter.11
  478.1 53.2 reduce-scatter.17
  533.8 53.3 reduce-scatter.15
  591.5 66.5 all-reduce.3

commit v2 on v1

--- a/solution.py
+++ b/solution.py
@@ -70,16 +70,16 @@
         tot=None
         for b in range(nb):
             js=slice(b*BLK,(b+1)*BLK)
-            p=jnp.exp2(s_scr[js,:]*scale-top)
-            t=jnp.sum(p,axis=0,keepdims=True)
+            p=jnp.exp2(s_scr[js,:]*scale-top).astype(bf)
+            t=jnp.sum(p.astype(f32),axis=0,keepdims=True)
             tot=t if tot is None else tot+t
-            p_ref[0,h,js,:]=p.astype(bf)
+            p_ref[0,h,js,:]=p
         linv=jnp.where(pos<length,1.0/tot,0.0)
         linv_ref[0,0,h:h+1,:]=linv
         ctx=nn(vT[h*HEAD_DIM:(h+1)*HEAD_DIM,:],p_ref[0,h])*linv
         ctxT_ref[h*HEAD_DIM:(h+1)*HEAD_DIM,:]=ctx.astype(bf)
 
-def attn_fwd(qkv,pkr,pq,lengths,heads):
+def attn_fwd(q,k,v,pkr,pq,lengths,heads):
     M=lengths.shape[0]; D=heads*HEAD_DIM
     S=pq.shape[0]//2
     NP=heads//2; L=2*HEAD_DIM
@@ -90,8 +90,8 @@
             num_scalar_prefetch=1,grid=grid,
             in_specs=[
                 pl.BlockSpec((S,L),lambda p,m,_:(m,p)),
-                pl.BlockSpec((S,L),lambda p,m,_:(m,NP+p)),
-                pl.BlockSpec((S,L),lambda p,m,_:(m,2*NP+p)),
+                pl.BlockSpec((S,L),lambda p,m,_:(m,p)),
+                pl.BlockSpec((S,L),lambda p,m,_:(m,p)),
                 pl.BlockSpec((2*S,L),lambda p,m,_:(0,p)),
                 pl.BlockSpec((2*S,L),lambda p,m,_:(0,p)),
             ],
@@ -105,9 +105,9 @@
         out_shape=[jax.ShapeDtypeStruct((D,M*S),bf),jax.ShapeDtypeStruct((M,heads,S,S),bf),jax.ShapeDtypeStruct((M,NP,2,S),f32)],
         compiler_params=pltpu.CompilerParams(vmem_limit_bytes=40*1024*1024),
         cost_estimate=pl.CostEstimate(flops=int(2*M*heads*S*S*64*12),bytes_accessed=int(M*heads*S*S*2),transcendentals=M*heads*S*S),
-    )(lengths,qkv,qkv,qkv,pkr,pq)
-
-def attn_bwd_kernel(q_ref,k_ref,v_ref,dcT_ref,ctxT_ref,p_ref,linv_ref,pk_ref,pq_ref,dq_ref,dk_ref,dv_ref,ko_ref,qo_ref,ds_scr):
+    )(lengths,q,k,v,pkr,pq)
+
+def attn_bwd_kernel(q_ref,k_ref,v_ref,dcT_ref,p_ref,linv_ref,pk_ref,pq_ref,dq_ref,dk_ref,dv_ref,ko_ref,qo_ref,ds_scr,p_scr,t_scr):
     S=q_ref.shape[0]
     nb=S//BLK
     W=S+BLK
@@ -137,17 +137,24 @@
         pkh=jnp.where(mine_t,pk_ref[...],zero); pqh=jnp.where(mine_t,pq_ref[...],zero)
         linv=linv_ref[0,0,h:h+1,:]
         dc=dcT_ref[hs,:].astype(f32)*linv
-        delta=jnp.sum(dc*ctxT_ref[hs,:].astype(f32),axis=0,keepdims=True)*scale
         dcl=dc.astype(bf); dcs=(dc*scale).astype(bf)
         def wide(x): return jnp.concatenate([x,zrow] if h==0 else [zrow,x],axis=0)
         t=nt(p_ref[0,h],wide(dcl))
         dv=t if dv is None else dv+t
         dcw=wide(dcs)
+        delta=None
         for b in range(nb):
             js=slice(b*BLK,(b+1)*BLK)
-            dp=nn(vr[js],dcw)
             p=nn(flip,p_ref[0,h,(nb-1-b)*BLK:(nb-b)*BLK,:])
-            ds=(p*(dp-delta)).astype(bf)
+            t=p*nn(vr[js],dcw)
+            p_scr[js,:]=p
+            t_scr[js,:]=t
+            t=jnp.sum(t,axis=0,keepdims=True)
+            delta=t if delta is None else delta+t
+        delta=delta*linv
+        for b in range(nb):
+            js=slice(b*BLK,(b+1)*BLK)
+            ds=(t_scr[js,:]-p_scr[js,:]*delta).astype(bf)
             ds_scr[js,:]=ds
             far=pltpu.roll(jnp.concatenate([ds,pad],axis=1),0,1,stride=1,stride_axis=0)
             st=b*BLK
@@ -167,7 +174,7 @@
         dq_ref[b*BLK:(b+1)*BLK,:]=dq[b].astype(bf)
         dk_ref[(nb-1-b)*BLK:(nb-b)*BLK,:]=nn(flip,dk[b].astype(bf)).astype(bf)
 
-def attn_bwd(qkv,dcT,ctxT,p,linv,pk,pq):
+def attn_bwd(q,k,v,dcT,p,linv,pk,pq):
     M,heads,S,_=p.shape; D=heads*HEAD_DIM
     NP=heads//2; L=2*HEAD_DIM
     tok=lambda off: pl.BlockSpec((S,L),lambda p,m:(m,off+p))
@@ -176,16 +183,16 @@
     return pl.pallas_call(
         attn_bwd_kernel,
         grid=(NP,M),
-        in_specs=[tok(0),tok(NP),tok(2*NP),colT,colT,
+        in_specs=[tok(0),tok(0),tok(0),colT,
             pl.BlockSpec((1,2,S,S),lambda p,m:(m,p,0,0)),
             pl.BlockSpec((1,1,2,S),lambda p,m:(m,p,0,0)),
             tab,tab],
         out_specs=[tok(0),tok(0),tok(0),pl.BlockSpec((L,2*S),lambda p,m:(p,0)),pl.BlockSpec((L,2*S),lambda p,m:(p,0))],
         out_shape=[jax.ShapeDtypeStruct((M*S,D),bf)]*3+[jax.ShapeDtypeStruct((D,2*S),f32)]*2,
-        scratch_shapes=[pltpu.VMEM((S,S),bf)],
+        scratch_shapes=[pltpu.VMEM((S,S),bf),pltpu.VMEM((S,S),f32),pltpu.VMEM((S,S),f32)],
         compiler_params=pltpu.CompilerParams(vmem_limit_bytes=40*1024*1024),
         cost_estimate=pl.CostEstimate(flops=int(2*M*heads*S*S*64*24),bytes_accessed=int(M*heads*S*S*2),transcendentals=0),
-    )(qkv,qkv,qkv,dcT,ctxT,p,linv,pk,pq)
+    )(q,k,v,dcT,p,linv,pk,pq)
 
 
 def bucket_index(offset_of):
@@ -227,6 +234,91 @@
     cumulative = 0.5 * (1.0 + lax.erf(values * (1.0 / math.sqrt(2.0))))
     density = jnp.exp(-0.5 * values * values) * (1.0 / math.sqrt(2.0 * math.pi))
     return cumulative + values * density
+
+
+TILE = 16
+
+
+def swap_core(a):
+    n = lax.axis_size("fsdp")
+    return lax.ppermute(a, "fsdp", [(i, i ^ 1) for i in range(n)])
+
+
+def swap_line(a):
+    n = lax.axis_size("fsdp")
+    groups = [list(range(c, n, 2)) for c in range(2)]
+    return lax.all_to_all(a, "fsdp", 0, 0, tiled=True, axis_index_groups=groups)
+
+
+def along_line(a, step):
+    n = lax.axis_size("fsdp")
+    return lax.ppermute(a, "fsdp", [(i, i + 2 * step) for i in range(n) if 0 <= i + 2 * step < n])
+
+
+def swap_rep(a):
+    return lax.all_to_all(a, "rep", 0, 0, tiled=True)
+
+
+def flip_rep(a, bit):
+    return lax.ppermute(a, "rep", [(i, i ^ bit) for i in range(lax.axis_size("rep"))])
+
+
+def spread(a, copies):
+    return jnp.broadcast_to(a[None], (copies,) + a.shape)
+
+
+def gather_rep(a):
+    reps = lax.axis_size("rep")
+    bits = [1 << k for k in range(reps.bit_length() - 1)]
+    width = a.shape[-1] // len(bits)
+    me = lax.axis_index("rep")
+    shares = []
+    for k in range(len(bits)):
+        share = a[None, ..., k * width : (k + 1) * width]
+        order = bits[k:] + bits[:k]
+        for bit in order:
+            other = flip_rep(share, bit)
+            high = (me // bit) % 2 == 1
+            share = jnp.concatenate([jnp.where(high, other, share), jnp.where(high, share, other)])
+        at = np.zeros(reps, np.int32)
+        for place in range(reps):
+            rep = sum(bit for i, bit in enumerate(order) if (place >> i) & 1)
+            at[rep] = place
+        shares.append(jnp.stack([share[int(p)] for p in at]))
+    return jnp.concatenate(shares, axis=-1)
+
+
+def gather_parts(mine, shard, *others):
+    places = lax.axis_size("fsdp") // 2
+    place = lax.axis_index("fsdp") // 2
+    steps = [k for d in range(1, places) for k in (d, -d)]
+    seen = {-k: along_line(mine, k) for k in steps}
+    line = jnp.stack([seen[k] for k in range(1 - places, places) if k])
+    line = lax.dynamic_slice_in_dim(line, places - 1 - place, places - 1, 0)
+    line, *others = lax.optimization_barrier((line, *others))
+    every = gather_rep(line)
+    at = jnp.arange(places)[None, :, None, None]
+    before = jnp.pad(every, ((0, 0), (0, 1), (0, 0), (0, 0)))
+    behind = jnp.pad(every, ((0, 0), (1, 0), (0, 0), (0, 0)))
+    every = jnp.where(at == place, shard[:, None], jnp.where(at < place, before, behind))
+    other = swap_core(every)
+    first = lax.axis_index("fsdp") % 2 == 0
+    return jnp.stack([jnp.where(first, every, other), jnp.where(first, other, every)], axis=2), others
+
+
+def reduce_core(values):
+    core = lax.axis_index("fsdp") % 2
+    keep = lax.dynamic_index_in_dim(values, core, 2, keepdims=False)
+    give = lax.dynamic_index_in_dim(values, 1 - core, 2, keepdims=False)
+    return (keep.astype(f32) + swap_core(give).astype(f32)).astype(bf)
+
+
+def summed_over(a):
+    return jnp.sum(a.astype(f32), 0).astype(bf)
+
+
+def pad_tail(a, rows, columns):
+    return jnp.pad(a, [(0, 0)] * (a.ndim - 2) + [(0, rows - a.shape[-2]), (0, columns - a.shape[-1])])
 
 
 def per_device(
@@ -238,20 +330,35 @@
     micros, seqs, seq_len, features = tokens.shape
     rows = micros * seqs * seq_len
     heads = features // HEAD_DIM
-    gather = lambda a: lax.all_gather(a, "fsdp", axis=0, tiled=True)
-    vectors = (b_query, b_key, b_value, b_out, first_gain, first_shift, b_up, b_down,
-               second_gain, second_shift, type_table[0], type_table[1])
-    sizes = [v.shape[0] for v in vectors]
-    packed = gather(jnp.concatenate(vectors)[None, :])
-    ends = np.cumsum([0] + sizes)
-    wide = [packed[:, a:b].reshape(-1).astype(f32) for a, b in zip(ends[:-1], ends[1:])]
-    (v_query, v_key, v_value, v_out, g_first, s_first, v_up, v_down, g_second, s_second,
-     type_zero, type_one) = wide
-    w_qkv = gather(jnp.concatenate([w_query, w_key, w_value], axis=1))
-    rel = gather(rel_table)
-    w_o = gather(w_out)
-    w_u = gather(w_up)
-    w_d = gather(w_down)
+    fs, reps = lax.axis_size("fsdp"), lax.axis_size("rep")
+    places = fs // 2
+    cut = w_query.shape[0]
+    unit = 4 * cut // reps
+    table_cut = rel_table.shape[0] // reps
+    up_parts = w_up.shape[1] // features
+    vectors = jnp.stack([b_query, b_key, b_value, b_out, first_gain, first_shift, b_down, second_gain,
+                         second_shift, type_table[0], type_table[1]] + [b_up[k * cut : (k + 1) * cut] for k in range(up_parts)])
+    vector_count = vectors.shape[0]
+    vector_rows = -(-vector_count // TILE) * TILE
+    vectors = pad_tail(vectors, vector_rows, features)
+    shard = jnp.concatenate([
+        jnp.stack([w_query, w_key, w_value, w_out]).reshape(reps, unit, features),
+        rel_table.reshape(reps, table_cut, features),
+        spread(vectors, reps)], axis=1)
+    mine = lax.dynamic_index_in_dim(shard, lax.axis_index("rep"), 0, keepdims=False)
+    first, (w_up, w_down) = gather_parts(mine, shard, w_up, w_down)
+    w_u = lax.all_gather(w_up, "fsdp", axis=0, tiled=True)
+    w_d = lax.all_gather(w_down, "fsdp", axis=0, tiled=True)
+    four = first[:, :, :, :unit].reshape(4, reps // 4, fs, unit, features).transpose(0, 2, 1, 3, 4)
+    four = four.reshape(4, features, features)
+    rel = first[:, :, :, unit : unit + table_cut].transpose(1, 2, 0, 3, 4).reshape(-1, features)
+    wide = first[0, :, :, unit + table_cut : unit + table_cut + vector_count, :cut].reshape(fs, vector_count, cut)
+    wide = wide.transpose(1, 0, 2).astype(f32)
+    v_up = wide[vector_count - up_parts :].transpose(1, 0, 2).reshape(-1)
+    wide = wide.reshape(vector_count, features)
+    (v_query, v_key, v_value, v_out, g_first, s_first, v_down, g_second, s_second,
+     type_zero, type_one) = [wide[k] for k in range(vector_count - up_parts)]
+    w_q, w_k, w_v, w_o = [four[k] for k in range(4)]
 
     offsets = np.clip(np.arange(2 * seq_len) - (seq_len - 1), 1 - seq_len, seq_len - 1)
     pick = jnp.asarray(pick_rows(offsets), bf)
@@ -261,15 +368,16 @@
     second_part = (positions[None, None, :] >= boundary[:, :, None]).reshape(rows, 1)
     summed = tokens.reshape(rows, features).astype(f32) + jnp.where(second_part, type_one, type_zero)
     summed_low = summed.astype(bf)
-    v_qkv = jnp.concatenate([v_query, v_key, v_value])
-    qkv = (nn(summed_low, w_qkv) + v_qkv).astype(bf)
-    pos = (nn(rel, w_qkv[:, : 2 * features]) + v_qkv[: 2 * features]).astype(bf)
-    pos_query, pos_key = pos[:, :features], pos[:, features:]
+    queries = (nn(summed_low, w_q) + v_query).astype(bf)
+    keys = (nn(summed_low, w_k) + v_key).astype(bf)
+    values = (nn(summed_low, w_v) + v_value).astype(bf)
+    pos_query = (nn(rel, w_q) + v_query).astype(bf)
+    pos_key = (nn(rel, w_k) + v_key).astype(bf)
     key_rows = nn(pick, pos_key).astype(bf)
     key_rows_back = nn(pick_back, pos_key).astype(bf)
     query_rows = nn(pick, pos_query).astype(bf)
     flat_lengths = lengths.reshape(-1)
-    context_t, probs, inverse_total = attn_fwd(qkv, key_rows_back, query_rows, flat_lengths, heads)
+    context_t, probs, inverse_total = attn_fwd(queries, keys, values, key_rows_back, query_rows, flat_lengths, heads)
     attended = tn(context_t, w_o) + v_out
     first_normed, first_inverse = normalize(summed + attended)
     hidden = first_normed * g_first + s_first
@@ -289,6 +397,9 @@
     grad_raised = (nt(grad_ffn, w_d) * gelu_slope(raised)).astype(bf)
     d_w_up = tn(hidden_low, grad_raised)
     d_b_up = jnp.sum(grad_raised.astype(f32), 0)
+    share = lambda a: lax.psum_scatter(a, "fsdp", scatter_dimension=0, tiled=True)
+    s_down = share(d_w_down.astype(bf))
+    s_up = share(d_w_up.astype(bf))
     grad_hidden = nt(grad_raised, w_u) + grad_mixed
     d_first_gain = jnp.sum(grad_hidden * first_normed, 0)
     d_first_shift = jnp.sum(grad_hidden, 0)
@@ -298,8 +409,11 @@
     d_b_out = jnp.sum(grad_attended.astype(f32), 0)
     grad_context_t = nt(w_o, grad_attended).astype(bf)
     d_query, d_key, d_value, key_off, query_off = attn_bwd(
-        qkv, grad_context_t, context_t, probs, inverse_total, key_rows, query_rows
-    )
+        queries, keys, values, grad_context_t, probs, inverse_total, key_rows, query_rows
+    )
+    d_query, d_key, d_value, key_off, query_off, s_down, s_up = lax.optimization_barrier(
+        (d_query, d_key, d_value, key_off, query_off, s_down, s_up))
+    s_down, s_up = lax.psum((s_down, s_up), "rep")
     grad_pos_key = lax.dot_general(
         pick, key_off.astype(bf), (((0,), (1,)), ((), ())), preferred_element_type=f32)
     grad_pos_query = lax.dot_general(
@@ -312,31 +426,41 @@
     d_b_query = jnp.sum(d_query.astype(f32), 0) + jnp.sum(grad_pos_query, 0)
     d_b_key = jnp.sum(d_key.astype(f32), 0) + jnp.sum(grad_pos_key, 0)
     d_b_value = jnp.sum(d_value.astype(f32), 0)
-    w_q, w_k, w_v = w_qkv[:, :features], w_qkv[:, features : 2 * features], w_qkv[:, 2 * features :]
     d_rel = nt(low_pos_key, w_k) + nt(low_pos_query, w_q)
     grad_summed = nt(d_query, w_q) + nt(d_key, w_k) + nt(d_value, w_v) + grad_first
     whole = jnp.sum(grad_summed, 0)
     d_type_one = jnp.sum(jnp.where(second_part, grad_summed, 0.0), 0)
     tokens_grad = grad_summed.astype(bf).reshape(tokens.shape)
 
-    share = lambda a: lax.psum_scatter(a.astype(bf), "fsdp", scatter_dimension=0, tiled=True)
-    s_down, s_up, s_out = share(d_w_down), share(d_w_up), share(d_w_out)
-    s_q, s_k, s_v, s_rel = share(d_w_query), share(d_w_key), share(d_w_value), share(d_rel)
-    small = (d_b_query, d_b_key, d_b_value, d_b_out, d_first_gain, d_first_shift, d_b_up, d_b_down,
-             d_second_gain, d_second_shift, whole - d_type_one, d_type_one)
-    devices = lax.axis_size("fsdp")
-    small = jnp.concatenate([a.reshape(devices, -1) for a in small], axis=1)
-    small = lax.psum(small, ("rep", "fsdp"))
-    small = lax.dynamic_index_in_dim(small, lax.axis_index("fsdp"), 0, keepdims=False)
-    (d_b_query, d_b_key, d_b_value, d_b_out, d_first_gain, d_first_shift, d_b_up, d_b_down,
+    small = jnp.stack([d_b_query, d_b_key, d_b_value, d_b_out, d_first_gain, d_first_shift, d_b_down,
+                       d_second_gain, d_second_shift, whole - d_type_one, d_type_one])
+    small = small.astype(bf).reshape(-1, fs, cut).transpose(1, 0, 2)
+    small = jnp.concatenate([small, d_b_up.astype(bf).reshape(fs, up_parts, cut)], axis=1)
+    small = pad_tail(small.reshape(places, 2, vector_count, cut), vector_rows, features)
+    four = jnp.stack([a.astype(bf) for a in (d_w_query, d_w_key, d_w_value, d_w_out)])
+    four = four.reshape(4, places, 2, reps // 4, unit, features).transpose(0, 3, 1, 2, 4, 5)
+    last = jnp.concatenate([
+        four.reshape(reps, places, 2, unit, features),
+        d_rel.astype(bf).reshape(places, 2, reps, table_cut, features).transpose(2, 0, 1, 3, 4),
+        spread(small, reps)], axis=3)
+    last = summed_over(swap_rep(reduce_core(last)))
+    last, s_down, s_up = lax.optimization_barrier((last, s_down, s_up))
+    last = summed_over(swap_line(last))
+    small = last[unit + table_cut :, :cut].astype(f32)
+    both = swap_rep(spread(last[: unit + table_cut], reps)).astype(f32)
+    four = both[:, :unit].reshape(4, cut, features)
+    s_q, s_k, s_v, s_o = four[0], four[1], four[2], four[3]
+    s_rel = both[:, unit:].reshape(-1, features)
+    (d_b_query, d_b_key, d_b_value, d_b_out, d_first_gain, d_first_shift, d_b_down,
      d_second_gain, d_second_shift, d_type_zero, d_type_one) = [
-        small[a:b] for a, b in zip(ends[:-1], ends[1:])]
-    total = lambda a: lax.psum(a, "rep").astype(f32)
+        small[k] for k in range(vector_count - up_parts)]
+    d_b_up = small[vector_count - up_parts : vector_count].reshape(-1)
+    s_down, s_up = s_down.astype(f32), s_up.astype(f32)
     return (
         layer_out, tokens_grad,
-        total(s_q), d_b_query, total(s_k), d_b_key, total(s_v), d_b_value, total(s_out), d_b_out,
-        d_first_gain, d_first_shift, total(s_up), d_b_up, total(s_down), d_b_down,
-        d_second_gain, d_second_shift, total(s_rel), jnp.stack([d_type_zero, d_type_one]),
+        s_q, d_b_query, s_k, d_b_key, s_v, d_b_value, s_o, d_b_out,
+        d_first_gain, d_first_shift, s_up, d_b_up, s_down, d_b_down,
+        d_second_gain, d_second_shift, s_rel, jnp.stack([d_type_zero, d_type_one]),
     )
 
 

time: 683 us -> 501 us (0.73)
  waiting for transfers between devices: 264 us -> 120 us
  blocking collectives: 86.9 us -> 24.8 us
  starting transfers between devices: 0.95 us -> 27.5 us
  local copies, waits for them, and re-layouts: 20.3 us -> 28.9 us
    reduce_scatter x7 -> x2, waiting for transfers between devices: 231 us -> 0.04 us  [per_device(): lax.psum_scatter(a, 'fsdp', scatter_dimension=0, tiled=True)]
    all_to_all x0 -> x2, waiting for transfers between devices: none -> 50.5 us  [swap_rep(): return lax.all_to_all(a, 'rep', 0, 0, tiled=True)]
    ppermute x0 -> x12, waiting for transfers between devices: none -> 44.1 us  [the longest x4 17.6 us: flip_rep(): lax.ppermute(a, 'rep', [(i, i ^ bit) for i in range(lax.axis_size('rep'))])]
    psum x1 -> x0, blocking collectives: 38.2 us -> none  [per_device(): small = lax.psum(small, ('rep', 'fsdp'))]
    unnamed x1 -> x0, blocking collectives: 31.6 us -> none
    all_to_all x0 -> x1, blocking collectives: none -> 24.8 us  [swap_line(): return lax.all_to_all(a, 'fsdp', 0, 0, tiled=True, axis_index_groups=groups)]
    ppermute x0 -> x12, starting transfers between devices: none -> 20 us  [the longest x6 14.6 us: along_line(): lax.ppermute(a, 'fsdp', [(i, i + 2 * step) for i in range(n) if 0 <= i +...]
    all_gather x1 -> x0, blocking collectives: 17.1 us -> none  [per_device(): gather = lambda a: lax.all_gather(a, 'fsdp', axis=0, tiled=True)]
  transfers between devices with their start and end apart: 12 -> 19, of which waited for: 8 -> 12; matrix products, arithmetic and copies ran while one was open for 19% -> 22% of each run, Pallas kernels for 5% -> 22%
where the time goes in v2:
time: 501 us; the launch traced here: 497 us
  matrix products  139 us (28%)
  waiting for transfers between devices  120 us (24%)
  Pallas kernels  110 us (22%)
  other arithmetic  31.3 us (6%)
  local copies, waits for them, and re-layouts  28.9 us (6%)
  starting transfers between devices  27.5 us (5%)
  blocking collectives  24.8 us (5%)
  between operations  15.3 us (3%)
    pallas_call x1, Pallas kernels, attn_bwd(): pl.pallas_call(attn_bwd_kernel, grid=(NP, M), in_specs=[tok(0), tok(0), t...  72.2 us
    dot_general x10, matrix products, nn(): lax.dot_general(a, b, (((1,), (0,)), ((), ())), preferred_element_type=f32)  67.3 us
    all_to_all x2, waiting for transfers between devices, swap_rep(): return lax.all_to_all(a, 'rep', 0, 0, tiled=True)  50.5 us
    pallas_call x1, Pallas kernels, attn_fwd(): pl.pallas_call(attn_fwd_kernel, grid_spec=pltpu.PrefetchScalarGridSpec(nu...  37.6 us
    dot_general x8, matrix products, nt(): lax.dot_general(a, b, (((1,), (1,)), ((), ())), preferred_element_type=f32)  36.1 us
    dot_general x8, matrix products, tn(): lax.dot_general(a, b, (((0,), (0,)), ((), ())), preferred_element_type=f32)  31.4 us
    psum x1, waiting for transfers between devices, per_device(): s_down, s_up = lax.psum((s_down, s_up), 'rep')  24.9 us
    all_to_all x1, blocking collectives, swap_line(): return lax.all_to_all(a, 'fsdp', 0, 0, tiled=True, axis_index_groups=groups)  24.8 us
  transfers between devices with their start and end apart: 19, of which 12 were waited for; matrix products, arithmetic and copies ran while one was open for 22% of the time, Pallas kernels for 22%

profile of v2, /device:TPU:0, one launch (start us, length us, event | category | flops | bytes accessed | tf_op | source)
XLA Modules:
  0.0 497.0 jit_solution(5052728074103003417)
XLA Ops:
  10.9 7.0 %collective-permute-start = (bf16[128,768]{1,0:T(8,128)(2,1)S(1)}, bf16[128,768]{1,0:T(8,128)(2,1)S(1)}, u32[]{:S(2)}, u32[]{:S(2)}) collective-permute-start(bf16[128,768]{1,0:T(8,128)(2,1)S(1)} %dynamic-slice_bitcast_fusion.1), channel_id=1, source_target_pairs={{0,6},{1,7},{8,14},{9,15},{16,22},{17,23},{24,30},{25,31}} | collective-permute-start | bytes 589832 | tf_op jit(solution)/shard_map/ppermute | solution.py:255
  27.5 3.0 collective-permute-done.2
  30.6 11.4 %collective-permute-done.4 = bf16[128,768]{1,0:T(8,128)(2,1)S(1)} collective-permute-done((bf16[128,768]{1,0:T(8,128)(2,1)S(1)}, bf16[128,768]{1,0:T(8,128)(2,1)S(1)}, u32[]{:S(2)}, u32[]{:S(2)}) %collective-permute-start.4) | collective-permute-done | bytes 196640 | tf_op jit(solution)/shard_map/ppermute | solution.py:255
  45.3 4.5 collective-permute-done.6
  53.6 10.5 %collective-permute-done.7 = bf16[2,3,128,384]{3,2,1,0:T(8,128)(2,1)S(1)} collective-permute-done((bf16[2,3,128,384]{3,2,1,0:T(8,128)(2,1)S(1)}, bf16[2,3,128,384]{3,2,1,0:T(8,128)(2,1)S(1)}, u32[]{:S(2)}, u32[]{:S(2)}) %collective-permute-start.7) | collective-permute-done | bytes 589856 | tf_op jit(solution)/shard_map/ppermute | solution.py:263
  69.8 4.4 collective-permute-done.10
  92.3 3.5 fusion.31.pq_ref
  96.1 2.9 fusion.30.pkr_ref
  100.5 37.6 %shard_map.386 = (bf16[768,1024]{1,0:T(8,128)(2,1)S(1)}, bf16[2,12,512,512]{3,2,1,0:T(8,128)(2,1)}, f32[2,6,2,512]{3,2,1,0:T(2,128)S(1)}) custom-call(s32[2]{0:T(128)S(1)} %bitcast.200, bf16[1024,768]{1,0:T(8,128)(2,1)S(1)} %copy-done.10, bf16[1024,768]{1,0:T(8,128)(2,1)S(1)} %add_convert_fusion.2.k_ref, bf16[1024,768]{1,0:T(8,128)(2,1)S(1)} %add_convert_fusion.1.v_ref, ...), custom_call_target="tpu_custom_call" | custom-call | flops 9663676416 | bytes 12582912 | tf_op jit(solution)/shard_map/pallas_call | solution.py:87
  138.2 3.4 fusion.51
  145.0 37.2 %fusion.2 = (bf16[1024,3072]{1,0:T(8,128)(2,1)}, f32[1024,3072]{1,0:T(8,128)}) fusion(f32[3072]{0:T(1024)S(1)} %add.260, bf16[768,3072]{1,0:T(8,128)(2,1)} %all-gather.3.cloned.1.call-done, f32[1024,768]{1,0:T(8,128)} %get-tuple-element.212, f32[768]{0:T(1024)S(1)} %add.257, f32[768]{0:T(1024)S(1)} %mul.138, f32[1024]{0:T(1024)S(1)} %add_rsqrt_fusion.1, ...), kind=kOutput, calls=%fused_computation.4 | convolution fusion | flops 5043388416 | bytes 26765312 | tf_op jit(solution)/shard_map/dot_general | solution.py:21
  182.2 9.7 %fusion.52 = (f32[1024]{0:T(1024)S(1)}, f32[1024,768]{1,0:T(8,128)S(1)}) fusion(f32[768]{0:T(1024)S(1)} %add.264, bf16[1024,3072]{1,0:T(8,128)(2,1)} %get-tuple-element.213, bf16[3072,768]{1,0:T(8,128)(2,1)} %all-gather.5.cloned.1.call-done, f32[768]{0:T(1024)S(1)} %add.257, f32[768]{0:T(1024)S(1)} %mul.138, f32[1024]{0:T(1024)S(1)} %add_rsqrt_fusion.1, ...), kind=kOutput, calls=%fused_computation.180 | convolution fusion | flops 4837342208 | bytes 17323008 | tf_op jit(solution)/shard_map/dot_general | solution.py:21
  196.4 12.8 %fusion.53 = (bf16[3072]{0:T(1024)(128)(2,1)S(1)}, bf16[1024,3072]{1,0:T(8,128)(2,1)S(1)}) fusion(f32[1024,3072]{1,0:T(8,128)} %get-tuple-element.214, f32[3072]{0:T(1024)S(1)} %add.260, bf16[3072,768]{1,0:T(8,128)(2,1)S(1)} %bitcast.250, f32[1024,768]{1,0:T(8,128)S(1)} %get-tuple-element.153), kind=kOutput, calls=%fused_computation.181 | convolution fusion | flops 4870370304 | bytes 26757120 | tf_op jit(solution)/shard_map/dot_general | solution.py:22
  211.9 7.9 %convolution_convert_fusion = bf16[768,3072]{1,0:T(8,128)(2,1)} fusion(bf16[1024,3072]{1,0:T(8,128)(2,1)S(1)} %get-tuple-element.220, f32[1024,768]{1,0:T(8,128)S(1)} %copy-done.18, f32[768]{0:T(1024)S(1)} %add.257, f32[768]{0:T(1024)S(1)} %mul.138, f32[1024]{0:T(1024)S(1)} %add_rsqrt_fusion.1, f32[1024]{0:T(1024)S(1)} %broadcast_multiply_fusion.4), kind=kOutput, calls=%fused_computation.29 | convolution fusion | flops 4838129664 | bytes 14170112 | tf_op jit(solution)/shard_map/dot_general | solution.py:216
  219.8 10.2 %convolution_convert_fusion.1 = bf16[3072,768]{1,0:T(8,128)(2,1)} fusion(bf16[1024,3072]{1,0:T(8,128)(2,1)} %get-tuple-element.213, f32[1024,768]{1,0:T(8,128)} %copy-done.28), kind=kOutput, calls=%fused_computation.30 | convolution fusion | flops 4834983936 | bytes 14155776 | tf_op jit(solution)/shard_map/dot_general | solution.py:216
  230.4 3.8 fusion.32.pk_ref
  234.3 10.2 %multiply_reduce_fusion = (bf16[768]{0:T(1024)(128)(2,1)S(1)}, f32[1024]{0:T(1024)S(1)}, f32[1024]{0:T(1024)S(1)}, bf16[768]{0:T(1024)(128)(2,1)S(1)}, f32[1024,768]{1,0:T(8,128)S(1)}) fusion(f32[1024,768]{1,0:T(8,128)S(1)} %copy-done.19, f32[1024]{0:T(1024)S(1)} %add_rsqrt_fusion.1, f32[1024]{0:T(1024)S(1)} %broadcast_multiply_fusion.4, ...), kind=kOutput, calls=%fused_computation.44 | convolution fusion | flops 4839698432 | bytes 20469760 | tf_op jit(solution)/shard_map/dot_general | solution.py:22
  246.2 3.3 convolution_convert_fusion.5.dcT_ref
  253.3 72.2 %shard_map.387 = (bf16[1024,768]{1,0:T(8,128)(2,1)S(1)}, bf16[1024,768]{1,0:T(8,128)(2,1)S(1)}, bf16[1024,768]{1,0:T(8,128)(2,1)S(1)}, f32[768,1024]{1,0:T(8,128)}, f32[768,1024]{1,0:T(8,128)}) custom-call(bf16[1024,768]{1,0:T(8,128)(2,1)S(1)} %copy-done.11, bf16[1024,768]{1,0:T(8,128)(2,1)S(1)} %copy-done.9, bf16[1024,768]{1,0:T(8,128)(2,1)S(1)} %copy-done.13, ...), custom_call_target="tpu_custom_call" | custom-call | flops 19327352832 | bytes 12582912 | tf_op jit(solution)/shard_map/pallas_call | solution.py:183
  326.8 3.3 fusion.57
  332.7 3.5 select_reduce_fusion
  336.2 2.9 fusion.58
  339.1 2.9 fusion.59
  345.3 3.3 fusion.54
  362.5 5.7 %collective-permute-done.11 = bf16[4,4,128,768]{3,2,1,0:T(8,128)(2,1)} collective-permute-done((bf16[4,4,128,768]{3,2,1,0:T(8,128)(2,1)S(1)}, bf16[4,4,128,768]{3,2,1,0:T(8,128)(2,1)}, u32[]{:S(2)}, u32[]{:S(2)}) %collective-permute-start.11) | collective-permute-done | bytes 3145760 | tf_op jit(solution)/shard_map/ppermute | solution.py:244
  368.2 5.5 %fusion.16 = bf16[4,4,128,768]{3,2,1,0:T(8,128)(2,1)} fusion(bf16[4,4,128,768]{3,2,1,0:T(8,128)(2,1)} %collective-permute-done.11, bf16[4,4,2,128,768]{4,3,2,1,0:T(8,128)(2,1)} %copy-done.14, s32[]{:T(128)S(6)} %select_n.155), kind=kLoop, calls=%fused_computation.28 | loop fusion | flops 6291456 | bytes 9437188 | tf_op jit(solution)/shard_map/convert_element_type | solution.py:313
  373.7 3.7 all-to-all-start
  377.9 45.6 %all-to-all-done = bf16[4,4,128,768]{3,2,1,0:T(8,128)(2,1)S(1)} async-done(((bf16[4,4,128,768]{3,2,1,0:T(8,128)(2,1)}), bf16[4,4,128,768]{3,2,1,0:T(8,128)(2,1)S(1)}, u32[]{:S(2)}, u32[]{:S(2)}) %all-to-all-start) | async-done | bytes 3145760 | tf_op jit(solution)/shard_map/all_to_all | solution.py:259
  425.2 24.9 %all-reduce.7.cloned.1.call-done = (bf16[384,768]{1,0:T(8,128)(2,1)}, bf16[96,3072]{1,0:T(8,128)(2,1)}) async-done(((bf16[384,768]{1,0:T(8,128)(2,1)}, bf16[96,3072]{1,0:T(8,128)(2,1)}), (bf16[384,768]{1,0:T(8,128)(2,1)}, bf16[96,3072]{1,0:T(8,128)(2,1)})) %all-reduce.7.cloned.1.call-update) | async-done | bytes 1179664 | tf_op jit(solution)/shard_map/psum | solution.py:416
  450.1 24.8 %all_to_all.15 = bf16[4,128,768]{2,1,0:T(8,128)(2,1)S(1)} all-to-all(bf16[4,128,768]{2,1,0:T(8,128)(2,1)} %reduce_sum.253), channel_id=1, replica_groups={{0,2,4,6},{1,3,5,7},{8,10,12,14},{9,11,13,15},{16,18,20,22},{17,19,21,2..., dimensions={0} | all-to-all | bytes 1572864 | tf_op jit(solution)/shard_map/all_to_all | solution.py:250
  476.0 3.5 all-to-all-start.2
  483.5 4.9 all-to-all-done.2
  (289 shorter events, 91.6 us)
Async XLA Ops:
  7.2 137.8 %all-gather.3.cloned.1.call-start = ((), (), s32[]{:S(2)}) async-start(), calls=%async_computation.5 | async-start | bytes 5308416 | tf_op jit(solution)/shard_map/all_gather | solution.py:350
  10.9 13.4 %collective-permute-start = (bf16[128,768]{1,0:T(8,128)(2,1)S(1)}, bf16[128,768]{1,0:T(8,128)(2,1)S(1)}, u32[]{:S(2)}, u32[]{:S(2)}) collective-permute-start(bf16[128,768]{1,0:T(8,128)(2,1)S(1)} %dynamic-slice_bitcast_fusion.1), channel_id=1, source_target_pairs={{0,6},{1,7},{8,14},{9,15},{16,22},{17,23},{24,30},{25,31}} | collective-permute-start | bytes 589832 | tf_op jit(solution)/shard_map/ppermute | solution.py:255
  17.9 9.6 %collective-permute-start.1 = (bf16[128,768]{1,0:T(8,128)(2,1)S(1)}, bf16[128,768]{1,0:T(8,128)(2,1)S(1)}, u32[]{:S(2)}, u32[]{:S(2)}) collective-permute-start(bf16[128,768]{1,0:T(8,128)(2,1)S(1)} %dynamic-slice_bitcast_fusion.1), channel_id=1, source_target_pairs={{0,4},{1,5},{2,6},{3,7},{8,12},{9,13},{10,14},{11,15},{16,20},{17,... | collective-permute-start | bytes 589832 | tf_op jit(solution)/shard_map/ppermute | solution.py:255
  19.2 11.3 %collective-permute-start.2 = (bf16[128,768]{1,0:T(8,128)(2,1)S(1)}, bf16[128,768]{1,0:T(8,128)(2,1)S(1)}, u32[]{:S(2)}, u32[]{:S(2)}) collective-permute-start(bf16[128,768]{1,0:T(8,128)(2,1)S(1)} %dynamic-slice_bitcast_fusion.1), channel_id=1, source_target_pairs={{0,2},{1,3},{2,4},{3,5},{4,6},{5,7},{8,10},{9,11},{10,12},{11,13},... | collective-permute-start | bytes 589832 | tf_op jit(solution)/shard_map/ppermute | solution.py:255
  21.7 8.9 %collective-permute-start.3 = (bf16[128,768]{1,0:T(8,128)(2,1)S(1)}, bf16[128,768]{1,0:T(8,128)(2,1)S(1)}, u32[]{:S(2)}, u32[]{:S(2)}) collective-permute-start(bf16[128,768]{1,0:T(8,128)(2,1)S(1)} %dynamic-slice_bitcast_fusion.1), channel_id=1, source_target_pairs={{2,0},{3,1},{4,2},{5,3},{6,4},{7,5},{10,8},{11,9},{12,10},{13,11},... | collective-permute-start | bytes 589832 | tf_op jit(solution)/shard_map/ppermute | solution.py:255
  23.0 19.0 %collective-permute-start.4 = (bf16[128,768]{1,0:T(8,128)(2,1)S(1)}, bf16[128,768]{1,0:T(8,128)(2,1)S(1)}, u32[]{:S(2)}, u32[]{:S(2)}) collective-permute-start(bf16[128,768]{1,0:T(8,128)(2,1)S(1)} %dynamic-slice_bitcast_fusion.1), channel_id=1, source_target_pairs={{4,0},{5,1},{6,2},{7,3},{12,8},{13,9},{14,10},{15,11},{20,16},{21,... | collective-permute-start | bytes 589832 | tf_op jit(solution)/shard_map/ppermute | solution.py:255
  24.3 17.7 %collective-permute-start.5 = (bf16[128,768]{1,0:T(8,128)(2,1)S(1)}, bf16[128,768]{1,0:T(8,128)(2,1)S(1)}, u32[]{:S(2)}, u32[]{:S(2)}) collective-permute-start(bf16[128,768]{1,0:T(8,128)(2,1)S(1)} %dynamic-slice_bitcast_fusion.1), channel_id=1, source_target_pairs={{6,0},{7,1},{14,8},{15,9},{22,16},{23,17},{30,24},{31,25}} | collective-permute-start | bytes 589832 | tf_op jit(solution)/shard_map/ppermute | solution.py:255
  42.2 140.0 %all-gather.5.cloned.1.call-start = ((), (), s32[]{:S(2)}) async-start(), calls=%async_computation.6 | async-start | bytes 5308416 | tf_op jit(solution)/shard_map/all_gather | solution.py:351
  42.3 7.6 %collective-permute-start.6 = (bf16[1,3,128,384]{3,2,1,0:T(8,128)(2,1)S(1)}, bf16[1,3,128,384]{3,2,1,0:T(8,128)(2,1)S(1)}, u32[]{:S(2)}, u32[]{:S(2)}) collective-permute-start(bf16[1,3,128,384]{3,2,1,0:T(8,128)(2,1)S(1)} %get-tuple-element.178), channel_id=1, source_target_pairs={{0,8},{8,0},{16,24},{24,16},{1,9},{9,1},{17,25},{25,17},{2,10},{10... | collective-permute-start | bytes 884744 | tf_op jit(solution)/shard_map/ppermute | solution.py:263
  43.8 7.3 %collective-permute-start.8 = (bf16[1,3,128,384]{3,2,1,0:T(8,128)(2,1)S(1)}, bf16[1,3,128,384]{3,2,1,0:T(8,128)(2,1)S(1)}, u32[]{:S(2)}, u32[]{:S(2)}) collective-permute-start(bf16[1,3,128,384]{3,2,1,0:T(8,128)(2,1)S(1)} %get-tuple-element.179), channel_id=1, source_target_pairs={{0,16},{8,24},{16,0},{24,8},{1,17},{9,25},{17,1},{25,9},{2,18},{10... | collective-permute-start | bytes 884744 | tf_op jit(solution)/shard_map/ppermute | solution.py:263
  51.3 12.7 %collective-permute-start.7 = (bf16[2,3,128,384]{3,2,1,0:T(8,128)(2,1)S(1)}, bf16[2,3,128,384]{3,2,1,0:T(8,128)(2,1)S(1)}, u32[]{:S(2)}, u32[]{:S(2)}) collective-permute-start(bf16[2,3,128,384]{3,2,1,0:T(8,128)(2,1)S(1)} %pad_maximum_fusion.6), channel_id=1, source_target_pairs={{0,16},{8,24},{16,0},{24,8},{1,17},{9,25},{17,1},{25,9},{2,18},{10... | collective-permute-start | bytes 1769480 | tf_op jit(solution)/shard_map/ppermute | solution.py:263
  53.0 12.5 %collective-permute-start.9 = (bf16[2,3,128,384]{3,2,1,0:T(8,128)(2,1)S(1)}, bf16[2,3,128,384]{3,2,1,0:T(8,128)(2,1)S(1)}, u32[]{:S(2)}, u32[]{:S(2)}) collective-permute-start(bf16[2,3,128,384]{3,2,1,0:T(8,128)(2,1)S(1)} %pad_maximum_fusion.7), channel_id=1, source_target_pairs={{0,8},{8,0},{16,24},{24,16},{1,9},{9,1},{17,25},{25,17},{2,10},{10... | collective-permute-start | bytes 1769480 | tf_op jit(solution)/shard_map/ppermute | solution.py:263
  68.2 6.0 %collective-permute-start.10 = (bf16[4,4,128,768]{3,2,1,0:T(8,128)(2,1)}, bf16[4,4,128,768]{3,2,1,0:T(8,128)(2,1)}, u32[]{:S(2)}, u32[]{:S(2)}) collective-permute-start(bf16[4,4,128,768]{3,2,1,0:T(8,128)(2,1)} %select_select_fusion), channel_id=1, source_target_pairs={{0,1},{1,0},{2,3},{3,2},{4,5},{5,4},{6,7},{7,6},{8,9},{9,8},{10,11... | collective-permute-start | bytes 9437192 | tf_op jit(solution)/shard_map/ppermute | solution.py:244
  69.5 257.2 %reduce-scatter.5.cloned.1.call-start = ((), (), s32[]{:S(2)}) async-start(), calls=%async_computation.8 | async-start | bytes 5308416 | tf_op jit(solution)/shard_map/reduce_scatter | solution.py:400
  78.4 9.5 %copy-start.33 = (bf16[1,4,2,96,768]{4,3,2,1,0:T(8,128)(2,1)}, bf16[1,4,2,96,768]{4,3,2,1,0:T(8,128)(2,1)S(1)}, u32[]{:S(2)}) copy-start(bf16[1,4,2,96,768]{4,3,2,1,0:T(8,128)(2,1)S(1)} %get-tuple-element.158) | copy-start | bytes 3538948
  89.4 11.0 %copy-start.8 = (bf16[1024,768]{1,0:T(8,128)(2,1)}, bf16[1024,768]{1,0:T(8,128)(2,1)S(1)}, u32[]{:S(2)}) copy-start(bf16[1024,768]{1,0:T(8,128)(2,1)S(1)} %add_convert_fusion.2.k_ref) | copy-start | bytes 4718596
  100.4 37.7 %copy-start.12 = (bf16[1024,768]{1,0:T(8,128)(2,1)}, bf16[1024,768]{1,0:T(8,128)(2,1)S(1)}, u32[]{:S(2)}) copy-start(bf16[1024,768]{1,0:T(8,128)(2,1)S(1)} %add_convert_fusion.1.v_ref) | copy-start | bytes 4718596
  100.5 37.6 %copy-start.24 = (bf16[2,1,512,768]{3,2,1,0:T(8,128)(2,1)S(1)}, bf16[2,1,512,768]{3,2,1,0:T(8,128)(2,1)}, u32[]{:S(2)}) copy-start(bf16[2,1,512,768]{3,2,1,0:T(8,128)(2,1)} %param.24) | copy-start | bytes 4718596
  100.5 37.6 %copy-start.38 = (bf16[1,4,2,96,768]{4,3,2,1,0:T(8,128)(2,1)S(1)}, bf16[1,4,2,96,768]{4,3,2,1,0:T(8,128)(2,1)}, u32[]{:S(2)}) copy-start(bf16[1,4,2,96,768]{4,3,2,1,0:T(8,128)(2,1)} %get-tuple-element.156) | copy-start | bytes 3538948
  100.5 37.6 %copy-start.42 = (f32[768]{0:T(1024)S(1)}, f32[768]{0:T(1024)}, u32[]{:S(2)}) copy-start(f32[768]{0:T(1024)} %squeeze.67) | copy-start | bytes 9220
  100.5 37.7 %copy-start.45 = (f32[768]{0:T(1024)S(1)}, f32[768]{0:T(1024)}, u32[]{:S(2)}) copy-start(f32[768]{0:T(1024)} %squeeze.68) | copy-start | bytes 9220
  100.5 37.7 %copy-start.55 = (pred[1024]{0:T(1024)(128)(4,1)S(1)}, pred[1024]{0:T(1024)(128)(4,1)}, u32[]{:S(2)}) copy-start(pred[1024]{0:T(1024)(128)(4,1)} %ge.32) | copy-start | bytes 3076
  196.4 12.9 %copy-start.28 = (f32[1024,768]{1,0:T(8,128)}, f32[1024,768]{1,0:T(8,128)S(1)}, u32[]{:S(2)}) copy-start(f32[1024,768]{1,0:T(8,128)S(1)} %get-tuple-element.153) | copy-start | bytes 9437188
  196.4 15.4 %copy-start.18 = (f32[1024,768]{1,0:T(8,128)S(1)}, f32[1024,768]{1,0:T(8,128)}, u32[]{:S(2)}) copy-start(f32[1024,768]{1,0:T(8,128)} %get-tuple-element.212) | copy-start | bytes 9437188
  219.8 107.0 %reduce-scatter.3.cloned.1.call-start = ((), (), s32[]{:S(2)}) async-start(), calls=%async_computation.7 | async-start | bytes 5308416 | tf_op jit(solution)/shard_map/reduce_scatter | solution.py:400
  234.2 10.3 %copy-start.20 = (f32[1024,768]{1,0:T(8,128)S(1)}, f32[1024,768]{1,0:T(8,128)}, u32[]{:S(2)}) copy-start(f32[1024,768]{1,0:T(8,128)} %get-tuple-element.212) | copy-start | bytes 9437188
  362.4 5.8 %collective-permute-start.11 = (bf16[4,4,128,768]{3,2,1,0:T(8,128)(2,1)S(1)}, bf16[4,4,128,768]{3,2,1,0:T(8,128)(2,1)}, u32[]{:S(2)}, u32[]{:S(2)}) collective-permute-start(bf16[4,4,128,768]{3,2,1,0:T(8,128)(2,1)S(1)} %dynamic-slice_bitcast_fusion), channel_id=1, source_target_pairs={{0,1},{1,0},{2,3},{3,2},{4,5},{5,4},{6,7},{7,6},{8,9},{9,8},{10,11... | collective-permute-start | bytes 9437192 | tf_op jit(solution)/shard_map/ppermute | solution.py:244
  373.7 49.9 %all-to-all-start = ((bf16[4,4,128,768]{3,2,1,0:T(8,128)(2,1)}), bf16[4,4,128,768]{3,2,1,0:T(8,128)(2,1)S(1)}, u32[]{:S(2)}, u32[]{:S(2)}) async-start(bf16[4,4,128,768]{3,2,1,0:T(8,128)(2,1)} %fusion.16), calls=%async_computation.2 | async-start | bytes 6291456 | tf_op jit(solution)/shard_map/all_to_all | solution.py:259
  377.4 72.7 %all-reduce.7.cloned.1.call-start = ((), (), s32[]{:S(2)}) async-start(), calls=%async_computation.9 | async-start | bytes 2359296 | tf_op jit(solution)/shard_map/psum | solution.py:416
  450.1 29.4 %copy-start.40 = (bf16[96,3072]{1,0:T(8,128)(2,1)S(1)}, bf16[96,3072]{1,0:T(8,128)(2,1)}, u32[]{:S(2)}) copy-start(bf16[96,3072]{1,0:T(8,128)(2,1)} %get-tuple-element.60) | copy-start | bytes 1769476
  450.1 30.5 %copy-start.39 = (bf16[384,768]{1,0:T(8,128)(2,1)S(1)}, bf16[384,768]{1,0:T(8,128)(2,1)}, u32[]{:S(2)}) copy-start(bf16[384,768]{1,0:T(8,128)(2,1)} %get-tuple-element.61) | copy-start | bytes 1769476
  476.0 12.4 %all-to-all-start.2 = ((bf16[4,112,768]{2,1,0:T(8,128)(2,1)}), bf16[4,112,768]{2,1,0:T(8,128)(2,1)S(1)}, u32[]{:S(2)}, u32[]{:S(2)}) async-start(bf16[4,112,768]{2,1,0:T(8,128)(2,1)} %broadcast_in_dim.106), calls=%async_computation.4 | async-start | bytes 1376256 | tf_op jit(solution)/shard_map/all_to_all | solution.py:259
  (52 other events, 153.0 us)
Sparse Core Ops, SparseCore 0:
  42.3 49.9 all-gather.2
  93.9 50.5 all-gather.4
  219.9 51.2 reduce-scatter.4
  273.4 53.3 reduce-scatter.2
  381.0 69.0 all-reduce.6

commit v3 on v2

v3 whole, which is shorter than its diff:
```python
import math

import jax
import jax.numpy as jnp
import numpy as np
from jax import lax
from jax.experimental import pallas as pl
from jax.experimental.pallas import tpu as pltpu
from jax.sharding import PartitionSpec as P

BUCKETS = 256
MAX_POS = 512
NORM_EPS = 1e-07
VMEM_LIMIT = 62 * 1024 * 1024

HEAD_DIM=64
MASKED=-1e30
f32=jnp.float32; bf=jnp.bfloat16
BLK=128
LOG2E=math.log2(math.e)

def nn(a,b): return lax.dot_general(a,b,(((1,),(0,)),((),())),preferred_element_type=f32)
def nt(a,b): return lax.dot_general(a,b,(((1,),(1,)),((),())),preferred_element_type=f32)

def eye(rows, flip=False):
    r=lax.broadcasted_iota(jnp.int32,(rows,rows),0)
    c=lax.broadcasted_iota(jnp.int32,(rows,rows),1)
    return jnp.where((r+c==rows-1) if flip else (r==c),1.0,0.0).astype(bf)

def attn_fwd_kernel(len_ref,q_ref,k_ref,v_ref,pkrT_ref,pqT_ref,ctxT_ref,p_ref,linv_ref,c_scr,s_scr):
    S=q_ref.shape[0]
    nb=S//BLK
    W=S+BLK
    m=pl.program_id(1)
    length=len_ref[m]
    scale=LOG2E/math.sqrt(3*HEAD_DIM)
    q=q_ref[...]; k=k_ref[...]
    pqT=pqT_ref[...]
    vT=v_ref[...].T; qT=q.T
    row_h=lax.broadcasted_iota(jnp.int32,(2*HEAD_DIM,S),0)
    lane_s=lax.broadcasted_iota(jnp.int32,(S,2*HEAD_DIM),1)
    row_s=lax.broadcasted_iota(jnp.int32,(S,2*HEAD_DIM),0)
    row_t=lax.broadcasted_iota(jnp.int32,(2*HEAD_DIM,2*S),0)
    bias=jnp.where(row_s<length,0.0,MASKED).astype(bf)
    zero=jnp.zeros((),bf)
    pos=lax.broadcasted_iota(jnp.int32,(1,S),1)
    for h in range(2):
        mine=(lane_s<HEAD_DIM) if h==0 else (lane_s>=HEAD_DIM)
        spare=HEAD_DIM if h==0 else 0
        qh=jnp.where(mine,q,zero)
        kb=jnp.where(mine,k,jnp.where(lane_s==spare,bias,zero))
        pqh=jnp.where(row_t==spare,jnp.ones((),bf),pqT)
        qTh=jnp.where((row_h<HEAD_DIM) if h==0 else (row_h>=HEAD_DIM),qT,zero)
        for b in range(nb):
            st=(nb-1-b)*BLK
            c=nn(qh[b*BLK:(b+1)*BLK],pkrT_ref[:,st:st+W]).astype(bf)
            c_scr[h,b*BLK:(b+1)*BLK,:]=pltpu.roll(c,S+1,1,stride=1,stride_axis=0)[:,:S]
        top=None
        for b in range(nb):
            st=(nb-1-b)*BLK
            js=slice(b*BLK,(b+1)*BLK)
            d=nn(kb[js],pqh[:,st:st+W]).astype(bf)
            d=pltpu.roll(d,S+1,1,stride=1,stride_axis=0)[:,:S]
            s=nn(k[js],qTh)+(c_scr[h,:,js].T.astype(f32)+d.astype(f32))
            s_scr[h,js,:]=s
            t=jnp.max(s,axis=0,keepdims=True)
            top=t if top is None else jnp.maximum(top,t)
        top=top*scale
        tot=None
        for b in range(nb):
            js=slice(b*BLK,(b+1)*BLK)
            p=jnp.exp2(s_scr[h,js,:]*scale-top).astype(bf)
            t=jnp.sum(p.astype(f32),axis=0,keepdims=True)
            tot=t if tot is None else tot+t
            p_ref[0,h,js,:]=p
        linv=jnp.where(pos<length,1.0/tot,0.0)
        linv_ref[0,0,h:h+1,:]=linv
        ctx=nn(vT[h*HEAD_DIM:(h+1)*HEAD_DIM,:],p_ref[0,h])*linv
        ctxT_ref[h*HEAD_DIM:(h+1)*HEAD_DIM,:]=ctx.astype(bf)

def attn_fwd(q,k,v,pkr,pq,lengths,heads):
    M=lengths.shape[0]; D=heads*HEAD_DIM
    S=pq.shape[1]//2
    NP=heads//2; L=2*HEAD_DIM
    grid=(NP,M)
    return pl.pallas_call(
        attn_fwd_kernel,
        grid_spec=pltpu.PrefetchScalarGridSpec(
            num_scalar_prefetch=1,grid=grid,
            in_specs=[
                pl.BlockSpec((S,L),lambda p,m,_:(m,p)),
                pl.BlockSpec((S,L),lambda p,m,_:(m,p)),
                pl.BlockSpec((S,L),lambda p,m,_:(m,p)),
                pl.BlockSpec((L,2*S),lambda p,m,_:(p,0)),
                pl.BlockSpec((L,2*S),lambda p,m,_:(p,0)),
            ],
            out_specs=[
                pl.BlockSpec((L,S),lambda p,m,_:(p,m)),
                pl.BlockSpec((1,2,S,S),lambda p,m,_:(m,p,0,0)),
                pl.BlockSpec((1,1,2,S),lambda p,m,_:(m,p,0,0)),
            ],
            scratch_shapes=[pltpu.VMEM((2,S,S),bf),pltpu.VMEM((2,S,S),f32)],
        ),
        out_shape=[jax.ShapeDtypeStruct((D,M*S),bf),jax.ShapeDtypeStruct((M,heads,S,S),bf),jax.ShapeDtypeStruct((M,NP,2,S),f32)],
        compiler_params=pltpu.CompilerParams(vmem_limit_bytes=VMEM_LIMIT),
        cost_estimate=pl.CostEstimate(flops=int(2*M*heads*S*S*64*12),bytes_accessed=int(M*heads*S*S*2),transcendentals=M*heads*S*S),
    )(lengths,q,k,v,pkr,pq)

def attn_bwd_kernel(q_ref,k_ref,v_ref,dcT_ref,p_ref,linv_ref,pk_ref,pq_ref,dq_ref,dk_ref,dv_ref,ko_out,qo_out,ds_scr,p_scr,t_scr,ko_ref,qo_ref):
    S=q_ref.shape[0]
    nb=S//BLK
    W=S+BLK
    m=pl.program_id(1)
    scale=1.0/math.sqrt(3*HEAD_DIM)
    zero=jnp.zeros((),bf)
    flip=eye(BLK,True)
    q=q_ref[...]
    def reverse(x):
        return jnp.concatenate([nn(flip,x[(nb-1-b)*BLK:(nb-b)*BLK]).astype(bf) for b in range(nb)],axis=0)
    kr=reverse(k_ref[...]); vr=reverse(v_ref[...])
    qT=q.T; krT=kr.T
    lane_s=lax.broadcasted_iota(jnp.int32,(S,2*HEAD_DIM),1)
    lane_t=lax.broadcasted_iota(jnp.int32,(2*S,2*HEAD_DIM),1)
    pad=jnp.zeros((BLK,BLK),bf)
    @pl.when(m==0)
    def _():
        ko_ref[...]=jnp.zeros_like(ko_ref)
        qo_ref[...]=jnp.zeros_like(qo_ref)
    dq=[None]*nb; dk=[None]*nb; dv=None
    zrow=jnp.zeros((HEAD_DIM,S),bf)
    for h in range(2):
        hs=slice(h*HEAD_DIM,(h+1)*HEAD_DIM)
        mine=(lane_s<HEAD_DIM) if h==0 else (lane_s>=HEAD_DIM)
        mine_t=(lane_t<HEAD_DIM) if h==0 else (lane_t>=HEAD_DIM)
        qh=jnp.where(mine,q,zero); krh=jnp.where(mine,kr,zero)
        pkh=jnp.where(mine_t,pk_ref[...],zero); pqh=jnp.where(mine_t,pq_ref[...],zero)
        linv=linv_ref[0,0,h:h+1,:]
        dc=dcT_ref[hs,:].astype(f32)*linv
        dcl=dc.astype(bf); dcs=(dc*scale).astype(bf)
        def wide(x): return jnp.concatenate([x,zrow] if h==0 else [zrow,x],axis=0)
        t=nt(p_ref[0,h],wide(dcl))
        dv=t if dv is None else dv+t
        dcw=wide(dcs)
        delta=None
        for b in range(nb):
            js=slice(b*BLK,(b+1)*BLK)
            p=nn(flip,p_ref[0,h,(nb-1-b)*BLK:(nb-b)*BLK,:])
            t=p*nn(vr[js],dcw)
            p_scr[h,js,:]=p
            t_scr[h,js,:]=t
            t=jnp.sum(t,axis=0,keepdims=True)
            delta=t if delta is None else delta+t
        delta=delta*linv
        for b in range(nb):
            js=slice(b*BLK,(b+1)*BLK)
            ds=(t_scr[h,js,:]-p_scr[h,js,:]*delta).astype(bf)
            ds_scr[h,js,:]=ds
            far=pltpu.roll(jnp.concatenate([ds,pad],axis=1),0,1,stride=1,stride_axis=0)
            st=b*BLK
            t=nn(ds,qh)+nn(far,pqh[st:st+W])
            dk[b]=t if dk[b] is None else dk[b]+t
            qo_ref[hs,st:st+W]+=nn(krT[hs,js],far)
        for b in range(nb):
            js=slice(b*BLK,(b+1)*BLK)
            ds=ds_scr[h,:,js].T
            near=pltpu.roll(jnp.concatenate([ds,pad],axis=1),0,1,stride=1,stride_axis=0)
            st=b*BLK
            t=nn(ds,krh)+nn(near,pkh[st:st+W])
            dq[b]=t if dq[b] is None else dq[b]+t
            ko_ref[hs,st:st+W]+=nn(qT[hs,js],near)
    @pl.when(m==pl.num_programs(1)-1)
    def _():
        ko_out[...]=ko_ref[...].astype(bf)
        qo_out[...]=qo_ref[...].astype(bf)
    dv_ref[...]=dv.astype(bf)
    for b in range(nb):
        dq_ref[b*BLK:(b+1)*BLK,:]=dq[b].astype(bf)
        dk_ref[(nb-1-b)*BLK:(nb-b)*BLK,:]=nn(flip,dk[b].astype(bf)).astype(bf)

def attn_bwd(q,k,v,dcT,p,linv,pk,pq):
    M,heads,S,_=p.shape; D=heads*HEAD_DIM
    NP=heads//2; L=2*HEAD_DIM
    tok=lambda off: pl.BlockSpec((S,L),lambda p,m:(m,off+p))
    colT=pl.BlockSpec((L,S),lambda p,m:(p,m))
    tab=pl.BlockSpec((2*S,L),lambda p,m:(0,p))
    return pl.pallas_call(
        attn_bwd_kernel,
        grid=(NP,M),
        in_specs=[tok(0),tok(0),tok(0),colT,
            pl.BlockSpec((1,2,S,S),lambda p,m:(m,p,0,0)),
            pl.BlockSpec((1,1,2,S),lambda p,m:(m,p,0,0)),
            tab,tab],
        out_specs=[tok(0),tok(0),tok(0),pl.BlockSpec((L,2*S),lambda p,m:(p,0)),pl.BlockSpec((L,2*S),lambda p,m:(p,0))],
        out_shape=[jax.ShapeDtypeStruct((M*S,D),bf)]*3+[jax.ShapeDtypeStruct((D,2*S),bf)]*2,
        scratch_shapes=[pltpu.VMEM((2,S,S),bf),pltpu.VMEM((2,S,S),f32),pltpu.VMEM((2,S,S),f32),pltpu.VMEM((L,2*S),f32),pltpu.VMEM((L,2*S),f32)],
        compiler_params=pltpu.CompilerParams(vmem_limit_bytes=VMEM_LIMIT),
        cost_estimate=pl.CostEstimate(flops=int(2*M*heads*S*S*64*24),bytes_accessed=int(M*heads*S*S*2),transcendentals=0),
    )(q,k,v,dcT,p,linv,pk,pq)


def bucket_index(offset_of):
    middle = BUCKETS // 2
    sign_of = np.sign(offset_of)
    magnitude = np.where(
        (offset_of < middle) & (offset_of > -middle), middle - 1, np.abs(offset_of)
    )
    log_pos = (
        np.ceil(np.log(magnitude / middle) / np.log((MAX_POS - 1) / middle) * (middle - 1)) + middle
    )
    bucket = np.where(magnitude <= middle, offset_of, log_pos * sign_of)
    return np.clip(bucket + BUCKETS, 0, 2 * BUCKETS - 1)


def pick_rows(offsets):
    return (bucket_index(offsets)[:, None] == np.arange(2 * BUCKETS)[None, :]).astype(np.float32)


def tn(a, b):
    return lax.dot_general(a, b, (((0,), (0,)), ((), ())), preferred_element_type=f32)

COLUMNS = 256


def second_rows(bound_ref, rows, seq_len):
    at = lax.broadcasted_iota(jnp.int32, (rows, 1), 0)
    second = at < 0
    for m in range(rows // seq_len):
        second = second | ((at >= m * seq_len + bound_ref[m]) & (at < (m + 1) * seq_len))
    return second


def project_kernel(
    bound_ref, tokens_ref, w_q_ref, w_k_ref, w_v_ref, rel_ref, pick_ref, pick_t_ref, pick_back_t_ref, vec_ref,
    type_ref, q_ref, k_ref, v_ref, key_ref, query_ref, key_back_ref, query_t_ref, low_ref, *, seq_len,
):
    rows = tokens_ref.shape[0]

    @pl.when(pl.program_id(0) == 0)
    def _():
        second = second_rows(bound_ref, rows, seq_len)
        low_ref[...] = (
            tokens_ref[...].astype(f32) + jnp.where(second, type_ref[1:2, :], type_ref[0:1, :])
        ).astype(bf)

    low = low_ref[...]
    rel = rel_ref[...].reshape(-1, tokens_ref.shape[1])
    features = tokens_ref.shape[1]
    w_q, w_k, w_v = [r[...].reshape(features, -1) for r in (w_q_ref, w_k_ref, w_v_ref)]
    b_q, b_k = vec_ref[0:1, :], vec_ref[1:2, :]
    q_ref[...] = (nn(low, w_q) + b_q).astype(bf)
    k_ref[...] = (nn(low, w_k) + b_k).astype(bf)
    v_ref[...] = (nn(low, w_v) + vec_ref[2:3, :]).astype(bf)
    pos_query = (nn(rel, w_q) + b_q).astype(bf)
    pos_key = (nn(rel, w_k) + b_k).astype(bf)
    query_ref[...] = nn(pick_ref[...], pos_query).astype(bf)
    key_ref[...] = nn(pick_ref[...], pos_key).astype(bf)
    key_back_ref[...] = tn(pos_key, pick_back_t_ref[...]).astype(bf)
    query_t_ref[...] = tn(pos_query, pick_t_ref[...]).astype(bf)


def weight_view(view, g, columns):
    lead, rows = view[1], view[2]
    return pl.BlockSpec(lead + (1, rows, columns), lambda i, *_: (0, 0, g, 0, i if columns == COLUMNS else 0),
                        pipeline_mode=None if columns == COLUMNS else pl.Buffered(1))


def table_view(view):
    return pl.BlockSpec(view[4], lambda i, *_: view[5], pipeline_mode=pl.Buffered(1))


def project(boundary, tokens, view, pick, pick_t, pick_back_t, vec, types, seq_len):
    total, features = tokens.shape
    four, table = view[0], view[3]
    table_rows = pick.shape[1]
    whole = lambda a: pl.BlockSpec(a.shape, lambda i, _: (0,) * a.ndim, pipeline_mode=pl.Buffered(1))
    weight = lambda g: weight_view(view, g, COLUMNS)
    columns = lambda rows: pl.BlockSpec((rows, COLUMNS), lambda i, _: (0, i))
    shape = jax.ShapeDtypeStruct
    offsets = pick.shape[0]
    return pl.pallas_call(
        lambda *refs: project_kernel(*refs, seq_len=seq_len),
        grid_spec=pltpu.PrefetchScalarGridSpec(
            num_scalar_prefetch=1,
            grid=(features // COLUMNS,),
            in_specs=[whole(tokens), weight(0), weight(1), weight(2), table_view(view), whole(pick),
                      whole(pick_t), whole(pick_back_t), columns(vec.shape[0]), whole(types)],
            out_specs=[columns(total)] * 3 + [columns(offsets)] * 2
            + [pl.BlockSpec((COLUMNS, offsets), lambda i, _: (i, 0))] * 2
            + [pl.BlockSpec((total, features), lambda i, _: (0, 0))],
        ),
        out_shape=[shape((total, features), bf)] * 3 + [shape((offsets, features), bf)] * 2
        + [shape((features, offsets), bf)] * 2
        + [shape((total, features), bf)],
        compiler_params=pltpu.CompilerParams(vmem_limit_bytes=VMEM_LIMIT),
        cost_estimate=pl.CostEstimate(
            flops=2 * features * features * (3 * total + 2 * table_rows) + 6 * offsets * features * table_rows,
            bytes_accessed=2 * features * (3 * features + 5 * total + 3 * offsets), transcendentals=0),
    )(boundary, tokens, four, four, four, table, pick, pick_t, pick_back_t, vec, types)


def unproject_kernel(
    bound_ref, core_ref, low_ref, dq_ref, dk_ref, dv_ref, key_off_ref, query_off_ref, w_q_ref, w_k_ref, w_v_ref,
    rel_ref, pick_t_ref, grad_first_ref, context_ref, grad_att_ref, sums_ref, sum_up_ref,
    *refs, seq_len, direct,
):
    if direct:
        keep_ref, give_ref, grad_ref, sum_ref, rel_sum_ref, small_ref = refs
    else:
        dw_ref, drel_ref, small_ref, grad_ref, sum_ref, rel_sum_ref = refs
    step = pl.program_id(0)
    rows, features = low_ref.shape
    first = core_ref[0] == 0

    @pl.when(step == 0)
    def _():
        sum_ref[...] = grad_first_ref[...]
        rel_sum_ref[...] = jnp.zeros_like(rel_sum_ref)
        small_ref[...] = jnp.zeros_like(small_ref)

    low, rel = low_ref[...], rel_ref[...].reshape(-1, features)
    w_q, w_k, w_v = [r[...].reshape(features, -1) for r in (w_q_ref, w_k_ref, w_v_ref)]
    dq, dk, dv = dq_ref[...], dk_ref[...], dv_ref[...]
    columns = pl.ds(pl.multiple_of(step * COLUMNS, COLUMNS), COLUMNS)

    def put(at, rows_at, values):
        if direct:
            _, places, part, _ = keep_ref.shape
            values = values.astype(bf).reshape(places, 2, -1, values.shape[-1])
            keep_ref[at, :, rows_at, columns] = jnp.where(first, values[:, 0], values[:, 1])
            give_ref[at, :, rows_at, columns] = jnp.where(first, values[:, 1], values[:, 0])
        else:
            dw_ref[at] = values.astype(bf)

    unit = direct
    pos_query = nt(pick_t_ref[...], query_off_ref[...])
    pos_key = nt(pick_t_ref[...], key_off_ref[...])
    low_query, low_key = pos_query.astype(bf), pos_key.astype(bf)
    put(0, slice(0, unit), tn(low, dq) + tn(rel, low_query))
    put(1, slice(0, unit), tn(low, dk) + tn(rel, low_key))
    put(2, slice(0, unit), tn(low, dv))
    put(3, slice(0, unit), nn(context_ref[...], grad_att_ref[...]))
    total = lambda a: jnp.sum(a.astype(f32), 0, keepdims=True)
    small_ref[0:1, columns] = total(dq) + total(pos_query)
    small_ref[1:2, columns] = total(dk) + total(pos_key)
    small_ref[2:3, columns] = total(dv)
    sum_ref[...] += nt(dq, w_q) + nt(dk, w_k) + nt(dv, w_v)
    rel_sum_ref[...] += nt(low_key, w_k) + nt(low_query, w_q)

    @pl.when(step == pl.num_programs(0) - 1)
    def _():
        values = sum_ref[...]
        grad_ref[...] = values.astype(bf)
        second = second_rows(bound_ref, rows, seq_len)
        for at, k in ((3, 5), (4, 3), (5, 4), (6, 2), (7, 0), (8, 1)):
            small_ref[at : at + 1, :] = sums_ref[k : k + 1, :]
        small_ref[9:10, :] = total(jnp.where(second, 0.0, values))
        small_ref[10:11, :] = total(jnp.where(second, values, 0.0))
        for k in range(sum_up_ref.shape[1] // features):
            small_ref[11 + k : 12 + k, :] = sum_up_ref[:, k * features : (k + 1) * features]
        if direct:
            reps, places, part, _ = keep_ref.shape
            table = rel_sum_ref[...].astype(bf).reshape(places, 2, reps, -1, features)
            small = small_ref[...].astype(bf)
            end = unit + table.shape[3]
            for r in range(reps):
                keep_ref[r, :, unit:end, :] = jnp.where(first, table[:, 0, r], table[:, 1, r])
                give_ref[r, :, unit:end, :] = jnp.where(first, table[:, 1, r], table[:, 0, r])
                for z in range(places):
                    keep_ref[r, z, end:part, :] = small
                    give_ref[r, z, end:part, :] = small
        else:
            drel_ref[...] = rel_sum_ref[...].astype(bf)


def unproject(boundary, core, low, dq, dk, dv, key_off, query_off, view, pick_t, grad_first, context_t, grad_att,
              sums, sum_up, seq_len, direct, parts):
    total, features = low.shape
    four, table = view[0], view[3]
    table_rows = pick_t.shape[0]
    whole = lambda a: pl.BlockSpec(a.shape, lambda i, *_: (0,) * a.ndim, pipeline_mode=pl.Buffered(1))
    weight = lambda g: weight_view(view, g, COLUMNS)
    columns = lambda rows: pl.BlockSpec((rows, COLUMNS), lambda i, *_: (0, i))
    turned = pl.BlockSpec((COLUMNS, key_off.shape[1]), lambda i, *_: (i, 0))
    fixed = lambda s: pl.BlockSpec(s, lambda i, *_: (0,) * len(s))
    shape = jax.ShapeDtypeStruct
    small = (16, features)
    scratch = [pltpu.VMEM((total, features), f32), pltpu.VMEM((table_rows, features), f32)]
    if direct:
        out_specs = [fixed(parts), fixed(parts), fixed((total, features))]
        out_shape = [shape(parts, bf), shape(parts, bf), shape((total, features), bf)]
        scratch.append(pltpu.VMEM(small, f32))
    else:
        out_specs = [pl.BlockSpec((4, features, COLUMNS), lambda i, *_: (0, 0, i)), fixed((table_rows, features)),
                     fixed(small), fixed((total, features))]
        out_shape = [shape((4, features, features), bf), shape((table_rows, features), bf), shape(small, f32),
                     shape((total, features), bf)]
    return pl.pallas_call(
        lambda *refs: unproject_kernel(*refs, seq_len=seq_len, direct=direct),
        grid_spec=pltpu.PrefetchScalarGridSpec(
            num_scalar_prefetch=2,
            grid=(features // COLUMNS,),
            in_specs=[whole(low), columns(total), columns(total), columns(total), turned, turned,
                      weight(0), weight(1), weight(2), table_view(view), whole(pick_t), whole(grad_first),
                      whole(context_t), columns(total), whole(sums), whole(sum_up)],
            out_specs=out_specs,
            scratch_shapes=scratch,
        ),
        out_shape=out_shape,
        compiler_params=pltpu.CompilerParams(vmem_limit_bytes=VMEM_LIMIT),
        cost_estimate=pl.CostEstimate(
            flops=2 * features * features * (7 * total + 4 * table_rows) + 8 * total * features * table_rows,
            bytes_accessed=2 * features * (7 * features + 10 * total), transcendentals=0),
    )(boundary, core, low, dq, dk, dv, key_off, query_off, four, four, four, table, pick_t, grad_first, context_t,
      grad_att, sums, sum_up)


ROWS = 256
CHUNK = 512


def normalize(values):
    centred = values - jnp.mean(values, -1, keepdims=True)
    inverse = lax.rsqrt(jnp.mean(centred * centred, -1, keepdims=True) + NORM_EPS)
    return centred * inverse, inverse


def normalize_back(grad, normed, inverse):
    return inverse * (
        grad
        - jnp.mean(grad, -1, keepdims=True)
        - normed * jnp.mean(grad * normed, -1, keepdims=True)
    )


def ffn_kernel(
    bound_ref, context_ref, tokens_ref, grad_ref, w_o_ref, w_u_ref, w_d_ref, vec_ref, v_up_ref,
    out_ref, hidden_ref, active_ref, grad_ffn_ref, grad_raised_ref, grad_first_ref, grad_att_ref,
    grad_ctx_ref, sums_ref, sum_up_ref, slope_ref, *, seq_len,
):
    step = pl.program_id(0)
    rows = tokens_ref.shape[0]
    wide = w_u_ref.shape[1]
    vec = lambda k: vec_ref[k : k + 1, :]
    v_out, g_first, s_first, v_down, g_second, s_second = [vec(k) for k in range(3, 9)]
    seq = step * rows // seq_len
    pos = step * rows - seq * seq_len + lax.broadcasted_iota(jnp.int32, (rows, 1), 0)
    second = pos >= bound_ref[seq]
    summed = tokens_ref[...].astype(f32) + jnp.where(second, vec(10), vec(9))
    first_normed, first_inverse = normalize(summed + tn(context_ref[...], w_o_ref[...].reshape(tokens_ref.shape[1], -1)) + v_out)
    hidden = first_normed * g_first + s_first
    hidden_low = hidden.astype(bf)
    hidden_ref[...] = hidden_low
    for c in range(0, wide, CHUNK):
        at = slice(c, c + CHUNK)
        raised = nn(hidden_low, w_u_ref[:, at]) + v_up_ref[:, at]
        cumulative = 0.5 + 0.5 * lax.erf(raised * (1.0 / math.sqrt(2.0)))
        active_ref[:, at] = (raised * cumulative).astype(bf)
        density = jnp.exp(-0.5 * raised * raised) * (1.0 / math.sqrt(2.0 * math.pi))
        slope_ref[:, at] = cumulative + raised * density
    second_normed, second_inverse = normalize(hidden + nn(active_ref[...], w_d_ref[...]) + v_down)
    out_ref[...] = (second_normed * g_second + s_second).astype(bf)
    grad = grad_ref[...].astype(f32)
    grad_mixed = normalize_back(grad * g_second, second_normed, second_inverse)
    grad_ffn = grad_mixed.astype(bf)
    grad_ffn_ref[...] = grad_ffn

    @pl.when(step == 0)
    def _():
        sums_ref[...] = jnp.zeros_like(sums_ref)
        sum_up_ref[...] = jnp.zeros_like(sum_up_ref)

    def add_sum(k, values):
        sums_ref[k : k + 1, :] += jnp.sum(values, 0, keepdims=True)

    add_sum(0, grad * second_normed)
    add_sum(1, grad)
    add_sum(2, grad_ffn.astype(f32))
    for c in range(0, wide, CHUNK):
        at = slice(c, c + CHUNK)
        grad_raised = (nt(grad_ffn, w_d_ref[at, :]) * slope_ref[:, at]).astype(bf)
        grad_raised_ref[:, at] = grad_raised
        sum_up_ref[:, at] += jnp.sum(grad_raised.astype(f32), 0, keepdims=True)
    grad_hidden = nt(grad_raised_ref[...], w_u_ref[...]) + grad_mixed
    add_sum(3, grad_hidden * first_normed)
    add_sum(4, grad_hidden)
    grad_first = normalize_back(grad_hidden * g_first, first_normed, first_inverse)
    grad_first_ref[...] = grad_first
    grad_att = grad_first.astype(bf)
    grad_att_ref[...] = grad_att
    add_sum(5, grad_att.astype(f32))
    grad_ctx_ref[...] = nt(w_o_ref[...].reshape(tokens_ref.shape[1], -1), grad_att).astype(bf)


def ffn(boundary, context_t, tokens, out_grad, view, w_u, w_d, vec, v_up, seq_len):
    total, features = tokens.shape
    wide = w_u.shape[1]
    whole = lambda a: pl.BlockSpec(a.shape, lambda i, _: (0, 0), pipeline_mode=pl.Buffered(1))
    narrow = pl.BlockSpec((ROWS, features), lambda i, _: (i, 0))
    broad = pl.BlockSpec((ROWS, wide), lambda i, _: (i, 0))
    turned = pl.BlockSpec((features, ROWS), lambda i, _: (0, i))
    shape = jax.ShapeDtypeStruct
    return pl.pallas_call(
        lambda *refs: ffn_kernel(*refs, seq_len=seq_len),
        grid_spec=pltpu.PrefetchScalarGridSpec(
            num_scalar_prefetch=1,
            grid=(total // ROWS,),
            in_specs=[turned, narrow, narrow, weight_view(view, 3, features), whole(w_u), whole(w_d), whole(vec), whole(v_up)],
            out_specs=[
                narrow, narrow, broad, narrow, broad, narrow, narrow, turned,
                pl.BlockSpec((8, features), lambda i, _: (0, 0)),
                pl.BlockSpec((1, wide), lambda i, _: (0, 0)),
            ],
            scratch_shapes=[pltpu.VMEM((ROWS, wide), f32)],
        ),
        out_shape=[
            shape((total, features), bf), shape((total, features), bf), shape((total, wide), bf),
            shape((total, features), bf), shape((total, wide), bf), shape((total, features), f32),
            shape((total, features), bf), shape((features, total), bf),
            shape((8, features), f32), shape((1, wide), f32),
        ],
        compiler_params=pltpu.CompilerParams(vmem_limit_bytes=VMEM_LIMIT),
        cost_estimate=pl.CostEstimate(
            flops=2 * total * features * (4 * wide + 2 * features),
            bytes_accessed=2 * (2 * features * wide + 2 * total * wide + 8 * total * features),
            transcendentals=2 * total * wide),
    )(boundary, context_t, tokens, out_grad, view[0], w_u, w_d, vec, v_up)


def outer_kernel(left_ref, right_ref, out_ref):
    out_ref[0] = tn(left_ref[...], right_ref[...]).astype(bf)


def outer(left, right, cut_left):
    total, features = left.shape if not cut_left else right.shape
    blocks = (left if cut_left else right).shape[1] // features
    moving = pl.BlockSpec((total, features), lambda i: (0, i))
    fixed = pl.BlockSpec((total, features), lambda i: (0, 0), pipeline_mode=pl.Buffered(1))
    return pl.pallas_call(
        outer_kernel,
        grid=(blocks,),
        in_specs=[moving, fixed] if cut_left else [fixed, moving],
        out_specs=pl.BlockSpec((1, features, features), lambda i: (i, 0, 0)),
        out_shape=jax.ShapeDtypeStruct((blocks, features, features), bf),
        compiler_params=pltpu.CompilerParams(vmem_limit_bytes=VMEM_LIMIT),
        cost_estimate=pl.CostEstimate(
            flops=2 * total * features * features * blocks,
            bytes_accessed=2 * blocks * features * (features + total), transcendentals=0),
    )(left, right)


TILE = 16


def swap_core(a):
    n = lax.axis_size("fsdp")
    return lax.ppermute(a, "fsdp", [(i, i ^ 1) for i in range(n)])


def swap_line(a):
    n = lax.axis_size("fsdp")
    groups = [list(range(c, n, 2)) for c in range(2)]
    return lax.all_to_all(a, "fsdp", 0, 0, tiled=True, axis_index_groups=groups)


def along_line(a, step):
    n = lax.axis_size("fsdp")
    return lax.ppermute(a, "fsdp", [(i, i + 2 * step) for i in range(n) if 0 <= i + 2 * step < n])


def swap_rep(a):
    return lax.all_to_all(a, "rep", 0, 0, tiled=True)


def flip_rep(a, bit):
    return lax.ppermute(a, "rep", [(i, i ^ bit) for i in range(lax.axis_size("rep"))])


def after(a, *others):
    return lax.optimization_barrier((a,) + others)[0]


def spread(a, copies):
    return jnp.broadcast_to(a[None], (copies,) + a.shape)


def gather_rep(a):
    reps = lax.axis_size("rep")
    bits = [1 << k for k in range(reps.bit_length() - 1)]
    width = a.shape[-1] // len(bits)
    me = lax.axis_index("rep")
    shares = []
    for k in range(len(bits)):
        share = a[None, ..., k * width : (k + 1) * width]
        order = bits[k:] + bits[:k]
        for bit in order:
            other = flip_rep(share, bit)
            high = (me // bit) % 2 == 1
            share = jnp.concatenate([jnp.where(high, other, share), jnp.where(high, share, other)])
        at = np.zeros(reps, np.int32)
        for place in range(reps):
            rep = sum(bit for i, bit in enumerate(order) if (place >> i) & 1)
            at[rep] = place
        shares.append(jnp.stack([share[int(p)] for p in at]))
    return jnp.concatenate(shares, axis=-1)


def gather_parts(mine, shard, *others):
    places = lax.axis_size("fsdp") // 2
    place = lax.axis_index("fsdp") // 2
    steps = [k for d in range(1, places) for k in (d, -d)]
    seen = {-k: along_line(mine, k) for k in steps}
    line = jnp.stack([seen[k] for k in range(1 - places, places) if k])
    line = lax.dynamic_slice_in_dim(line, places - 1 - place, places - 1, 0)
    line, *others = lax.optimization_barrier((line, *others))
    every = gather_rep(line)
    at = jnp.arange(places)[:, None, None, None]
    every = every.swapaxes(0, 1)
    before = jnp.pad(every, ((0, 1), (0, 0), (0, 0), (0, 0)))
    behind = jnp.pad(every, ((1, 0), (0, 0), (0, 0), (0, 0)))
    every = jnp.where(at == place, shard[None], jnp.where(at < place, before, behind))
    other = swap_core(every)
    first = lax.axis_index("fsdp") % 2 == 0
    return jnp.stack([jnp.where(first, every, other), jnp.where(first, other, every)], axis=1), others


def summed_over(a):
    return jnp.sum(a.astype(f32), 0).astype(bf)


def pad_tail(a, rows, columns):
    return jnp.pad(a, [(0, 0)] * (a.ndim - 2) + [(0, rows - a.shape[-2]), (0, columns - a.shape[-1])])


def per_device(
    tokens, lengths, boundary,
    w_query, b_query, w_key, b_key, w_value, b_value, w_out, b_out,
    first_gain, first_shift, w_up, b_up, w_down, b_down,
    second_gain, second_shift, rel_table, type_table, out_grad,
):
    micros, seqs, seq_len, features = tokens.shape
    rows = micros * seqs * seq_len
    heads = features // HEAD_DIM
    fs, reps = lax.axis_size("fsdp"), lax.axis_size("rep")
    places = fs // 2
    cut = w_query.shape[0]
    unit = 4 * cut // reps
    table_cut = rel_table.shape[0] // reps
    up_parts = w_up.shape[1] // features
    vectors = jnp.stack([b_query, b_key, b_value, b_out, first_gain, first_shift, b_down, second_gain,
                         second_shift, type_table[0], type_table[1]] + [b_up[k * cut : (k + 1) * cut] for k in range(up_parts)])
    vector_count = vectors.shape[0]
    vector_rows = -(-vector_count // TILE) * TILE
    vectors = pad_tail(vectors, vector_rows, features)
    shard = jnp.concatenate([
        jnp.stack([w_query, w_key, w_value, w_out]).reshape(reps, unit, features),
        rel_table.reshape(reps, table_cut, features),
        spread(vectors, reps)], axis=1)
    mine = lax.dynamic_index_in_dim(shard, lax.axis_index("rep"), 0, keepdims=False)
    first, (w_up, w_down) = gather_parts(mine, shard, w_up, w_down)
    w_u = lax.all_gather(w_up, "fsdp", axis=0, tiled=True)
    w_d = lax.all_gather(w_down, "fsdp", axis=0, tiled=True)
    direct = unit if unit == cut and cut % TILE == 0 and table_cut % TILE == 0 else 0
    part = unit + table_cut + vector_rows
    if direct:
        view = (first, (places, 2), cut, first, (places, 2, reps, table_cut, features), (0, 0, 0, unit // table_cut, 0))
    else:
        four = first[:, :, :, :unit].reshape(fs, 4, reps // 4, unit, features).transpose(1, 0, 2, 3, 4)
        rel = first[:, :, :, unit : unit + table_cut].reshape(1, 1, 1, -1, features)
        view = (four.reshape(1, 1, 4, features, features), (1, 1), features, rel, rel.shape, (0,) * 5)
    wide = first[:, :, 0, unit + table_cut : unit + table_cut + vector_count, :cut].reshape(fs, vector_count, cut)
    wide = wide.transpose(1, 0, 2).astype(f32)
    v_up = wide[vector_count - up_parts :].transpose(1, 0, 2).reshape(1, -1)
    wide = wide.reshape(vector_count, features)

    offsets = np.clip(np.arange(2 * seq_len) - (seq_len - 1), 1 - seq_len, seq_len - 1)
    pick = pick_rows(offsets)
    pick_back = pick_rows(-offsets)
    flat_bound, flat_lengths = boundary.reshape(-1), lengths.reshape(-1)
    flat_tokens, flat_grad = tokens.reshape(rows, features), out_grad.reshape(rows, features)
    queries, keys, values, key_rows, query_rows, key_back_t, query_t, summed_low = project(
        flat_bound, flat_tokens, view, jnp.asarray(pick, bf), jnp.asarray(pick.T, bf), jnp.asarray(pick_back.T, bf),
        wide, wide[9:11], seq_len)
    context_t, probs, inverse_total = attn_fwd(
        queries, keys, values, key_back_t, query_t, flat_lengths, heads)
    (layer_out, hidden_low, active, grad_ffn, grad_raised, grad_first, grad_attended, grad_context_t,
     sums, sum_up) = ffn(flat_bound, context_t, flat_tokens, flat_grad, view, w_u, w_d, wide, v_up, seq_len)
    d_down = outer(active, grad_ffn, True).reshape(-1, features)
    s_down = lax.psum_scatter(d_down, "fsdp", scatter_dimension=0, tiled=True)
    s_up = lax.psum_scatter(outer(hidden_low, grad_raised, False), "fsdp", scatter_dimension=1, tiled=True)
    d_query, d_key, d_value, key_off, query_off = attn_bwd(
        queries, keys, values, grad_context_t, probs, inverse_total, key_rows, query_rows)
    core = lax.axis_index("fsdp") % 2
    *made, tokens_grad = unproject(
        flat_bound, core.reshape(1), summed_low, d_query, d_key, d_value, key_off, query_off, view,
        jnp.asarray(pick.T, bf), grad_first, context_t, grad_attended, sums, sum_up, seq_len, direct,
        (reps, places, part, features))
    if direct:
        keep, give = made
    else:
        four, d_rel, small = made
        four = four.reshape(4, places, 2, reps // 4, unit, features).transpose(0, 3, 1, 2, 4, 5)
        small = jnp.broadcast_to(small.astype(bf), (reps, places, 2) + small.shape)
        last = jnp.concatenate([
            four.reshape(reps, places, 2, unit, features),
            d_rel.reshape(places, 2, reps, table_cut, features).transpose(2, 0, 1, 3, 4), small], axis=3)
        keep = lax.dynamic_index_in_dim(last, core, 2, keepdims=False)
        give = lax.dynamic_index_in_dim(last, 1 - core, 2, keepdims=False)
    last = (keep.astype(f32) + swap_core(give).astype(f32)).astype(bf)
    early = jnp.concatenate([s_down, s_up.reshape(-1, features)])
    early = lax.psum_scatter(early, "rep", scatter_dimension=0, tiled=True)
    last = summed_over(swap_rep(last))
    early = after(early, last)
    early = lax.all_gather(early, "rep", axis=0, tiled=True)
    last = summed_over(swap_line(last))
    small = last[unit + table_cut : unit + table_cut + vector_count].astype(f32)
    small = lax.dynamic_slice_in_dim(small[: vector_count - up_parts], lax.axis_index("fsdp") * cut, cut, 1)
    d_b_up = last[unit + table_cut + vector_count - up_parts : unit + table_cut + vector_count].astype(f32)
    d_b_up = lax.dynamic_slice_in_dim(d_b_up.reshape(-1), lax.axis_index("fsdp") * up_parts * cut, up_parts * cut, 0)
    both = swap_rep(spread(last[: unit + table_cut], reps)).astype(f32)
    four = both[:, :unit].reshape(4, cut, features)
    s_q, s_k, s_v, s_o = four[0], four[1], four[2], four[3]
    s_rel = both[:, unit:].reshape(-1, features)
    (d_b_query, d_b_key, d_b_value, d_b_out, d_first_gain, d_first_shift, d_b_down,
     d_second_gain, d_second_shift, d_type_zero, d_type_one) = [
        small[k] for k in range(vector_count - up_parts)]
    s_down = early[: w_down.shape[0]].astype(f32)
    s_up = early[w_down.shape[0] :].reshape(up_parts, cut, features).transpose(1, 0, 2)
    s_up = s_up.reshape(cut, -1).astype(f32)
    return (
        layer_out.reshape(tokens.shape), tokens_grad.reshape(tokens.shape),
        s_q, d_b_query, s_k, d_b_key, s_v, d_b_value, s_o, d_b_out,
        d_first_gain, d_first_shift, s_up, d_b_up, s_down, d_b_down,
        d_second_gain, d_second_shift, s_rel, jnp.stack([d_type_zero, d_type_one]),
    )


def solution(mesh):
    seq = P(None, ("rep", "fsdp"), None, None)
    flat = P(None, ("rep", "fsdp"))
    mat, vec = P("fsdp", None), P("fsdp")
    weights = (mat, vec, mat, vec, mat, vec, mat, vec, vec, vec, mat, vec, mat, vec, vec, vec, mat,
               P(None, "fsdp"))
    return jax.shard_map(
        per_device,
        mesh=mesh,
        in_specs=(seq, flat, flat) + weights + (seq,),
        out_specs=(seq, seq) + weights,
        check_vma=False,
    )
```

time: 501 us -> 396 us (0.79)
  matrix products: 139 us -> 0 us
  Pallas kernels: 110 us -> 182 us
  blocking collectives: 24.8 us -> 0 us
  local copies, waits for them, and re-layouts: 28.9 us -> 12 us
  waiting for transfers between devices: 120 us -> 129 us
  other arithmetic: 31.3 us -> 25.8 us
    dot_general x28 -> x0, matrix products: 139 us -> none  [the longest x10 67.3 us: nn(): lax.dot_general(a, b, (((1,), (0,)), ((), ())), preferred_element_type=f32)]
    pallas_call x0 -> x5, Pallas kernels: none -> 99.4 us  [the longest x1 42.3 us: ffn(): pl.pallas_call(lambda *refs: ffn_kernel(*refs, seq_len=seq_len), grid_spe...]
    psum x1 -> x0, waiting for transfers between devices: 24.9 us -> none  [per_device(): s_down, s_up = lax.psum((s_down, s_up), 'rep')]
    all_to_all x1 -> x0, blocking collectives: 24.8 us -> none  [swap_line(): return lax.all_to_all(a, 'fsdp', 0, 0, tiled=True, axis_index_groups=groups)]
    pallas_call x1, Pallas kernels: 72.2 us -> 51.5 us  [attn_bwd(): pl.pallas_call(attn_bwd_kernel, grid=(NP, M), in_specs=[tok(0), tok(0), t...]
    reduce_scatter x2 -> x3, waiting for transfers between devices: 0.04 us -> 15.4 us  [the longest x1 10 us: per_device(): lax.psum_scatter(outer(hidden_low, grad_raised, False), 'fsdp', scatter_d...]
    all_to_all x0 -> x1, waiting for transfers between devices: none -> 14.3 us  [swap_line(): return lax.all_to_all(a, 'fsdp', 0, 0, tiled=True, axis_index_groups=groups)]
    unnamed x147 -> x11, local copies, waits for them, and re-layouts: 12.6 us -> 1.69 us
  transfers between devices with their start and end apart: 19 -> 21, of which waited for: 12 -> 15; matrix products, arithmetic and copies ran while one was open for 22% -> 7% of each run, Pallas kernels for 22% -> 33%
where the time goes in v3:
time: 396 us
  Pallas kernels  182 us (46%)
  waiting for transfers between devices  129 us (33%)
  starting transfers between devices  32.2 us (8%)
  other arithmetic  25.8 us (7%)
  between operations  14.5 us (4%)
  local copies, waits for them, and re-layouts  12 us (3%)
    pallas_call x1, Pallas kernels, attn_bwd(): pl.pallas_call(attn_bwd_kernel, grid=(NP, M), in_specs=[tok(0), tok(0), t...  51.5 us
    all_to_all x2, waiting for transfers between devices, swap_rep(): return lax.all_to_all(a, 'rep', 0, 0, tiled=True)  44.2 us
    pallas_call x1, Pallas kernels, ffn(): pl.pallas_call(lambda *refs: ffn_kernel(*refs, seq_len=seq_len), grid_spe...  42.3 us
    pallas_call x1, Pallas kernels, attn_fwd(): pl.pallas_call(attn_fwd_kernel, grid_spec=pltpu.PrefetchScalarGridSpec(nu...  31.5 us
    pallas_call x1, Pallas kernels, unproject(): pl.pallas_call(lambda *refs: unproject_kernel(*refs, seq_len=seq_len, dir...  23.6 us
    pallas_call x2, Pallas kernels, outer(): pl.pallas_call(outer_kernel, grid=(blocks,), in_specs=[moving, fixed] if...  18.8 us
    ppermute x6, waiting for transfers between devices, along_line(): lax.ppermute(a, 'fsdp', [(i, i + 2 * step) for i in range(n) if 0 <= i +...  16.3 us
    ppermute x4, waiting for transfers between devices, flip_rep(): lax.ppermute(a, 'rep', [(i, i ^ bit) for i in range(lax.axis_size('rep'))])  15.7 us
  transfers between devices with their start and end apart: 21, of which 15 were waited for; matrix products, arithmetic and copies ran while one was open for 7% of the time, Pallas kernels for 33%

profile of v3, /device:TPU:0, one launch (start us, length us, event | category | flops | bytes accessed | tf_op | source)
XLA Modules:
  0.0 395.5 jit_solution(13161172745631720049)
XLA Ops:
  10.9 7.0 %collective-permute-start = (bf16[128,768]{1,0:T(8,128)(2,1)S(1)}, bf16[128,768]{1,0:T(8,128)(2,1)S(1)}, u32[]{:S(2)}, u32[]{:S(2)}) collective-permute-start(bf16[128,768]{1,0:T(8,128)(2,1)S(1)} %dynamic-slice_bitcast_fusion), channel_id=1, source_target_pairs={{0,6},{1,7},{8,14},{9,15},{16,22},{17,23},{24,30},{25,31}} | collective-permute-start | bytes 589832 | tf_op jit(solution)/shard_map/ppermute | solution.py:567
  19.2 2.5 collective-permute-start.2
  25.7 1.8 collective-permute-done.1
  27.5 3.0 collective-permute-done.2
  30.6 11.4 %collective-permute-done.4 = bf16[128,768]{1,0:T(8,128)(2,1)S(1)} collective-permute-done((bf16[128,768]{1,0:T(8,128)(2,1)S(1)}, bf16[128,768]{1,0:T(8,128)(2,1)S(1)}, u32[]{:S(2)}, u32[]{:S(2)}) %collective-permute-start.4) | collective-permute-done | bytes 196640 | tf_op jit(solution)/shard_map/ppermute | solution.py:567
  45.4 4.5 %collective-permute-done.8 = bf16[1,3,128,384]{3,2,0,1:T(8,128)(2,1)S(1)} collective-permute-done((bf16[1,3,128,384]{3,2,0,1:T(8,128)(2,1)S(1)}, bf16[1,3,128,384]{3,2,0,1:T(8,128)(2,1)S(1)}, u32[]{:S(2)}, u32[]{:S(2)}) %collective-permute-start.8) | collective-permute-done | bytes 294944 | tf_op jit(solution)/shard_map/ppermute | solution.py:575
  54.4 9.4 %collective-permute-done.9 = bf16[2,3,128,384]{3,2,0,1:T(8,128)(2,1)S(1)} collective-permute-done((bf16[2,3,128,384]{3,2,0,1:T(8,128)(2,1)S(1)}, bf16[2,3,128,384]{3,2,0,1:T(8,128)(2,1)S(1)}, u32[]{:S(2)}, u32[]{:S(2)}) %collective-permute-start.9) | collective-permute-done | bytes 589856 | tf_op jit(solution)/shard_map/ppermute | solution.py:575
  64.1 1.6 collective-permute-done.7
  66.2 2.4 select_select_fusion
  68.6 6.0 %collective-permute-done.10 = bf16[4,4,128,768]{3,2,1,0:T(8,128)(2,1)} collective-permute-done((bf16[4,4,128,768]{3,2,1,0:T(8,128)(2,1)}, bf16[4,4,128,768]{3,2,1,0:T(8,128)(2,1)}, u32[]{:S(2)}, u32[]{:S(2)}) %collective-permute-start.10) | collective-permute-done | bytes 3145760 | tf_op jit(solution)/shard_map/ppermute | solution.py:556
  74.6 4.0 %select_bitcast_fusion.1 = (bf16[4,1,4,128,768]{4,3,2,1,0:T(8,128)(2,1)S(1)}, bf16[4,1,4,128,768]{4,3,2,1,0:T(8,128)(2,1)S(1)}) fusion(bf16[4,4,128,768]{3,2,1,0:T(8,128)(2,1)} %collective-permute-done.10, pred[]{:T(512)S(6)} %eq.29, bf16[3,4,128,768]{3,2,1,0:T(8,128)(2,1)} %copy-done.1, pred[4]{0:T(512)(128)(4,1)S(1)} %get-tuple-element.161, ...), kind=kLoop, calls=%fused_computation.5 | loop fusion | flops 6291456 | bytes 12582921 | tf_op jit(solution)/shard_map/stack | solution.py:623
  82.4 5.1 %pad_maximum_fusion.refs_2_.refs_3_.refs_4_.refs_5_.refs_8_.refs_9_.refs_10_.refs_11_ = bf16[4,2,4,128,768]{4,3,2,1,0:T(8,128)(2,1)} fusion(bf16[4,1,4,128,768]{4,3,2,1,0:T(8,128)(2,1)} %copy-done, bf16[4,1,4,128,768]{4,3,2,1,0:T(8,128)(2,1)S(1)} %get-tuple-element.126), kind=kLoop, calls=%fused_computation.1 | loop fusion | flops 3145728 | bytes 12582912 | tf_op jit(solution)/shard_map/stack | solution.py:623
  87.5 14.7 %shard_map.401 = (bf16[1024,768]{1,0:T(8,128)(2,1)}, bf16[1024,768]{1,0:T(8,128)(2,1)}, bf16[1024,768]{1,0:T(8,128)(2,1)}, bf16[1024,768]{1,0:T(8,128)(2,1)}, bf...) custom-call(s32[2]{0:T(128)} %bitcast.121, ...), custom_call_target="tpu_custom_call" | custom-call | flops 7247757312 | bytes 16121856 | tf_op jit(solution)/shard_map/pallas_call | solution.py:280
  102.2 31.5 %shard_map.402 = (bf16[768,1024]{1,0:T(8,128)(2,1)}, bf16[2,12,512,512]{3,2,1,0:T(8,128)(2,1)}, f32[2,6,2,512]{3,2,1,0:T(2,128)}) custom-call(s32[2]{0:T(128)} %bitcast.134, bf16[1024,768]{1,0:T(8,128)(2,1)} %get-tuple-element.54.q_ref, bf16[1024,768]{1,0:T(8,128)(2,1)} %get-tuple-element.55.k_ref, bf16[1024,768]{1,0:T(8,128)(2,1)} %get-tuple-element.56.v_ref, ...), custom_call_target="tpu_custom_call" | custom-call | flops 9663676416 | bytes 12582912 | tf_op jit(solution)/shard_map/pallas_call | solution.py:86
  133.7 10.8 %all-gather.6.cloned.1.call-done.refs_6_ = bf16[3072,768]{1,0:T(8,128)(2,1)} async-done(((bf16[384,768]{1,0:T(8,128)(2,1)}), bf16[3072,768]{1,0:T(8,128)(2,1)}) %all-gather.6.cloned.1.call-update) | async-done | bytes 4718608 | tf_op jit(solution)/shard_map/all_gather | solution.py:661
  144.4 42.3 %shard_map.403 = (bf16[1024,768]{1,0:T(8,128)(2,1)}, bf16[1024,768]{1,0:T(8,128)(2,1)}, bf16[1024,3072]{1,0:T(8,128)(2,1)}, bf16[1024,768]{1,0:T(8,128)(2,1)}, b...) custom-call(s32[2]{0:T(128)} %bitcast.122, ...), custom_call_target="tpu_custom_call" | custom-call | flops 21743271936 | bytes 34603008 | tf_op jit(solution)/shard_map/pallas_call | solution.py:502
  186.8 9.2 %shard_map.406 = bf16[4,768,768]{2,1,0:T(8,128)(2,1)} custom-call(bf16[1024,3072]{1,0:T(8,128)(2,1)} %get-tuple-element.81.left_ref, bf16[1024,768]{1,0:T(8,128)(2,1)} %get-tuple-element.82.right_ref), custom_call_target="tpu_custom_call" | custom-call | flops 4831838208 | bytes 11010048 | tf_op jit(solution)/shard_map/pallas_call | solution.py:538
  196.0 9.6 %shard_map.407 = bf16[4,768,768]{2,1,0:T(8,128)(2,1)} custom-call(bf16[1024,768]{1,0:T(8,128)(2,1)} %get-tuple-element.83.left_ref, bf16[1024,3072]{1,0:T(8,128)(2,1)} %get-tuple-element.84.right_ref), custom_call_target="tpu_custom_call" | custom-call | flops 4831838208 | bytes 11010048 | tf_op jit(solution)/shard_map/pallas_call | solution.py:538
  205.6 51.5 %shard_map.404 = (bf16[1024,768]{1,0:T(8,128)(2,1)}, bf16[1024,768]{1,0:T(8,128)(2,1)}, bf16[1024,768]{1,0:T(8,128)(2,1)}, bf16[768,1024]{1,0:T(8,128)(2,1)}, bf16[768,1024]{1,0:T(8,128)(2,1)}) custom-call(bf16[1024,768]{1,0:T(8,128)(2,1)} %get-tuple-element.54.q_ref, bf16[1024,768]{1,0:T(8,128)(2,1)} %get-tuple-element.55.k_ref, ...), custom_call_target="tpu_custom_call" | custom-call | flops 19327352832 | bytes 12582912 | tf_op jit(solution)/shard_map/pallas_call | solution.py:186
  257.1 23.6 %shard_map.405 = (bf16[4,4,128,768]{3,2,1,0:T(8,128)(2,1)}, bf16[4,4,128,768]{3,2,1,0:T(8,128)(2,1)}, bf16[1024,768]{1,0:T(8,128)(2,1)}) custom-call(s32[2]{0:T(128)} %bitcast.123, s32[1]{0:T(128)} %bitcast.41.refs_1_, bf16[1024,768]{1,0:T(8,128)(2,1)} %get-tuple-element.63.refs_2_, bf16[1024,768]{1,0:T(8,128)(2,1)} %get-tuple-element.69.refs_3_, ...), custom_call_target="tpu_custom_call" | custom-call | flops 14092861440 | bytes 23986176 | tf_op jit(solution)/shard_map/pallas_call | solution.py:397
  281.3 5.7 %collective-permute-done.11 = bf16[4,4,128,768]{3,2,1,0:T(8,128)(2,1)S(1)} collective-permute-done((bf16[4,4,128,768]{3,2,1,0:T(8,128)(2,1)}, bf16[4,4,128,768]{3,2,1,0:T(8,128)(2,1)S(1)}, u32[]{:S(2)}, u32[]{:S(2)}) %collective-permute-start.11) | collective-permute-done | bytes 3145760 | tf_op jit(solution)/shard_map/ppermute | solution.py:556
  287.0 4.6 %add_convert_fusion = bf16[4,4,128,768]{3,2,1,0:T(8,128)(2,1)} fusion(bf16[4,4,128,768]{3,2,1,0:T(8,128)(2,1)S(1)} %collective-permute-done.11, bf16[4,4,128,768]{3,2,1,0:T(8,128)(2,1)} %get-tuple-element.79), kind=kLoop, calls=%fused_computation.3 | loop fusion | flops 6291456 | bytes 9437184 | tf_op jit(solution)/shard_map/convert_element_type | solution.py:708
  291.6 3.7 all-to-all-start
  295.4 10.0 %reduce-scatter.6.cloned.1.call-done = bf16[4,96,768]{2,1,0:T(8,128)(2,1)} async-done(((bf16[4,768,768]{2,1,0:T(8,128)(2,1)}), bf16[4,96,768]{2,1,0:T(8,128)(2,1)}) %reduce-scatter.6.cloned.1.call-update) | async-done | bytes 589840 | tf_op jit(solution)/shard_map/reduce_scatter | solution.py:689
  305.4 2.3 pad_maximum_fusion.2
  307.7 30.5 %all-to-all-done = bf16[4,4,128,768]{3,2,1,0:T(8,128)(2,1)S(1)} async-done(((bf16[4,4,128,768]{3,2,1,0:T(8,128)(2,1)}), bf16[4,4,128,768]{3,2,1,0:T(8,128)(2,1)S(1)}, u32[]{:S(2)}, u32[]{:S(2)}) %all-to-all-start) | async-done | bytes 3145760 | tf_op jit(solution)/shard_map/all_to_all | solution.py:571
  339.8 3.6 all-to-all-start.1
  343.5 5.4 %reduce-scatter.8.cloned.1.call-done = bf16[192,768]{1,0:T(8,128)(2,1)} async-done(((bf16[768,768]{1,0:T(8,128)(2,1)}), bf16[192,768]{1,0:T(8,128)(2,1)}) %reduce-scatter.8.cloned.1.call-update) | async-done | bytes 294928 | tf_op jit(solution)/shard_map/reduce_scatter | solution.py:710
  348.8 14.3 %all-to-all-done.1 = bf16[4,128,768]{2,1,0:T(8,128)(2,1)S(1)} async-done(((bf16[4,128,768]{2,1,0:T(8,128)(2,1)}), bf16[4,128,768]{2,1,0:T(8,128)(2,1)S(1)}, u32[]{:S(2)}, u32[]{:S(2)}) %all-to-all-start.1) | async-done | bytes 786464 | tf_op jit(solution)/shard_map/all_to_all | solution.py:562
  364.2 3.5 all-to-all-start.2
  369.6 13.7 %all-to-all-done.2 = bf16[4,112,768]{2,1,0:T(8,128)(2,1)S(1)} async-done(((bf16[4,112,768]{2,1,0:T(8,128)(2,1)}), bf16[4,112,768]{2,1,0:T(8,128)(2,1)S(1)}, u32[]{:S(2)}, u32[]{:S(2)}) %all-to-all-start.2) | async-done | bytes 688160 | tf_op jit(solution)/shard_map/all_to_all | solution.py:571
  385.1 2.4 slice_convert_fusion
  (83 shorter events, 29.4 us)
Async XLA Ops:
  7.2 126.5 %all-gather.4.cloned.1.call-start = ((), (), s32[]{:S(2)}) async-start(), calls=%async_computation.6 | async-start | bytes 5308416 | tf_op jit(solution)/shard_map/all_gather | solution.py:660
  10.9 55.2 %copy-start.2 = (bf16[4,128,768]{2,1,0:T(8,128)(2,1)}, bf16[4,128,768]{2,1,0:T(8,128)(2,1)S(1)}, u32[]{:S(2)}) copy-start(bf16[4,128,768]{2,1,0:T(8,128)(2,1)S(1)} %pad_maximum_fusion.3) | copy-start | bytes 2359300
  10.9 13.4 %collective-permute-start = (bf16[128,768]{1,0:T(8,128)(2,1)S(1)}, bf16[128,768]{1,0:T(8,128)(2,1)S(1)}, u32[]{:S(2)}, u32[]{:S(2)}) collective-permute-start(bf16[128,768]{1,0:T(8,128)(2,1)S(1)} %dynamic-slice_bitcast_fusion), channel_id=1, source_target_pairs={{0,6},{1,7},{8,14},{9,15},{16,22},{17,23},{24,30},{25,31}} | collective-permute-start | bytes 589832 | tf_op jit(solution)/shard_map/ppermute | solution.py:567
  17.9 9.6 %collective-permute-start.1 = (bf16[128,768]{1,0:T(8,128)(2,1)S(1)}, bf16[128,768]{1,0:T(8,128)(2,1)S(1)}, u32[]{:S(2)}, u32[]{:S(2)}) collective-permute-start(bf16[128,768]{1,0:T(8,128)(2,1)S(1)} %dynamic-slice_bitcast_fusion), channel_id=1, source_target_pairs={{0,4},{1,5},{2,6},{3,7},{8,12},{9,13},{10,14},{11,15},{16,20},{17,... | collective-permute-start | bytes 589832 | tf_op jit(solution)/shard_map/ppermute | solution.py:567
  19.2 11.3 %collective-permute-start.2 = (bf16[128,768]{1,0:T(8,128)(2,1)S(1)}, bf16[128,768]{1,0:T(8,128)(2,1)S(1)}, u32[]{:S(2)}, u32[]{:S(2)}) collective-permute-start(bf16[128,768]{1,0:T(8,128)(2,1)S(1)} %dynamic-slice_bitcast_fusion), channel_id=1, source_target_pairs={{0,2},{1,3},{2,4},{3,5},{4,6},{5,7},{8,10},{9,11},{10,12},{11,13},... | collective-permute-start | bytes 589832 | tf_op jit(solution)/shard_map/ppermute | solution.py:567
  21.7 8.9 %collective-permute-start.3 = (bf16[128,768]{1,0:T(8,128)(2,1)S(1)}, bf16[128,768]{1,0:T(8,128)(2,1)S(1)}, u32[]{:S(2)}, u32[]{:S(2)}) collective-permute-start(bf16[128,768]{1,0:T(8,128)(2,1)S(1)} %dynamic-slice_bitcast_fusion), channel_id=1, source_target_pairs={{2,0},{3,1},{4,2},{5,3},{6,4},{7,5},{10,8},{11,9},{12,10},{13,11},... | collective-permute-start | bytes 589832 | tf_op jit(solution)/shard_map/ppermute | solution.py:567
  23.0 19.0 %collective-permute-start.4 = (bf16[128,768]{1,0:T(8,128)(2,1)S(1)}, bf16[128,768]{1,0:T(8,128)(2,1)S(1)}, u32[]{:S(2)}, u32[]{:S(2)}) collective-permute-start(bf16[128,768]{1,0:T(8,128)(2,1)S(1)} %dynamic-slice_bitcast_fusion), channel_id=1, source_target_pairs={{4,0},{5,1},{6,2},{7,3},{12,8},{13,9},{14,10},{15,11},{20,16},{21,... | collective-permute-start | bytes 589832 | tf_op jit(solution)/shard_map/ppermute | solution.py:567
  24.3 17.7 %collective-permute-start.5 = (bf16[128,768]{1,0:T(8,128)(2,1)S(1)}, bf16[128,768]{1,0:T(8,128)(2,1)S(1)}, u32[]{:S(2)}, u32[]{:S(2)}) collective-permute-start(bf16[128,768]{1,0:T(8,128)(2,1)S(1)} %dynamic-slice_bitcast_fusion), channel_id=1, source_target_pairs={{6,0},{7,1},{14,8},{15,9},{22,16},{23,17},{30,24},{31,25}} | collective-permute-start | bytes 589832 | tf_op jit(solution)/shard_map/ppermute | solution.py:567
  42.2 102.3 %all-gather.6.cloned.1.call-start = ((), (), s32[]{:S(2)}) async-start(), calls=%async_computation.7 | async-start | bytes 5308416 | tf_op jit(solution)/shard_map/all_gather | solution.py:661
  42.3 7.6 %collective-permute-start.8 = (bf16[1,3,128,384]{3,2,0,1:T(8,128)(2,1)S(1)}, bf16[1,3,128,384]{3,2,0,1:T(8,128)(2,1)S(1)}, u32[]{:S(2)}, u32[]{:S(2)}) collective-permute-start(bf16[1,3,128,384]{3,2,0,1:T(8,128)(2,1)S(1)} %get-tuple-element.143), channel_id=1, source_target_pairs={{0,16},{8,24},{16,0},{24,8},{1,17},{9,25},{17,1},{25,9},{2,18},{10... | collective-permute-start | bytes 884744 | tf_op jit(solution)/shard_map/ppermute | solution.py:575
  43.9 7.9 %collective-permute-start.6 = (bf16[1,3,128,384]{3,2,1,0:T(8,128)(2,1)S(1)}, bf16[1,3,128,384]{3,2,1,0:T(8,128)(2,1)}, u32[]{:S(2)}, u32[]{:S(2)}) collective-permute-start(bf16[1,3,128,384]{3,2,1,0:T(8,128)(2,1)S(1)} %get-tuple-element.142), channel_id=1, source_target_pairs={{0,8},{8,0},{16,24},{24,16},{1,9},{9,1},{17,25},{25,17},{2,10},{10... | collective-permute-start | bytes 884744 | tf_op jit(solution)/shard_map/ppermute | solution.py:575
  50.0 13.7 %collective-permute-start.9 = (bf16[2,3,128,384]{3,2,0,1:T(8,128)(2,1)S(1)}, bf16[2,3,128,384]{3,2,0,1:T(8,128)(2,1)S(1)}, u32[]{:S(2)}, u32[]{:S(2)}) collective-permute-start(bf16[2,3,128,384]{3,2,0,1:T(8,128)(2,1)S(1)} %pad_maximum_fusion.5), channel_id=1, source_target_pairs={{0,8},{8,0},{16,24},{24,16},{1,9},{9,1},{17,25},{25,17},{2,10},{10... | collective-permute-start | bytes 1769480 | tf_op jit(solution)/shard_map/ppermute | solution.py:575
  51.6 243.7 %reduce-scatter.4.cloned.1.call-start = ((), (), s32[]{:S(2)}) async-start(), calls=%async_computation.8 | async-start | bytes 5308416 | tf_op jit(solution)/shard_map/reduce_scatter | solution.py:688
  52.9 12.8 %collective-permute-start.7 = (bf16[2,3,128,384]{3,2,1,0:T(8,128)(2,1)S(1)}, bf16[2,3,128,384]{3,2,1,0:T(8,128)(2,1)S(1)}, u32[]{:S(2)}, u32[]{:S(2)}) collective-permute-start(bf16[2,3,128,384]{3,2,1,0:T(8,128)(2,1)S(1)} %pad_maximum_fusion.4), channel_id=1, source_target_pairs={{0,16},{8,24},{16,0},{24,8},{1,17},{9,25},{17,1},{25,9},{2,18},{10... | collective-permute-start | bytes 1769480 | tf_op jit(solution)/shard_map/ppermute | solution.py:575
  66.1 2.5 copy-start.1
  68.6 6.0 %collective-permute-start.10 = (bf16[4,4,128,768]{3,2,1,0:T(8,128)(2,1)}, bf16[4,4,128,768]{3,2,1,0:T(8,128)(2,1)}, u32[]{:S(2)}, u32[]{:S(2)}) collective-permute-start(bf16[4,4,128,768]{3,2,1,0:T(8,128)(2,1)} %select_select_fusion), channel_id=1, source_target_pairs={{0,1},{1,0},{2,3},{3,2},{4,5},{5,4},{6,7},{7,6},{8,9},{9,8},{10,11... | collective-permute-start | bytes 9437192 | tf_op jit(solution)/shard_map/ppermute | solution.py:556
  78.6 1.6 copy-start
  195.9 109.4 %reduce-scatter.6.cloned.1.call-start = ((), (), s32[]{:S(2)}) async-start(), calls=%async_computation.9 | async-start | bytes 5308416 | tf_op jit(solution)/shard_map/reduce_scatter | solution.py:689
  280.7 6.2 %collective-permute-start.11 = (bf16[4,4,128,768]{3,2,1,0:T(8,128)(2,1)}, bf16[4,4,128,768]{3,2,1,0:T(8,128)(2,1)S(1)}, u32[]{:S(2)}, u32[]{:S(2)}) collective-permute-start(bf16[4,4,128,768]{3,2,1,0:T(8,128)(2,1)} %get-tuple-element.80), channel_id=1, source_target_pairs={{0,1},{1,0},{2,3},{3,2},{4,5},{5,4},{6,7},{7,6},{8,9},{9,8},{10,11... | collective-permute-start | bytes 9437192 | tf_op jit(solution)/shard_map/ppermute | solution.py:556
  291.6 46.7 %all-to-all-start = ((bf16[4,4,128,768]{3,2,1,0:T(8,128)(2,1)}), bf16[4,4,128,768]{3,2,1,0:T(8,128)(2,1)S(1)}, u32[]{:S(2)}, u32[]{:S(2)}) async-start(bf16[4,4,128,768]{3,2,1,0:T(8,128)(2,1)} %add_convert_fusion), calls=%async_computation | async-start | bytes 6291456 | tf_op jit(solution)/shard_map/all_to_all | solution.py:571
  295.3 53.5 %reduce-scatter.8.cloned.1.call-start = ((), (), s32[]{:S(2)}) async-start(), calls=%async_computation.10 | async-start | bytes 1474560 | tf_op jit(solution)/shard_map/reduce_scatter | solution.py:710
  339.8 23.3 %all-to-all-start.1 = ((bf16[4,128,768]{2,1,0:T(8,128)(2,1)}), bf16[4,128,768]{2,1,0:T(8,128)(2,1)S(1)}, u32[]{:S(2)}, u32[]{:S(2)}) async-start(bf16[4,128,768]{2,1,0:T(8,128)(2,1)} %reduce_sum.24), calls=%async_computation.1 | async-start | bytes 1572864 | tf_op jit(solution)/shard_map/all_to_all | solution.py:562
  343.4 41.7 %all-gather.8.cloned.1.call-start = ((), (), s32[]{:S(2)}) async-start(), calls=%async_computation.11 | async-start | bytes 1474560 | tf_op jit(solution)/shard_map/all_gather | solution.py:713
  364.2 19.0 %all-to-all-start.2 = ((bf16[4,112,768]{2,1,0:T(8,128)(2,1)}), bf16[4,112,768]{2,1,0:T(8,128)(2,1)S(1)}, u32[]{:S(2)}, u32[]{:S(2)}) async-start(bf16[4,112,768]{2,1,0:T(8,128)(2,1)} %broadcast_in_dim.50), calls=%async_computation.2 | async-start | bytes 1376256 | tf_op jit(solution)/shard_map/all_to_all | solution.py:571
Sparse Core Ops, SparseCore 0:
  42.3 49.9 all-gather.3
  93.9 50.5 all-gather.5
  196.1 53.7 reduce-scatter.3
  252.0 53.3 reduce-scatter.5
  308.7 40.0 reduce-scatter.7
  350.5 32.9 all-gather.7

commit v4 on v3

--- a/solution.py
+++ b/solution.py
@@ -142,10 +142,11 @@
         dv=t if dv is None else dv+t
         dcw=wide(dcs)
         delta=None
+        dp=nn(vr,dcw)
         for b in range(nb):
             js=slice(b*BLK,(b+1)*BLK)
             p=nn(flip,p_ref[0,h,(nb-1-b)*BLK:(nb-b)*BLK,:])
-            t=p*nn(vr[js],dcw)
+            t=p*dp[js]
             p_scr[h,js,:]=p
             t_scr[h,js,:]=t
             t=jnp.sum(t,axis=0,keepdims=True)
@@ -230,7 +231,8 @@
 
 
 def project_kernel(
-    bound_ref, tokens_ref, w_q_ref, w_k_ref, w_v_ref, rel_ref, pick_ref, pick_t_ref, pick_back_t_ref, vec_ref,
+    bound_ref, core_ref, tokens_ref, w_q_ref, w_q2_ref, w_k_ref, w_k2_ref, w_v_ref, w_v2_ref, rel_ref, rel2_ref,
+    pick_ref, pick_t_ref, pick_back_t_ref, vec_ref,
     type_ref, q_ref, k_ref, v_ref, key_ref, query_ref, key_back_ref, query_t_ref, low_ref, *, seq_len,
 ):
     rows = tokens_ref.shape[0]
@@ -243,9 +245,12 @@
         ).astype(bf)
 
     low = low_ref[...]
-    rel = rel_ref[...].reshape(-1, tokens_ref.shape[1])
+    first = core_ref[0] == 0
+    rel = in_order(rel_ref, rel2_ref, first, pick_ref.shape[1])
     features = tokens_ref.shape[1]
-    w_q, w_k, w_v = [r[...].reshape(features, -1) for r in (w_q_ref, w_k_ref, w_v_ref)]
+    w_q = in_order(w_q_ref, w_q2_ref, first, features)
+    w_k = in_order(w_k_ref, w_k2_ref, first, features)
+    w_v = in_order(w_v_ref, w_v2_ref, first, features)
     b_q, b_k = vec_ref[0:1, :], vec_ref[1:2, :]
     q_ref[...] = (nn(low, w_q) + b_q).astype(bf)
     k_ref[...] = (nn(low, w_k) + b_k).astype(bf)
@@ -259,34 +264,44 @@
 
 
 def weight_view(view, g, columns):
-    lead, rows = view[1], view[2]
-    return pl.BlockSpec(lead + (1, rows, columns), lambda i, *_: (0, 0, g, 0, i if columns == COLUMNS else 0),
+    spec = pl.BlockSpec((view[0].shape[0], 1, view[2], columns), lambda i, *_: (0, g, 0, i if columns == COLUMNS else 0),
                         pipeline_mode=None if columns == COLUMNS else pl.Buffered(1))
+    return [spec, spec]
 
 
 def table_view(view):
-    return pl.BlockSpec(view[4], lambda i, *_: view[5], pipeline_mode=pl.Buffered(1))
-
-
-def project(boundary, tokens, view, pick, pick_t, pick_back_t, vec, types, seq_len):
+    spec = pl.BlockSpec(view[5], lambda i, *_: view[6], pipeline_mode=pl.Buffered(1))
+    return [spec, spec]
+
+
+def in_order(own_ref, other_ref, first, rows):
+    own = own_ref[...]
+    columns = own.shape[-1]
+    if own.size == rows * columns:
+        return own.reshape(rows, columns)
+    other = other_ref[...]
+    both = jnp.stack([jnp.where(first, own, other), jnp.where(first, other, own)], axis=1)
+    return both.reshape(rows, columns)
+
+
+def project(boundary, core, tokens, view, pick, pick_t, pick_back_t, vec, types, seq_len):
     total, features = tokens.shape
-    four, table = view[0], view[3]
     table_rows = pick.shape[1]
-    whole = lambda a: pl.BlockSpec(a.shape, lambda i, _: (0,) * a.ndim, pipeline_mode=pl.Buffered(1))
+    whole = lambda a: pl.BlockSpec(a.shape, lambda i, *_: (0,) * a.ndim, pipeline_mode=pl.Buffered(1))
     weight = lambda g: weight_view(view, g, COLUMNS)
-    columns = lambda rows: pl.BlockSpec((rows, COLUMNS), lambda i, _: (0, i))
+    columns = lambda rows: pl.BlockSpec((rows, COLUMNS), lambda i, *_: (0, i))
     shape = jax.ShapeDtypeStruct
     offsets = pick.shape[0]
     return pl.pallas_call(
         lambda *refs: project_kernel(*refs, seq_len=seq_len),
         grid_spec=pltpu.PrefetchScalarGridSpec(
-            num_scalar_prefetch=1,
+            num_scalar_prefetch=2,
             grid=(features // COLUMNS,),
-            in_specs=[whole(tokens), weight(0), weight(1), weight(2), table_view(view), whole(pick),
+            in_specs=[whole(tokens), *weight(0), *weight(1), *weight(2), *table_view(view), whole(pick),
                       whole(pick_t), whole(pick_back_t), columns(vec.shape[0]), whole(types)],
             out_specs=[columns(total)] * 3 + [columns(offsets)] * 2
-            + [pl.BlockSpec((COLUMNS, offsets), lambda i, _: (i, 0))] * 2
-            + [pl.BlockSpec((total, features), lambda i, _: (0, 0))],
+            + [pl.BlockSpec((COLUMNS, offsets), lambda i, *_: (i, 0))] * 2
+            + [pl.BlockSpec((total, features), lambda i, *_: (0, 0))],
         ),
         out_shape=[shape((total, features), bf)] * 3 + [shape((offsets, features), bf)] * 2
         + [shape((features, offsets), bf)] * 2
@@ -295,30 +310,32 @@
         cost_estimate=pl.CostEstimate(
             flops=2 * features * features * (3 * total + 2 * table_rows) + 6 * offsets * features * table_rows,
             bytes_accessed=2 * features * (3 * features + 5 * total + 3 * offsets), transcendentals=0),
-    )(boundary, tokens, four, four, four, table, pick, pick_t, pick_back_t, vec, types)
+    )(boundary, core, tokens, *(view[:2] * 3), *view[3:5], pick, pick_t, pick_back_t, vec, types)
 
 
 def unproject_kernel(
-    bound_ref, core_ref, low_ref, dq_ref, dk_ref, dv_ref, key_off_ref, query_off_ref, w_q_ref, w_k_ref, w_v_ref,
-    rel_ref, pick_t_ref, grad_first_ref, context_ref, grad_att_ref, sums_ref, sum_up_ref,
+    bound_ref, core_ref, low_ref, dq_ref, dk_ref, dv_ref, key_off_ref, query_off_ref, w_q_ref, w_q2_ref,
+    w_k_ref, w_k2_ref, w_v_ref, w_v2_ref, rel_ref, rel2_ref, pick_t_ref, context_ref, grad_att_ref, sums_ref, sum_up_ref,
     *refs, seq_len, direct,
 ):
     if direct:
-        keep_ref, give_ref, grad_ref, sum_ref, rel_sum_ref, small_ref = refs
+        keep_ref, give_ref, rel_sum_ref, small_ref = refs
     else:
-        dw_ref, drel_ref, small_ref, grad_ref, sum_ref, rel_sum_ref = refs
+        dw_ref, drel_ref, small_ref, rel_sum_ref = refs
     step = pl.program_id(0)
     rows, features = low_ref.shape
     first = core_ref[0] == 0
 
     @pl.when(step == 0)
     def _():
-        sum_ref[...] = grad_first_ref[...]
         rel_sum_ref[...] = jnp.zeros_like(rel_sum_ref)
         small_ref[...] = jnp.zeros_like(small_ref)
-
-    low, rel = low_ref[...], rel_ref[...].reshape(-1, features)
-    w_q, w_k, w_v = [r[...].reshape(features, -1) for r in (w_q_ref, w_k_ref, w_v_ref)]
+        small_ref[9:11, :] = sums_ref[6:8, :]
+
+    low, rel = low_ref[...], in_order(rel_ref, rel2_ref, first, pick_t_ref.shape[0])
+    w_q = in_order(w_q_ref, w_q2_ref, first, features)
+    w_k = in_order(w_k_ref, w_k2_ref, first, features)
+    w_v = in_order(w_v_ref, w_v2_ref, first, features)
     dq, dk, dv = dq_ref[...], dk_ref[...], dv_ref[...]
     columns = pl.ds(pl.multiple_of(step * COLUMNS, COLUMNS), COLUMNS)
 
@@ -343,18 +360,21 @@
     small_ref[0:1, columns] = total(dq) + total(pos_query)
     small_ref[1:2, columns] = total(dk) + total(pos_key)
     small_ref[2:3, columns] = total(dv)
-    sum_ref[...] += nt(dq, w_q) + nt(dk, w_k) + nt(dv, w_v)
+    second = second_rows(bound_ref, rows, seq_len)
+    for values, weight in ((dq, w_q), (dk, w_k), (dv, w_v)):
+        wide = values.astype(f32)
+        parts = jnp.concatenate([total(jnp.where(second, 0.0, wide)), total(jnp.where(second, wide, 0.0))])
+        high = parts.astype(bf)
+        low_part = (parts - high.astype(f32)).astype(bf)
+        stacked = jnp.concatenate([high, low_part, jnp.zeros((12, parts.shape[1]), bf)])
+        product = nt(stacked, weight)
+        small_ref[9:11, :] += product[0:2] + product[2:4]
     rel_sum_ref[...] += nt(low_key, w_k) + nt(low_query, w_q)
 
     @pl.when(step == pl.num_programs(0) - 1)
     def _():
-        values = sum_ref[...]
-        grad_ref[...] = values.astype(bf)
-        second = second_rows(bound_ref, rows, seq_len)
         for at, k in ((3, 5), (4, 3), (5, 4), (6, 2), (7, 0), (8, 1)):
             small_ref[at : at + 1, :] = sums_ref[k : k + 1, :]
-        small_ref[9:10, :] = total(jnp.where(second, 0.0, values))
-        small_ref[10:11, :] = total(jnp.where(second, values, 0.0))
         for k in range(sum_up_ref.shape[1] // features):
             small_ref[11 + k : 12 + k, :] = sum_up_ref[:, k * features : (k + 1) * features]
         if direct:
@@ -372,10 +392,9 @@
             drel_ref[...] = rel_sum_ref[...].astype(bf)
 
 
-def unproject(boundary, core, low, dq, dk, dv, key_off, query_off, view, pick_t, grad_first, context_t, grad_att,
+def unproject(boundary, core, low, dq, dk, dv, key_off, query_off, view, pick_t, context_t, grad_att,
               sums, sum_up, seq_len, direct, parts):
     total, features = low.shape
-    four, table = view[0], view[3]
     table_rows = pick_t.shape[0]
     whole = lambda a: pl.BlockSpec(a.shape, lambda i, *_: (0,) * a.ndim, pipeline_mode=pl.Buffered(1))
     weight = lambda g: weight_view(view, g, COLUMNS)
@@ -384,23 +403,22 @@
     fixed = lambda s: pl.BlockSpec(s, lambda i, *_: (0,) * len(s))
     shape = jax.ShapeDtypeStruct
     small = (16, features)
-    scratch = [pltpu.VMEM((total, features), f32), pltpu.VMEM((table_rows, features), f32)]
+    scratch = [pltpu.VMEM((table_rows, features), f32)]
     if direct:
-        out_specs = [fixed(parts), fixed(parts), fixed((total, features))]
-        out_shape = [shape(parts, bf), shape(parts, bf), shape((total, features), bf)]
+        out_specs = [fixed(parts), fixed(parts)]
+        out_shape = [shape(parts, bf), shape(parts, bf)]
         scratch.append(pltpu.VMEM(small, f32))
     else:
         out_specs = [pl.BlockSpec((4, features, COLUMNS), lambda i, *_: (0, 0, i)), fixed((table_rows, features)),
-                     fixed(small), fixed((total, features))]
-        out_shape = [shape((4, features, features), bf), shape((table_rows, features), bf), shape(small, f32),
-                     shape((total, features), bf)]
+                     fixed(small)]
+        out_shape = [shape((4, features, features), bf), shape((table_rows, features), bf), shape(small, f32)]
     return pl.pallas_call(
         lambda *refs: unproject_kernel(*refs, seq_len=seq_len, direct=direct),
         grid_spec=pltpu.PrefetchScalarGridSpec(
             num_scalar_prefetch=2,
             grid=(features // COLUMNS,),
             in_specs=[whole(low), columns(total), columns(total), columns(total), turned, turned,
-                      weight(0), weight(1), weight(2), table_view(view), whole(pick_t), whole(grad_first),
+                      *weight(0), *weight(1), *weight(2), *table_view(view), whole(pick_t),
                       whole(context_t), columns(total), whole(sums), whole(sum_up)],
             out_specs=out_specs,
             scratch_shapes=scratch,
@@ -408,10 +426,35 @@
         out_shape=out_shape,
         compiler_params=pltpu.CompilerParams(vmem_limit_bytes=VMEM_LIMIT),
         cost_estimate=pl.CostEstimate(
-            flops=2 * features * features * (7 * total + 4 * table_rows) + 8 * total * features * table_rows,
+            flops=2 * features * features * (4 * total + 4 * table_rows) + 8 * total * features * table_rows,
             bytes_accessed=2 * features * (7 * features + 10 * total), transcendentals=0),
-    )(boundary, core, low, dq, dk, dv, key_off, query_off, four, four, four, table, pick_t, grad_first, context_t,
-      grad_att, sums, sum_up)
+    )(boundary, core, low, dq, dk, dv, key_off, query_off, *(view[:2] * 3), *view[3:5], pick_t,
+      context_t, grad_att, sums, sum_up)
+
+
+def token_kernel(core_ref, dq_ref, dk_ref, dv_ref, w_q_ref, w_q2_ref, w_k_ref, w_k2_ref, w_v_ref, w_v2_ref,
+                 grad_first_ref, grad_ref):
+    first, features = core_ref[0] == 0, dq_ref.shape[1]
+    grad_ref[...] = (
+        nt(dq_ref[...], in_order(w_q_ref, w_q2_ref, first, features))
+        + nt(dk_ref[...], in_order(w_k_ref, w_k2_ref, first, features))
+        + nt(dv_ref[...], in_order(w_v_ref, w_v2_ref, first, features)) + grad_first_ref[...]).astype(bf)
+
+
+def token_grads(core, dq, dk, dv, view, grad_first):
+    total, features = dq.shape
+    rows = pl.BlockSpec((total // 2, features), lambda i, *_: (i, 0))
+    weights = [spec for g in range(3) for spec in weight_view(view, g, features)]
+    return pl.pallas_call(
+        token_kernel,
+        grid_spec=pltpu.PrefetchScalarGridSpec(
+            num_scalar_prefetch=1, grid=(2,), in_specs=[rows, rows, rows, *weights, rows], out_specs=rows),
+        out_shape=jax.ShapeDtypeStruct((total, features), bf),
+        compiler_params=pltpu.CompilerParams(vmem_limit_bytes=VMEM_LIMIT),
+        cost_estimate=pl.CostEstimate(
+            flops=6 * total * features * features, bytes_accessed=2 * features * (6 * total + 3 * features),
+            transcendentals=0),
+    )(core, dq, dk, dv, *(view[:2] * 3), grad_first)
 
 
 ROWS = 256
@@ -433,7 +476,7 @@
 
 
 def ffn_kernel(
-    bound_ref, context_ref, tokens_ref, grad_ref, w_o_ref, w_u_ref, w_d_ref, vec_ref, v_up_ref,
+    bound_ref, core_ref, context_ref, tokens_ref, grad_ref, w_o_ref, w_o2_ref, w_u_ref, w_d_ref, vec_ref, v_up_ref,
     out_ref, hidden_ref, active_ref, grad_ffn_ref, grad_raised_ref, grad_first_ref, grad_att_ref,
     grad_ctx_ref, sums_ref, sum_up_ref, slope_ref, *, seq_len,
 ):
@@ -441,12 +484,13 @@
     rows = tokens_ref.shape[0]
     wide = w_u_ref.shape[1]
     vec = lambda k: vec_ref[k : k + 1, :]
+    w_o = in_order(w_o_ref, w_o2_ref, core_ref[0] == 0, tokens_ref.shape[1])
     v_out, g_first, s_first, v_down, g_second, s_second = [vec(k) for k in range(3, 9)]
     seq = step * rows // seq_len
     pos = step * rows - seq * seq_len + lax.broadcasted_iota(jnp.int32, (rows, 1), 0)
     second = pos >= bound_ref[seq]
     summed = tokens_ref[...].astype(f32) + jnp.where(second, vec(10), vec(9))
-    first_normed, first_inverse = normalize(summed + tn(context_ref[...], w_o_ref[...].reshape(tokens_ref.shape[1], -1)) + v_out)
+    first_normed, first_inverse = normalize(summed + tn(context_ref[...], w_o) + v_out)
     hidden = first_normed * g_first + s_first
     hidden_low = hidden.astype(bf)
     hidden_ref[...] = hidden_low
@@ -485,30 +529,32 @@
     add_sum(4, grad_hidden)
     grad_first = normalize_back(grad_hidden * g_first, first_normed, first_inverse)
     grad_first_ref[...] = grad_first
+    add_sum(6, jnp.where(second, 0.0, grad_first))
+    add_sum(7, jnp.where(second, grad_first, 0.0))
     grad_att = grad_first.astype(bf)
     grad_att_ref[...] = grad_att
     add_sum(5, grad_att.astype(f32))
-    grad_ctx_ref[...] = nt(w_o_ref[...].reshape(tokens_ref.shape[1], -1), grad_att).astype(bf)
-
-
-def ffn(boundary, context_t, tokens, out_grad, view, w_u, w_d, vec, v_up, seq_len):
+    grad_ctx_ref[...] = nt(w_o, grad_att).astype(bf)
+
+
+def ffn(boundary, core, context_t, tokens, out_grad, view, w_u, w_d, vec, v_up, seq_len):
     total, features = tokens.shape
     wide = w_u.shape[1]
-    whole = lambda a: pl.BlockSpec(a.shape, lambda i, _: (0, 0), pipeline_mode=pl.Buffered(1))
-    narrow = pl.BlockSpec((ROWS, features), lambda i, _: (i, 0))
-    broad = pl.BlockSpec((ROWS, wide), lambda i, _: (i, 0))
-    turned = pl.BlockSpec((features, ROWS), lambda i, _: (0, i))
+    whole = lambda a: pl.BlockSpec(a.shape, lambda i, *_: (0, 0), pipeline_mode=pl.Buffered(1))
+    narrow = pl.BlockSpec((ROWS, features), lambda i, *_: (i, 0))
+    broad = pl.BlockSpec((ROWS, wide), lambda i, *_: (i, 0))
+    turned = pl.BlockSpec((features, ROWS), lambda i, *_: (0, i))
     shape = jax.ShapeDtypeStruct
     return pl.pallas_call(
         lambda *refs: ffn_kernel(*refs, seq_len=seq_len),
         grid_spec=pltpu.PrefetchScalarGridSpec(
-            num_scalar_prefetch=1,
+            num_scalar_prefetch=2,
             grid=(total // ROWS,),
-            in_specs=[turned, narrow, narrow, weight_view(view, 3, features), whole(w_u), whole(w_d), whole(vec), whole(v_up)],
+            in_specs=[turned, narrow, narrow, *weight_view(view, 3, features), whole(w_u), whole(w_d), whole(vec), whole(v_up)],
             out_specs=[
                 narrow, narrow, broad, narrow, broad, narrow, narrow, turned,
-                pl.BlockSpec((8, features), lambda i, _: (0, 0)),
-                pl.BlockSpec((1, wide), lambda i, _: (0, 0)),
+                pl.BlockSpec((8, features), lambda i, *_: (0, 0)),
+                pl.BlockSpec((1, wide), lambda i, *_: (0, 0)),
             ],
             scratch_shapes=[pltpu.VMEM((ROWS, wide), f32)],
         ),
@@ -523,32 +569,52 @@
             flops=2 * total * features * (4 * wide + 2 * features),
             bytes_accessed=2 * (2 * features * wide + 2 * total * wide + 8 * total * features),
             transcendentals=2 * total * wide),
-    )(boundary, context_t, tokens, out_grad, view[0], w_u, w_d, vec, v_up)
-
-
-def outer_kernel(left_ref, right_ref, out_ref):
-    out_ref[0] = tn(left_ref[...], right_ref[...]).astype(bf)
-
-
-def outer(left, right, cut_left):
-    total, features = left.shape if not cut_left else right.shape
-    blocks = (left if cut_left else right).shape[1] // features
-    moving = pl.BlockSpec((total, features), lambda i: (0, i))
-    fixed = pl.BlockSpec((total, features), lambda i: (0, 0), pipeline_mode=pl.Buffered(1))
+    )(boundary, core, context_t, tokens, out_grad, *view[:2], w_u, w_d, vec, v_up)
+
+
+def outer_kernel(active_ref, grad_ffn_ref, hidden_ref, grad_raised_ref, out_ref):
+    parts, devices, cut, features = out_ref.shape
+    step = pl.program_id(0)
+    half = pl.num_programs(0) // 2
+
+    @pl.when(step < half)
+    def _():
+        for f in range(devices):
+            at = slice(f * parts * cut, (f + 1) * parts * cut)
+            values = tn(active_ref[:, at], grad_ffn_ref[...]).astype(bf)
+            for k in range(parts):
+                out_ref[k, f] = values[k * cut : (k + 1) * cut, :]
+
+    @pl.when(step >= half)
+    def _():
+        for k in range(parts):
+            values = tn(hidden_ref[...], grad_raised_ref[:, k * features : (k + 1) * features]).astype(bf)
+            for f in range(devices):
+                out_ref[k, f] = values[f * cut : (f + 1) * cut, :]
+
+
+def outer(active, grad_ffn, hidden, grad_raised, devices):
+    total, features = hidden.shape
+    wide = active.shape[1]
+    parts, cut = wide // features, features // devices
+    blocks = 2
+    fixed = lambda a: pl.BlockSpec(a.shape, lambda i: (0, 0), pipeline_mode=pl.Buffered(1))
     return pl.pallas_call(
         outer_kernel,
-        grid=(blocks,),
-        in_specs=[moving, fixed] if cut_left else [fixed, moving],
-        out_specs=pl.BlockSpec((1, features, features), lambda i: (i, 0, 0)),
-        out_shape=jax.ShapeDtypeStruct((blocks, features, features), bf),
+        grid=(2 * blocks,),
+        in_specs=[
+            pl.BlockSpec((total, wide // blocks), lambda i: (0, jnp.minimum(i, blocks - 1))), fixed(grad_ffn),
+            pl.BlockSpec((total, features // blocks), lambda i: (0, jnp.maximum(i - blocks, 0))), fixed(grad_raised)],
+        out_specs=pl.BlockSpec((parts, devices // blocks, cut, features), lambda i: (i // blocks, i % blocks, 0, 0)),
+        out_shape=jax.ShapeDtypeStruct((2 * parts, devices, cut, features), bf),
         compiler_params=pltpu.CompilerParams(vmem_limit_bytes=VMEM_LIMIT),
         cost_estimate=pl.CostEstimate(
-            flops=2 * total * features * features * blocks,
-            bytes_accessed=2 * blocks * features * (features + total), transcendentals=0),
-    )(left, right)
+            flops=4 * total * features * wide, bytes_accessed=4 * wide * (features + total), transcendentals=0),
+    )(active, grad_ffn, hidden, grad_raised)
 
 
 TILE = 16
+WAIT_FOR = 2
 
 
 def swap_core(a):
@@ -609,9 +675,10 @@
     place = lax.axis_index("fsdp") // 2
     steps = [k for d in range(1, places) for k in (d, -d)]
     seen = {-k: along_line(mine, k) for k in steps}
+    near = min(WAIT_FOR, places - 1)
+    seen[near], seen[-near], *others = lax.optimization_barrier((seen[near], seen[-near], *others))
     line = jnp.stack([seen[k] for k in range(1 - places, places) if k])
     line = lax.dynamic_slice_in_dim(line, places - 1 - place, places - 1, 0)
-    line, *others = lax.optimization_barrier((line, *others))
     every = gather_rep(line)
     at = jnp.arange(places)[:, None, None, None]
     every = every.swapaxes(0, 1)
@@ -619,8 +686,7 @@
     behind = jnp.pad(every, ((1, 0), (0, 0), (0, 0), (0, 0)))
     every = jnp.where(at == place, shard[None], jnp.where(at < place, before, behind))
     other = swap_core(every)
-    first = lax.axis_index("fsdp") % 2 == 0
-    return jnp.stack([jnp.where(first, every, other), jnp.where(first, other, every)], axis=1), others
+    return every, other, others
 
 
 def summed_over(a):
@@ -656,18 +722,25 @@
         rel_table.reshape(reps, table_cut, features),
         spread(vectors, reps)], axis=1)
     mine = lax.dynamic_index_in_dim(shard, lax.axis_index("rep"), 0, keepdims=False)
-    first, (w_up, w_down) = gather_parts(mine, shard, w_up, w_down)
+    own, other, (w_up, w_down) = gather_parts(mine, shard, w_up, w_down)
     w_u = lax.all_gather(w_up, "fsdp", axis=0, tiled=True)
     w_d = lax.all_gather(w_down, "fsdp", axis=0, tiled=True)
     direct = unit if unit == cut and cut % TILE == 0 and table_cut % TILE == 0 else 0
     part = unit + table_cut + vector_rows
+    core = lax.axis_index("fsdp") % 2
+    first = jnp.stack([jnp.where(core == 0, own, other), jnp.where(core == 0, other, own)], axis=1)
     if direct:
-        view = (first, (places, 2), cut, first, (places, 2, reps, table_cut, features), (0, 0, 0, unit // table_cut, 0))
+        view = (own, other, cut, own, other, (places, reps, table_cut, features), (0, 0, unit // table_cut, 0))
     else:
         four = first[:, :, :, :unit].reshape(fs, 4, reps // 4, unit, features).transpose(1, 0, 2, 3, 4)
-        rel = first[:, :, :, unit : unit + table_cut].reshape(1, 1, 1, -1, features)
-        view = (four.reshape(1, 1, 4, features, features), (1, 1), features, rel, rel.shape, (0,) * 5)
-    wide = first[:, :, 0, unit + table_cut : unit + table_cut + vector_count, :cut].reshape(fs, vector_count, cut)
+        four = four.reshape(1, 4, features, features)
+        rel = first[:, :, :, unit : unit + table_cut].reshape(1, 1, -1, features)
+        view = (four, four, features, rel, rel, rel.shape, (0,) * 4)
+    vector_at = slice(unit + table_cut, unit + table_cut + vector_count)
+    wide = [a[:, 0, vector_at, :cut] for a in (own, other)]
+    wide = jnp.stack([jnp.where(core == 0, *wide), jnp.where(core == 0, *wide[::-1])], axis=1)
+    wide = wide.reshape(fs, vector_count, cut)
+    core = core.reshape(1)
     wide = wide.transpose(1, 0, 2).astype(f32)
     v_up = wide[vector_count - up_parts :].transpose(1, 0, 2).reshape(1, -1)
     wide = wide.reshape(vector_count, features)
@@ -678,22 +751,21 @@
     flat_bound, flat_lengths = boundary.reshape(-1), lengths.reshape(-1)
     flat_tokens, flat_grad = tokens.reshape(rows, features), out_grad.reshape(rows, features)
     queries, keys, values, key_rows, query_rows, key_back_t, query_t, summed_low = project(
-        flat_bound, flat_tokens, view, jnp.asarray(pick, bf), jnp.asarray(pick.T, bf), jnp.asarray(pick_back.T, bf),
+        flat_bound, core, flat_tokens, view, jnp.asarray(pick, bf), jnp.asarray(pick.T, bf), jnp.asarray(pick_back.T, bf),
         wide, wide[9:11], seq_len)
     context_t, probs, inverse_total = attn_fwd(
         queries, keys, values, key_back_t, query_t, flat_lengths, heads)
     (layer_out, hidden_low, active, grad_ffn, grad_raised, grad_first, grad_attended, grad_context_t,
-     sums, sum_up) = ffn(flat_bound, context_t, flat_tokens, flat_grad, view, w_u, w_d, wide, v_up, seq_len)
-    d_down = outer(active, grad_ffn, True).reshape(-1, features)
-    s_down = lax.psum_scatter(d_down, "fsdp", scatter_dimension=0, tiled=True)
-    s_up = lax.psum_scatter(outer(hidden_low, grad_raised, False), "fsdp", scatter_dimension=1, tiled=True)
+     sums, sum_up) = ffn(flat_bound, core, context_t, flat_tokens, flat_grad, view, w_u, w_d, wide, v_up, seq_len)
+    d_ffn = outer(active, grad_ffn, hidden_low, grad_raised, fs)
+    early = lax.psum_scatter(d_ffn.reshape(-1, features, features), "fsdp", scatter_dimension=1, tiled=True)
     d_query, d_key, d_value, key_off, query_off = attn_bwd(
         queries, keys, values, grad_context_t, probs, inverse_total, key_rows, query_rows)
-    core = lax.axis_index("fsdp") % 2
-    *made, tokens_grad = unproject(
-        flat_bound, core.reshape(1), summed_low, d_query, d_key, d_value, key_off, query_off, view,
-        jnp.asarray(pick.T, bf), grad_first, context_t, grad_attended, sums, sum_up, seq_len, direct,
+    made = unproject(
+        flat_bound, core, summed_low, d_query, d_key, d_value, key_off, query_off, view,
+        jnp.asarray(pick.T, bf), context_t, grad_attended, sums, sum_up, seq_len, direct,
         (reps, places, part, features))
+    tokens_grad = token_grads(core, d_query, d_key, d_value, view, grad_first)
     if direct:
         keep, give = made
     else:
@@ -703,11 +775,10 @@
         last = jnp.concatenate([
             four.reshape(reps, places, 2, unit, features),
             d_rel.reshape(places, 2, reps, table_cut, features).transpose(2, 0, 1, 3, 4), small], axis=3)
-        keep = lax.dynamic_index_in_dim(last, core, 2, keepdims=False)
-        give = lax.dynamic_index_in_dim(last, 1 - core, 2, keepdims=False)
+        keep = lax.dynamic_index_in_dim(last, core[0], 2, keepdims=False)
+        give = lax.dynamic_index_in_dim(last, 1 - core[0], 2, keepdims=False)
     last = (keep.astype(f32) + swap_core(give).astype(f32)).astype(bf)
-    early = jnp.concatenate([s_down, s_up.reshape(-1, features)])
-    early = lax.psum_scatter(early, "rep", scatter_dimension=0, tiled=True)
+    early = lax.psum_scatter(early.reshape(-1, features), "rep", scatter_dimension=0, tiled=True)
     last = summed_over(swap_rep(last))
     early = after(early, last)
     early = lax.all_gather(early, "rep", axis=0, tiled=True)

time: 396 us -> 384 us (0.970)
  other arithmetic: 25.8 us -> 12.2 us
  starting transfers between devices: 32.2 us -> 36.4 us
  waiting for transfers between devices: 129 us -> 125 us
    ppermute x6, waiting for transfers between devices: 16.3 us -> 27.1 us  [along_line(): lax.ppermute(a, 'fsdp', [(i, i + 2 * step) for i in range(n) if 0 <= i +...]
    another operation x3 -> x1, other arithmetic: 9.06 us -> 0.01 us  [per_device(): jnp.stack([jnp.where(core == 0, *wide), jnp.where(core == 0, *wide[::-1])...]
    all_to_all x1, waiting for transfers between devices: 14.3 us -> 6.08 us  [swap_line(): return lax.all_to_all(a, 'fsdp', 0, 0, tiled=True, axis_index_groups=groups)]
    all_gather x1, waiting for transfers between devices: 10.8 us -> 2.6 us  [per_device(): w_d = lax.all_gather(w_down, 'fsdp', axis=0, tiled=True)]
    pallas_call x2, Pallas kernels: 18.8 us -> 24.9 us  [the longest x1 16.6 us: outer(): pl.pallas_call(outer_kernel, grid=(2 * blocks,), in_specs=[pl.BlockSpec((...]
    pallas_call x1, Pallas kernels: 23.6 us -> 19.4 us  [unproject(): pl.pallas_call(lambda *refs: unproject_kernel(*refs, seq_len=seq_len, dir...]
    reduce_scatter x3 -> x2, waiting for transfers between devices: 15.4 us -> 19.6 us  [the longest x1 14.1 us: per_device(): lax.psum_scatter(d_ffn.reshape(-1, features, features), 'fsdp', scatter_d...]
  transfers between devices with their start and end apart: 21 -> 20, of which waited for: 15 -> 16; matrix products, arithmetic and copies ran while one was open for 7% -> 4% of each run, Pallas kernels for 33% -> 32%
where the time goes in v4:
time: 384 us; the launch traced here: 383 us
  Pallas kernels  184 us (48%)
  waiting for transfers between devices  125 us (33%)
  starting transfers between devices  36.4 us (9%)
  between operations  14.2 us (4%)
  other arithmetic  12.2 us (3%)
  local copies, waits for them, and re-layouts  12.1 us (3%)
    pallas_call x1, Pallas kernels, attn_bwd(): pl.pallas_call(attn_bwd_kernel, grid=(NP, M), in_specs=[tok(0), tok(0), t...  50.6 us
    pallas_call x1, Pallas kernels, ffn(): pl.pallas_call(lambda *refs: ffn_kernel(*refs, seq_len=seq_len), grid_spe...  42.6 us
    all_to_all x2, waiting for transfers between devices, swap_rep(): return lax.all_to_all(a, 'rep', 0, 0, tiled=True)  42.5 us
    pallas_call x1, Pallas kernels, attn_fwd(): pl.pallas_call(attn_fwd_kernel, grid_spec=pltpu.PrefetchScalarGridSpec(nu...  31.5 us
    ppermute x6, waiting for transfers between devices, along_line(): lax.ppermute(a, 'fsdp', [(i, i + 2 * step) for i in range(n) if 0 <= i +...  27.1 us
    pallas_call x1, Pallas kernels, unproject(): pl.pallas_call(lambda *refs: unproject_kernel(*refs, seq_len=seq_len, dir...  19.4 us
    ppermute x6, starting transfers between devices, along_line(): lax.ppermute(a, 'fsdp', [(i, i + 2 * step) for i in range(n) if 0 <= i +...  18.5 us
    pallas_call x1, Pallas kernels, outer(): pl.pallas_call(outer_kernel, grid=(2 * blocks,), in_specs=[pl.BlockSpec((...  16.6 us
  transfers between devices with their start and end apart: 20, of which 16 were waited for; matrix products, arithmetic and copies ran while one was open for 4% of the time, Pallas kernels for 32%

profile of v4, /device:TPU:0, one launch (start us, length us, event | category | flops | bytes accessed | tf_op | source)
XLA Modules:
  0.0 383.4 jit_solution(4250628888193707323)
XLA Ops:
  13.1 6.0 %collective-permute-start.2 = (bf16[128,768]{1,0:T(8,128)(2,1)S(1)}, bf16[128,768]{1,0:T(8,128)(2,1)S(1)}, u32[]{:S(2)}, u32[]{:S(2)}) collective-permute-start(bf16[128,768]{1,0:T(8,128)(2,1)S(1)} %dynamic-slice_bitcast_fusion.2), channel_id=1, source_target_pairs={{0,4},{1,5},{2,6},{3,7},{8,12},{9,13},{10,14},{11,15},{16,20},{17,... | collective-permute-start | bytes 589832 | tf_op jit(solution)/shard_map/ppermute | solution.py:633
  19.1 7.2 %collective-permute-done.1 = bf16[128,768]{1,0:T(8,128)(2,1)S(1)} collective-permute-done((bf16[128,768]{1,0:T(8,128)(2,1)S(1)}, bf16[128,768]{1,0:T(8,128)(2,1)S(1)}, u32[]{:S(2)}, u32[]{:S(2)}) %collective-permute-start.1) | collective-permute-done | bytes 196640 | tf_op jit(solution)/shard_map/ppermute | solution.py:633
  26.3 7.4 %collective-permute-start = (bf16[128,768]{1,0:T(8,128)(2,1)S(1)}, bf16[128,768]{1,0:T(8,128)(2,1)S(1)}, u32[]{:S(2)}, u32[]{:S(2)}) collective-permute-start(bf16[128,768]{1,0:T(8,128)(2,1)S(1)} %dynamic-slice_bitcast_fusion.2), channel_id=1, source_target_pairs={{0,6},{1,7},{8,14},{9,15},{16,22},{17,23},{24,30},{25,31}} | collective-permute-start | bytes 589832 | tf_op jit(solution)/shard_map/ppermute | solution.py:633
  37.6 1.7 collective-permute-done
  39.4 7.5 %collective-permute-done.3 = bf16[128,768]{1,0:T(8,128)(2,1)S(1)} collective-permute-done((bf16[128,768]{1,0:T(8,128)(2,1)S(1)}, bf16[128,768]{1,0:T(8,128)(2,1)S(1)}, u32[]{:S(2)}, u32[]{:S(2)}) %collective-permute-start.3) | collective-permute-done | bytes 196640 | tf_op jit(solution)/shard_map/ppermute | solution.py:633
  46.9 10.8 %collective-permute-done.4 = bf16[128,768]{1,0:T(8,128)(2,1)S(1)} collective-permute-done((bf16[128,768]{1,0:T(8,128)(2,1)S(1)}, bf16[128,768]{1,0:T(8,128)(2,1)S(1)}, u32[]{:S(2)}, u32[]{:S(2)}) %collective-permute-start.4) | collective-permute-done | bytes 196640 | tf_op jit(solution)/shard_map/ppermute | solution.py:633
  57.8 2.5 collective-permute-start.8
  61.9 3.0 collective-permute-done.8
  65.1 2.5 collective-permute-start.9
  67.6 2.7 collective-permute-done.6
  70.5 8.7 %collective-permute-done.9 = bf16[2,3,128,384]{3,2,0,1:T(8,128)(2,1)S(1)} collective-permute-done((bf16[2,3,128,384]{3,2,0,1:T(8,128)(2,1)S(1)}, bf16[2,3,128,384]{3,2,0,1:T(8,128)(2,1)S(1)}, u32[]{:S(2)}, u32[]{:S(2)}) %collective-permute-start.9) | collective-permute-done | bytes 589856 | tf_op jit(solution)/shard_map/ppermute | solution.py:641
  82.2 5.8 %collective-permute-done.10.refs_4_.refs_6_.refs_8_.refs_10_.w_q2_ref.w_k2_ref.w_v2_ref.refs_9_.refs_11_.refs_13_.refs_15_ = bf16[4,4,128,768]{3,2,1,0:T(8,128)(2,1)} collective-permute-done((bf16[4,4,128,768]{3,2,1,0:T(8,128)(2,1)S(1)}, bf16[4,4,128,768]{3,2,1,0:T(8,128)(2,1)}, u32[]{:S(2)}, u32[]{:S(2)}) %collective-permute-start.10) | collective-permute-done | bytes 3145760 | tf_op jit(solution)/shard_map/ppermute | solution.py:622
  90.8 14.9 %shard_map.401 = (bf16[1024,768]{1,0:T(8,128)(2,1)}, bf16[1024,768]{1,0:T(8,128)(2,1)}, bf16[1024,768]{1,0:T(8,128)(2,1)}, bf16[1024,768]{1,0:T(8,128)(2,1)}, bf...) custom-call(s32[2]{0:T(128)} %bitcast.108, ...), custom_call_target="tpu_custom_call" | custom-call | flops 7247757312 | bytes 16121856 | tf_op jit(solution)/shard_map/pallas_call | solution.py:295
  105.7 31.5 %shard_map.402 = (bf16[768,1024]{1,0:T(8,128)(2,1)}, bf16[2,12,512,512]{3,2,1,0:T(8,128)(2,1)}, f32[2,6,2,512]{3,2,1,0:T(2,128)}) custom-call(s32[2]{0:T(128)} %bitcast.121, bf16[1024,768]{1,0:T(8,128)(2,1)} %get-tuple-element.55.q_ref, bf16[1024,768]{1,0:T(8,128)(2,1)} %get-tuple-element.56.k_ref, bf16[1024,768]{1,0:T(8,128)(2,1)} %get-tuple-element.57.v_ref, ...), custom_call_target="tpu_custom_call" | custom-call | flops 9663676416 | bytes 12582912 | tf_op jit(solution)/shard_map/pallas_call | solution.py:86
  137.2 2.6 all-gather.6.cloned.1.call-done.refs_8_
  139.8 42.6 %shard_map.403 = (bf16[1024,768]{1,0:T(8,128)(2,1)}, bf16[1024,768]{1,0:T(8,128)(2,1)}, bf16[1024,3072]{1,0:T(8,128)(2,1)}, bf16[1024,768]{1,0:T(8,128)(2,1)}, b...) custom-call(s32[2]{0:T(128)} %bitcast.109, ...), custom_call_target="tpu_custom_call" | custom-call | flops 21743271936 | bytes 34603008 | tf_op jit(solution)/shard_map/pallas_call | solution.py:548
  182.5 16.6 %shard_map.407 = bf16[8,8,96,768]{3,2,1,0:T(8,128)(2,1)} custom-call(bf16[1024,3072]{1,0:T(8,128)(2,1)} %get-tuple-element.81.active_ref, bf16[1024,768]{1,0:T(8,128)(2,1)} %get-tuple-element.82.grad_ffn_ref, bf16[1024,768]{1,0:T(8,128)(2,1)} %get-tuple-element.83.hidden_ref, bf16[1024,3072]{1,0:T(8,128)(2,1)} %get-tuple-element.84.grad_raised_ref), custom_call_target="tpu_custom_call" | custom-call | flops 9663676416 | bytes 22020096 | tf_op jit(solution)/shard_map/pallas_call | solution.py:602
  199.1 50.6 %shard_map.404 = (bf16[1024,768]{1,0:T(8,128)(2,1)}, bf16[1024,768]{1,0:T(8,128)(2,1)}, bf16[1024,768]{1,0:T(8,128)(2,1)}, bf16[768,1024]{1,0:T(8,128)(2,1)}, bf16[768,1024]{1,0:T(8,128)(2,1)}) custom-call(bf16[1024,768]{1,0:T(8,128)(2,1)} %get-tuple-element.55.q_ref, bf16[1024,768]{1,0:T(8,128)(2,1)} %get-tuple-element.56.k_ref, ...), custom_call_target="tpu_custom_call" | custom-call | flops 19327352832 | bytes 12582912 | tf_op jit(solution)/shard_map/pallas_call | solution.py:187
  249.7 19.4 %shard_map.406 = (bf16[4,4,128,768]{3,2,1,0:T(8,128)(2,1)}, bf16[4,4,128,768]{3,2,1,0:T(8,128)(2,1)}) custom-call(s32[2]{0:T(128)} %bitcast.110, s32[1]{0:T(128)} %bitcast.1.refs_1_.core_ref, bf16[1024,768]{1,0:T(8,128)(2,1)} %get-tuple-element.73.refs_2_, bf16[1024,768]{1,0:T(8,128)(2,1)} %get-tuple-element.69.dq_ref.refs_3_, ...), custom_call_target="tpu_custom_call" | custom-call | flops 10468982784 | bytes 23986176 | tf_op jit(solution)/shard_map/pallas_call | solution.py:415
  269.4 5.6 %collective-permute-done.11 = bf16[4,4,128,768]{3,2,1,0:T(8,128)(2,1)S(1)} collective-permute-done((bf16[4,4,128,768]{3,2,1,0:T(8,128)(2,1)}, bf16[4,4,128,768]{3,2,1,0:T(8,128)(2,1)S(1)}, u32[]{:S(2)}, u32[]{:S(2)}) %collective-permute-start.11) | collective-permute-done | bytes 3145760 | tf_op jit(solution)/shard_map/ppermute | solution.py:622
  275.0 4.6 %add_convert_fusion = bf16[4,4,128,768]{3,2,1,0:T(8,128)(2,1)} fusion(bf16[4,4,128,768]{3,2,1,0:T(8,128)(2,1)S(1)} %collective-permute-done.11, bf16[4,4,128,768]{3,2,1,0:T(8,128)(2,1)} %get-tuple-element.79), kind=kLoop, calls=%fused_computation | loop fusion | flops 6291456 | bytes 9437184 | tf_op jit(solution)/shard_map/convert_element_type | solution.py:780
  279.7 3.7 all-to-all-start
  283.5 14.1 %reduce-scatter.3.cloned.1.call-done = bf16[8,96,768]{2,1,0:T(8,128)(2,1)} async-done(((bf16[8,768,768]{2,1,0:T(8,128)(2,1)}), bf16[8,96,768]{2,1,0:T(8,128)(2,1)}) %reduce-scatter.3.cloned.1.call-update) | async-done | bytes 1179664 | tf_op jit(solution)/shard_map/reduce_scatter | solution.py:761
  297.6 28.8 %all-to-all-done = bf16[4,4,128,768]{3,2,1,0:T(8,128)(2,1)S(1)} async-done(((bf16[4,4,128,768]{3,2,1,0:T(8,128)(2,1)}), bf16[4,4,128,768]{3,2,1,0:T(8,128)(2,1)S(1)}, u32[]{:S(2)}, u32[]{:S(2)}) %all-to-all-start) | async-done | bytes 3145760 | tf_op jit(solution)/shard_map/all_to_all | solution.py:637
  326.4 1.6 reduce_sum.24
  328.0 3.5 all-to-all-start.1
  331.6 5.4 %reduce-scatter.5.cloned.1.call-done = bf16[192,768]{1,0:T(8,128)(2,1)} async-done(((bf16[768,768]{1,0:T(8,128)(2,1)}), bf16[192,768]{1,0:T(8,128)(2,1)}) %reduce-scatter.5.cloned.1.call-update) | async-done | bytes 294928 | tf_op jit(solution)/shard_map/reduce_scatter | solution.py:781
  337.1 8.2 %shard_map.405 = bf16[1024,768]{1,0:T(8,128)(2,1)} custom-call(s32[1]{0:T(128)} %bitcast.1.refs_1_.core_ref, bf16[1024,768]{1,0:T(8,128)(2,1)} %get-tuple-element.69.dq_ref.refs_3_, bf16[1024,768]{1,0:T(8,128)(2,1)} %get-tuple-element.70.dk_ref.refs_4_, bf16[1024,768]{1,0:T(8,128)(2,1)} %get-tuple-element.71.dv_ref.refs_5_, ...), custom_call_target="tpu_custom_call" | custom-call | flops 3623878656 | bytes 12976128 | tf_op jit(solution)/shard_map/pallas_call | solution.py:448
  345.3 6.1 %all-to-all-done.1 = bf16[4,128,768]{2,1,0:T(8,128)(2,1)S(1)} async-done(((bf16[4,128,768]{2,1,0:T(8,128)(2,1)}), bf16[4,128,768]{2,1,0:T(8,128)(2,1)S(1)}, u32[]{:S(2)}, u32[]{:S(2)}) %all-to-all-start.1) | async-done | bytes 786464 | tf_op jit(solution)/shard_map/all_to_all | solution.py:628
  352.4 3.5 all-to-all-start.2
  357.8 13.7 %all-to-all-done.2 = bf16[4,112,768]{2,1,0:T(8,128)(2,1)S(1)} async-done(((bf16[4,112,768]{2,1,0:T(8,128)(2,1)}), bf16[4,112,768]{2,1,0:T(8,128)(2,1)S(1)}, u32[]{:S(2)}, u32[]{:S(2)}) %all-to-all-start.2) | async-done | bytes 688160 | tf_op jit(solution)/shard_map/all_to_all | solution.py:637
  373.3 2.4 slice_convert_fusion
  (77 shorter events, 24.1 us)
Async XLA Ops:
  7.2 130.0 %all-gather.4.cloned.1.call-start = ((), (), s32[]{:S(2)}) async-start(), calls=%async_computation.5 | async-start | bytes 5308416 | tf_op jit(solution)/shard_map/all_gather | solution.py:726
  10.9 0.9 copy-start.1
  11.8 14.4 %collective-permute-start.1 = (bf16[128,768]{1,0:T(8,128)(2,1)S(1)}, bf16[128,768]{1,0:T(8,128)(2,1)S(1)}, u32[]{:S(2)}, u32[]{:S(2)}) collective-permute-start(bf16[128,768]{1,0:T(8,128)(2,1)S(1)} %dynamic-slice_bitcast_fusion.2), channel_id=1, source_target_pairs={{4,0},{5,1},{6,2},{7,3},{12,8},{13,9},{14,10},{15,11},{20,16},{21,... | collective-permute-start | bytes 589832 | tf_op jit(solution)/shard_map/ppermute | solution.py:633
  13.1 13.1 %collective-permute-start.2 = (bf16[128,768]{1,0:T(8,128)(2,1)S(1)}, bf16[128,768]{1,0:T(8,128)(2,1)S(1)}, u32[]{:S(2)}, u32[]{:S(2)}) collective-permute-start(bf16[128,768]{1,0:T(8,128)(2,1)S(1)} %dynamic-slice_bitcast_fusion.2), channel_id=1, source_target_pairs={{0,4},{1,5},{2,6},{3,7},{8,12},{9,13},{10,14},{11,15},{16,20},{17,... | collective-permute-start | bytes 589832 | tf_op jit(solution)/shard_map/ppermute | solution.py:633
  26.2 113.6 %all-gather.6.cloned.1.call-start = ((), (), s32[]{:S(2)}) async-start(), calls=%async_computation.6 | async-start | bytes 5308416 | tf_op jit(solution)/shard_map/all_gather | solution.py:727
  26.3 13.0 %collective-permute-start = (bf16[128,768]{1,0:T(8,128)(2,1)S(1)}, bf16[128,768]{1,0:T(8,128)(2,1)S(1)}, u32[]{:S(2)}, u32[]{:S(2)}) collective-permute-start(bf16[128,768]{1,0:T(8,128)(2,1)S(1)} %dynamic-slice_bitcast_fusion.2), channel_id=1, source_target_pairs={{0,6},{1,7},{8,14},{9,15},{16,22},{17,23},{24,30},{25,31}} | collective-permute-start | bytes 589832 | tf_op jit(solution)/shard_map/ppermute | solution.py:633
  33.7 13.2 %collective-permute-start.3 = (bf16[128,768]{1,0:T(8,128)(2,1)S(1)}, bf16[128,768]{1,0:T(8,128)(2,1)S(1)}, u32[]{:S(2)}, u32[]{:S(2)}) collective-permute-start(bf16[128,768]{1,0:T(8,128)(2,1)S(1)} %dynamic-slice_bitcast_fusion.2), channel_id=1, source_target_pairs={{0,2},{1,3},{2,4},{3,5},{4,6},{5,7},{8,10},{9,11},{10,12},{11,13},... | collective-permute-start | bytes 589832 | tf_op jit(solution)/shard_map/ppermute | solution.py:633
  35.0 22.7 %collective-permute-start.4 = (bf16[128,768]{1,0:T(8,128)(2,1)S(1)}, bf16[128,768]{1,0:T(8,128)(2,1)S(1)}, u32[]{:S(2)}, u32[]{:S(2)}) collective-permute-start(bf16[128,768]{1,0:T(8,128)(2,1)S(1)} %dynamic-slice_bitcast_fusion.2), channel_id=1, source_target_pairs={{2,0},{3,1},{4,2},{5,3},{6,4},{7,5},{10,8},{11,9},{12,10},{13,11},... | collective-permute-start | bytes 589832 | tf_op jit(solution)/shard_map/ppermute | solution.py:633
  36.3 21.4 %collective-permute-start.5 = (bf16[128,768]{1,0:T(8,128)(2,1)S(1)}, bf16[128,768]{1,0:T(8,128)(2,1)S(1)}, u32[]{:S(2)}, u32[]{:S(2)}) collective-permute-start(bf16[128,768]{1,0:T(8,128)(2,1)S(1)} %dynamic-slice_bitcast_fusion.2), channel_id=1, source_target_pairs={{6,0},{7,1},{14,8},{15,9},{22,16},{23,17},{30,24},{31,25}} | collective-permute-start | bytes 589832 | tf_op jit(solution)/shard_map/ppermute | solution.py:633
  57.8 7.2 %collective-permute-start.8 = (bf16[1,3,128,384]{3,2,0,1:T(8,128)(2,1)S(1)}, bf16[1,3,128,384]{3,2,0,1:T(8,128)(2,1)S(1)}, u32[]{:S(2)}, u32[]{:S(2)}) collective-permute-start(bf16[1,3,128,384]{3,2,0,1:T(8,128)(2,1)S(1)} %get-tuple-element.137), channel_id=1, source_target_pairs={{0,16},{8,24},{16,0},{24,8},{1,17},{9,25},{17,1},{25,9},{2,18},{10... | collective-permute-start | bytes 884744 | tf_op jit(solution)/shard_map/ppermute | solution.py:641
  60.3 237.3 %reduce-scatter.3.cloned.1.call-start = ((), (), s32[]{:S(2)}) async-start(), calls=%async_computation.7 | async-start | bytes 10616832 | tf_op jit(solution)/shard_map/reduce_scatter | solution.py:761
  60.4 9.9 %collective-permute-start.6 = (bf16[1,3,128,384]{3,2,1,0:T(8,128)(2,1)S(1)}, bf16[1,3,128,384]{3,2,1,0:T(8,128)(2,1)S(1)}, u32[]{:S(2)}, u32[]{:S(2)}) collective-permute-start(bf16[1,3,128,384]{3,2,1,0:T(8,128)(2,1)S(1)} %get-tuple-element.136), channel_id=1, source_target_pairs={{0,8},{8,0},{16,24},{24,16},{1,9},{9,1},{17,25},{25,17},{2,10},{10... | collective-permute-start | bytes 884744 | tf_op jit(solution)/shard_map/ppermute | solution.py:641
  65.1 14.1 %collective-permute-start.9 = (bf16[2,3,128,384]{3,2,0,1:T(8,128)(2,1)S(1)}, bf16[2,3,128,384]{3,2,0,1:T(8,128)(2,1)S(1)}, u32[]{:S(2)}, u32[]{:S(2)}) collective-permute-start(bf16[2,3,128,384]{3,2,0,1:T(8,128)(2,1)S(1)} %pad_maximum_fusion.3), channel_id=1, source_target_pairs={{0,8},{8,0},{16,24},{24,16},{1,9},{9,1},{17,25},{25,17},{2,10},{10... | collective-permute-start | bytes 1769480 | tf_op jit(solution)/shard_map/ppermute | solution.py:641
  70.4 9.9 %collective-permute-start.7 = (bf16[2,3,128,384]{3,2,1,0:T(8,128)(2,1)S(1)}, bf16[2,3,128,384]{3,2,1,0:T(8,128)(2,1)S(1)}, u32[]{:S(2)}, u32[]{:S(2)}) collective-permute-start(bf16[2,3,128,384]{3,2,1,0:T(8,128)(2,1)S(1)} %pad_maximum_fusion.2), channel_id=1, source_target_pairs={{0,16},{8,24},{16,0},{24,8},{1,17},{9,25},{17,1},{25,9},{2,18},{10... | collective-permute-start | bytes 1769480 | tf_op jit(solution)/shard_map/ppermute | solution.py:641
  80.5 1.1 copy-start.2
  82.1 5.9 %copy-start = (bf16[4,4,128,768]{3,2,1,0:T(8,128)(2,1)}, bf16[4,4,128,768]{3,2,1,0:T(8,128)(2,1)S(1)}, u32[]{:S(2)}) copy-start(bf16[4,4,128,768]{3,2,1,0:T(8,128)(2,1)S(1)} %select_select_fusion.refs_3_.refs_5_.refs_7_.refs_9_.w_q_ref.w_k_ref.w_v_ref.refs_8_.refs_10_.refs_12_.refs_14_) | copy-start | bytes 9437188
  82.1 5.9 %collective-permute-start.10 = (bf16[4,4,128,768]{3,2,1,0:T(8,128)(2,1)S(1)}, bf16[4,4,128,768]{3,2,1,0:T(8,128)(2,1)}, u32[]{:S(2)}, u32[]{:S(2)}) collective-permute-start(bf16[4,4,128,768]{3,2,1,0:T(8,128)(2,1)S(1)} %select_select_fusion.refs_3_.refs_5_.refs_7_.refs_9_.w_q_ref.w_k_ref.w_v_ref.refs_8_.refs_, ...), channel_id=1, source_target_pairs={{0,1},{1,0},{2,3},{3,2},{4,5},{5,4},{6,7},{7,6},{8,9},{9,8},{10,11... | collective-permute-start | bytes 9437192 | tf_op jit(solution)/shard_map/ppermute | solution.py:622
  269.1 5.9 %collective-permute-start.11 = (bf16[4,4,128,768]{3,2,1,0:T(8,128)(2,1)}, bf16[4,4,128,768]{3,2,1,0:T(8,128)(2,1)S(1)}, u32[]{:S(2)}, u32[]{:S(2)}) collective-permute-start(bf16[4,4,128,768]{3,2,1,0:T(8,128)(2,1)} %get-tuple-element.80), channel_id=1, source_target_pairs={{0,1},{1,0},{2,3},{3,2},{4,5},{5,4},{6,7},{7,6},{8,9},{9,8},{10,11... | collective-permute-start | bytes 9437192 | tf_op jit(solution)/shard_map/ppermute | solution.py:622
  279.7 46.7 %all-to-all-start = ((bf16[4,4,128,768]{3,2,1,0:T(8,128)(2,1)}), bf16[4,4,128,768]{3,2,1,0:T(8,128)(2,1)S(1)}, u32[]{:S(2)}, u32[]{:S(2)}) async-start(bf16[4,4,128,768]{3,2,1,0:T(8,128)(2,1)} %add_convert_fusion), calls=%async_computation | async-start | bytes 6291456 | tf_op jit(solution)/shard_map/all_to_all | solution.py:637
  283.4 53.6 %reduce-scatter.5.cloned.1.call-start = ((), (), s32[]{:S(2)}) async-start(), calls=%async_computation.8 | async-start | bytes 1474560 | tf_op jit(solution)/shard_map/reduce_scatter | solution.py:781
  328.0 23.4 %all-to-all-start.1 = ((bf16[4,128,768]{2,1,0:T(8,128)(2,1)}), bf16[4,128,768]{2,1,0:T(8,128)(2,1)S(1)}, u32[]{:S(2)}, u32[]{:S(2)}) async-start(bf16[4,128,768]{2,1,0:T(8,128)(2,1)} %reduce_sum.24), calls=%async_computation.1 | async-start | bytes 1572864 | tf_op jit(solution)/shard_map/all_to_all | solution.py:628
  331.5 41.7 %all-gather.8.cloned.1.call-start = ((), (), s32[]{:S(2)}) async-start(), calls=%async_computation.9 | async-start | bytes 1474560 | tf_op jit(solution)/shard_map/all_gather | solution.py:784
  352.4 19.0 %all-to-all-start.2 = ((bf16[4,112,768]{2,1,0:T(8,128)(2,1)}), bf16[4,112,768]{2,1,0:T(8,128)(2,1)S(1)}, u32[]{:S(2)}, u32[]{:S(2)}) async-start(bf16[4,112,768]{2,1,0:T(8,128)(2,1)} %broadcast_in_dim.50), calls=%async_computation.2 | async-start | bytes 1376256 | tf_op jit(solution)/shard_map/all_to_all | solution.py:637
Sparse Core Ops, SparseCore 0:
  26.4 61.9 all-gather.3
  90.0 49.7 all-gather.5
  199.2 98.2 reduce-scatter.2
  300.3 36.6 reduce-scatter.4
  338.7 32.9 all-gather.7

commit v5 on v4

--- a/solution.py
+++ b/solution.py
@@ -363,12 +363,12 @@
     second = second_rows(bound_ref, rows, seq_len)
     for values, weight in ((dq, w_q), (dk, w_k), (dv, w_v)):
         wide = values.astype(f32)
-        parts = jnp.concatenate([total(jnp.where(second, 0.0, wide)), total(jnp.where(second, wide, 0.0))])
+        row = lax.broadcasted_iota(jnp.int32, (16, wide.shape[1]), 0)
+        parts = jnp.where(row == 0, total(jnp.where(second, 0.0, wide)), 0.0)
+        parts = jnp.where(row == 1, total(jnp.where(second, wide, 0.0)), parts)
         high = parts.astype(bf)
-        low_part = (parts - high.astype(f32)).astype(bf)
-        stacked = jnp.concatenate([high, low_part, jnp.zeros((12, parts.shape[1]), bf)])
-        product = nt(stacked, weight)
-        small_ref[9:11, :] += product[0:2] + product[2:4]
+        product = nt(high, weight) + nt((parts - high.astype(f32)).astype(bf), weight)
+        small_ref[9:11, :] += product[0:2]
     rel_sum_ref[...] += nt(low_key, w_k) + nt(low_query, w_q)
 
     @pl.when(step == pl.num_programs(0) - 1)

time: 384 us -> 385 us (level)
  transfers between devices with their start and end apart: 20 -> 20, of which waited for: 16 -> 16; matrix products, arithmetic and copies ran while one was open for 4% -> 4% of each run, Pallas kernels for 32% -> 33%
where the time goes in v5:
time: 385 us; the launch traced here: 384 us
  Pallas kernels  185 us (48%)
  waiting for transfers between devices  125 us (32%)
  starting transfers between devices  36.4 us (9%)
  between operations  14.2 us (4%)
  other arithmetic  12.2 us (3%)
  local copies, waits for them, and re-layouts  12.1 us (3%)
    pallas_call x1, Pallas kernels, attn_bwd(): pl.pallas_call(attn_bwd_kernel, grid=(NP, M), in_specs=[tok(0), tok(0), t...  50.6 us
    all_to_all x2, waiting for transfers between devices, swap_rep(): return lax.all_to_all(a, 'rep', 0, 0, tiled=True)  43.3 us
    pallas_call x1, Pallas kernels, ffn(): pl.pallas_call(lambda *refs: ffn_kernel(*refs, seq_len=seq_len), grid_spe...  42.6 us
    pallas_call x1, Pallas kernels, attn_fwd(): pl.pallas_call(attn_fwd_kernel, grid_spec=pltpu.PrefetchScalarGridSpec(nu...  31.5 us
    ppermute x6, waiting for transfers between devices, along_line(): lax.ppermute(a, 'fsdp', [(i, i + 2 * step) for i in range(n) if 0 <= i +...  27.1 us
    pallas_call x1, Pallas kernels, unproject(): pl.pallas_call(lambda *refs: unproject_kernel(*refs, seq_len=seq_len, dir...  20.2 us
    ppermute x6, starting transfers between devices, along_line(): lax.ppermute(a, 'fsdp', [(i, i + 2 * step) for i in range(n) if 0 <= i +...  18.5 us
    pallas_call x1, Pallas kernels, outer(): pl.pallas_call(outer_kernel, grid=(2 * blocks,), in_specs=[pl.BlockSpec((...  16.6 us
  transfers between devices with their start and end apart: 20, of which 16 were waited for; matrix products, arithmetic and copies ran while one was open for 4% of the time, Pallas kernels for 33%

profile of v5, /device:TPU:0, one launch (start us, length us, event | category | flops | bytes accessed | tf_op | source)
XLA Modules:
  0.0 384.3 jit_solution(5551881069396828346)
XLA Ops:
  13.1 6.0 %collective-permute-start.2 = (bf16[128,768]{1,0:T(8,128)(2,1)S(1)}, bf16[128,768]{1,0:T(8,128)(2,1)S(1)}, u32[]{:S(2)}, u32[]{:S(2)}) collective-permute-start(bf16[128,768]{1,0:T(8,128)(2,1)S(1)} %dynamic-slice_bitcast_fusion.2), channel_id=1, source_target_pairs={{0,4},{1,5},{2,6},{3,7},{8,12},{9,13},{10,14},{11,15},{16,20},{17,... | collective-permute-start | bytes 589832 | tf_op jit(solution)/shard_map/ppermute | solution.py:633
  19.1 7.2 %collective-permute-done.1 = bf16[128,768]{1,0:T(8,128)(2,1)S(1)} collective-permute-done((bf16[128,768]{1,0:T(8,128)(2,1)S(1)}, bf16[128,768]{1,0:T(8,128)(2,1)S(1)}, u32[]{:S(2)}, u32[]{:S(2)}) %collective-permute-start.1) | collective-permute-done | bytes 196640 | tf_op jit(solution)/shard_map/ppermute | solution.py:633
  26.3 7.4 %collective-permute-start = (bf16[128,768]{1,0:T(8,128)(2,1)S(1)}, bf16[128,768]{1,0:T(8,128)(2,1)S(1)}, u32[]{:S(2)}, u32[]{:S(2)}) collective-permute-start(bf16[128,768]{1,0:T(8,128)(2,1)S(1)} %dynamic-slice_bitcast_fusion.2), channel_id=1, source_target_pairs={{0,6},{1,7},{8,14},{9,15},{16,22},{17,23},{24,30},{25,31}} | collective-permute-start | bytes 589832 | tf_op jit(solution)/shard_map/ppermute | solution.py:633
  37.6 1.7 collective-permute-done
  39.4 7.5 %collective-permute-done.3 = bf16[128,768]{1,0:T(8,128)(2,1)S(1)} collective-permute-done((bf16[128,768]{1,0:T(8,128)(2,1)S(1)}, bf16[128,768]{1,0:T(8,128)(2,1)S(1)}, u32[]{:S(2)}, u32[]{:S(2)}) %collective-permute-start.3) | collective-permute-done | bytes 196640 | tf_op jit(solution)/shard_map/ppermute | solution.py:633
  46.9 10.8 %collective-permute-done.4 = bf16[128,768]{1,0:T(8,128)(2,1)S(1)} collective-permute-done((bf16[128,768]{1,0:T(8,128)(2,1)S(1)}, bf16[128,768]{1,0:T(8,128)(2,1)S(1)}, u32[]{:S(2)}, u32[]{:S(2)}) %collective-permute-start.4) | collective-permute-done | bytes 196640 | tf_op jit(solution)/shard_map/ppermute | solution.py:633
  57.8 2.5 collective-permute-start.8
  61.9 3.0 collective-permute-done.8
  65.1 2.5 collective-permute-start.9
  67.6 2.7 collective-permute-done.6
  70.5 8.7 %collective-permute-done.9 = bf16[2,3,128,384]{3,2,0,1:T(8,128)(2,1)S(1)} collective-permute-done((bf16[2,3,128,384]{3,2,0,1:T(8,128)(2,1)S(1)}, bf16[2,3,128,384]{3,2,0,1:T(8,128)(2,1)S(1)}, u32[]{:S(2)}, u32[]{:S(2)}) %collective-permute-start.9) | collective-permute-done | bytes 589856 | tf_op jit(solution)/shard_map/ppermute | solution.py:641
  82.2 5.8 %collective-permute-done.10.refs_4_.refs_6_.refs_8_.refs_10_.w_q2_ref.w_k2_ref.w_v2_ref.refs_9_.refs_11_.refs_13_.refs_15_ = bf16[4,4,128,768]{3,2,1,0:T(8,128)(2,1)} collective-permute-done((bf16[4,4,128,768]{3,2,1,0:T(8,128)(2,1)S(1)}, bf16[4,4,128,768]{3,2,1,0:T(8,128)(2,1)}, u32[]{:S(2)}, u32[]{:S(2)}) %collective-permute-start.10) | collective-permute-done | bytes 3145760 | tf_op jit(solution)/shard_map/ppermute | solution.py:622
  90.8 14.9 %shard_map.401 = (bf16[1024,768]{1,0:T(8,128)(2,1)}, bf16[1024,768]{1,0:T(8,128)(2,1)}, bf16[1024,768]{1,0:T(8,128)(2,1)}, bf16[1024,768]{1,0:T(8,128)(2,1)}, bf...) custom-call(s32[2]{0:T(128)} %bitcast.108, ...), custom_call_target="tpu_custom_call" | custom-call | flops 7247757312 | bytes 16121856 | tf_op jit(solution)/shard_map/pallas_call | solution.py:295
  105.7 31.5 %shard_map.402 = (bf16[768,1024]{1,0:T(8,128)(2,1)}, bf16[2,12,512,512]{3,2,1,0:T(8,128)(2,1)}, f32[2,6,2,512]{3,2,1,0:T(2,128)}) custom-call(s32[2]{0:T(128)} %bitcast.121, bf16[1024,768]{1,0:T(8,128)(2,1)} %get-tuple-element.55.q_ref, bf16[1024,768]{1,0:T(8,128)(2,1)} %get-tuple-element.56.k_ref, bf16[1024,768]{1,0:T(8,128)(2,1)} %get-tuple-element.57.v_ref, ...), custom_call_target="tpu_custom_call" | custom-call | flops 9663676416 | bytes 12582912 | tf_op jit(solution)/shard_map/pallas_call | solution.py:86
  137.2 2.6 all-gather.6.cloned.1.call-done.refs_8_
  139.8 42.6 %shard_map.403 = (bf16[1024,768]{1,0:T(8,128)(2,1)}, bf16[1024,768]{1,0:T(8,128)(2,1)}, bf16[1024,3072]{1,0:T(8,128)(2,1)}, bf16[1024,768]{1,0:T(8,128)(2,1)}, b...) custom-call(s32[2]{0:T(128)} %bitcast.109, ...), custom_call_target="tpu_custom_call" | custom-call | flops 21743271936 | bytes 34603008 | tf_op jit(solution)/shard_map/pallas_call | solution.py:548
  182.5 16.6 %shard_map.407 = bf16[8,8,96,768]{3,2,1,0:T(8,128)(2,1)} custom-call(bf16[1024,3072]{1,0:T(8,128)(2,1)} %get-tuple-element.81.active_ref, bf16[1024,768]{1,0:T(8,128)(2,1)} %get-tuple-element.82.grad_ffn_ref, bf16[1024,768]{1,0:T(8,128)(2,1)} %get-tuple-element.83.hidden_ref, bf16[1024,3072]{1,0:T(8,128)(2,1)} %get-tuple-element.84.grad_raised_ref), custom_call_target="tpu_custom_call" | custom-call | flops 9663676416 | bytes 22020096 | tf_op jit(solution)/shard_map/pallas_call | solution.py:602
  199.1 50.6 %shard_map.404 = (bf16[1024,768]{1,0:T(8,128)(2,1)}, bf16[1024,768]{1,0:T(8,128)(2,1)}, bf16[1024,768]{1,0:T(8,128)(2,1)}, bf16[768,1024]{1,0:T(8,128)(2,1)}, bf16[768,1024]{1,0:T(8,128)(2,1)}) custom-call(bf16[1024,768]{1,0:T(8,128)(2,1)} %get-tuple-element.55.q_ref, bf16[1024,768]{1,0:T(8,128)(2,1)} %get-tuple-element.56.k_ref, ...), custom_call_target="tpu_custom_call" | custom-call | flops 19327352832 | bytes 12582912 | tf_op jit(solution)/shard_map/pallas_call | solution.py:187
  249.7 20.2 %shard_map.406 = (bf16[4,4,128,768]{3,2,1,0:T(8,128)(2,1)}, bf16[4,4,128,768]{3,2,1,0:T(8,128)(2,1)}) custom-call(s32[2]{0:T(128)} %bitcast.110, s32[1]{0:T(128)} %bitcast.1.refs_1_.core_ref, bf16[1024,768]{1,0:T(8,128)(2,1)} %get-tuple-element.73.refs_2_, bf16[1024,768]{1,0:T(8,128)(2,1)} %get-tuple-element.69.dq_ref.refs_3_, ...), custom_call_target="tpu_custom_call" | custom-call | flops 10468982784 | bytes 23986176 | tf_op jit(solution)/shard_map/pallas_call | solution.py:415
  270.2 5.7 %collective-permute-done.11 = bf16[4,4,128,768]{3,2,1,0:T(8,128)(2,1)S(1)} collective-permute-done((bf16[4,4,128,768]{3,2,1,0:T(8,128)(2,1)}, bf16[4,4,128,768]{3,2,1,0:T(8,128)(2,1)S(1)}, u32[]{:S(2)}, u32[]{:S(2)}) %collective-permute-start.11) | collective-permute-done | bytes 3145760 | tf_op jit(solution)/shard_map/ppermute | solution.py:622
  275.9 4.6 %add_convert_fusion = bf16[4,4,128,768]{3,2,1,0:T(8,128)(2,1)} fusion(bf16[4,4,128,768]{3,2,1,0:T(8,128)(2,1)S(1)} %collective-permute-done.11, bf16[4,4,128,768]{3,2,1,0:T(8,128)(2,1)} %get-tuple-element.79), kind=kLoop, calls=%fused_computation | loop fusion | flops 6291456 | bytes 9437184 | tf_op jit(solution)/shard_map/convert_element_type | solution.py:780
  280.5 3.7 all-to-all-start
  284.2 13.3 %reduce-scatter.3.cloned.1.call-done = bf16[8,96,768]{2,1,0:T(8,128)(2,1)} async-done(((bf16[8,768,768]{2,1,0:T(8,128)(2,1)}), bf16[8,96,768]{2,1,0:T(8,128)(2,1)}) %reduce-scatter.3.cloned.1.call-update) | async-done | bytes 1179664 | tf_op jit(solution)/shard_map/reduce_scatter | solution.py:761
  297.6 29.7 %all-to-all-done = bf16[4,4,128,768]{3,2,1,0:T(8,128)(2,1)S(1)} async-done(((bf16[4,4,128,768]{3,2,1,0:T(8,128)(2,1)}), bf16[4,4,128,768]{3,2,1,0:T(8,128)(2,1)S(1)}, u32[]{:S(2)}, u32[]{:S(2)}) %all-to-all-start) | async-done | bytes 3145760 | tf_op jit(solution)/shard_map/all_to_all | solution.py:637
  327.2 1.6 reduce_sum.24
  328.8 3.6 all-to-all-start.1
  332.5 5.3 %reduce-scatter.5.cloned.1.call-done = bf16[192,768]{1,0:T(8,128)(2,1)} async-done(((bf16[768,768]{1,0:T(8,128)(2,1)}), bf16[192,768]{1,0:T(8,128)(2,1)}) %reduce-scatter.5.cloned.1.call-update) | async-done | bytes 294928 | tf_op jit(solution)/shard_map/reduce_scatter | solution.py:781
  337.8 8.2 %shard_map.405 = bf16[1024,768]{1,0:T(8,128)(2,1)} custom-call(s32[1]{0:T(128)} %bitcast.1.refs_1_.core_ref, bf16[1024,768]{1,0:T(8,128)(2,1)} %get-tuple-element.69.dq_ref.refs_3_, bf16[1024,768]{1,0:T(8,128)(2,1)} %get-tuple-element.70.dk_ref.refs_4_, bf16[1024,768]{1,0:T(8,128)(2,1)} %get-tuple-element.71.dv_ref.refs_5_, ...), custom_call_target="tpu_custom_call" | custom-call | flops 3623878656 | bytes 12976128 | tf_op jit(solution)/shard_map/pallas_call | solution.py:448
  346.0 6.2 %all-to-all-done.1 = bf16[4,128,768]{2,1,0:T(8,128)(2,1)S(1)} async-done(((bf16[4,128,768]{2,1,0:T(8,128)(2,1)}), bf16[4,128,768]{2,1,0:T(8,128)(2,1)S(1)}, u32[]{:S(2)}, u32[]{:S(2)}) %all-to-all-start.1) | async-done | bytes 786464 | tf_op jit(solution)/shard_map/all_to_all | solution.py:628
  353.3 3.5 all-to-all-start.2
  358.7 13.7 %all-to-all-done.2 = bf16[4,112,768]{2,1,0:T(8,128)(2,1)S(1)} async-done(((bf16[4,112,768]{2,1,0:T(8,128)(2,1)}), bf16[4,112,768]{2,1,0:T(8,128)(2,1)S(1)}, u32[]{:S(2)}, u32[]{:S(2)}) %all-to-all-start.2) | async-done | bytes 688160 | tf_op jit(solution)/shard_map/all_to_all | solution.py:637
  374.2 2.4 slice_convert_fusion
  (77 shorter events, 24.1 us)
Async XLA Ops:
  7.2 130.0 %all-gather.4.cloned.1.call-start = ((), (), s32[]{:S(2)}) async-start(), calls=%async_computation.5 | async-start | bytes 5308416 | tf_op jit(solution)/shard_map/all_gather | solution.py:726
  10.9 0.9 copy-start.1
  11.8 14.4 %collective-permute-start.1 = (bf16[128,768]{1,0:T(8,128)(2,1)S(1)}, bf16[128,768]{1,0:T(8,128)(2,1)S(1)}, u32[]{:S(2)}, u32[]{:S(2)}) collective-permute-start(bf16[128,768]{1,0:T(8,128)(2,1)S(1)} %dynamic-slice_bitcast_fusion.2), channel_id=1, source_target_pairs={{4,0},{5,1},{6,2},{7,3},{12,8},{13,9},{14,10},{15,11},{20,16},{21,... | collective-permute-start | bytes 589832 | tf_op jit(solution)/shard_map/ppermute | solution.py:633
  13.1 13.1 %collective-permute-start.2 = (bf16[128,768]{1,0:T(8,128)(2,1)S(1)}, bf16[128,768]{1,0:T(8,128)(2,1)S(1)}, u32[]{:S(2)}, u32[]{:S(2)}) collective-permute-start(bf16[128,768]{1,0:T(8,128)(2,1)S(1)} %dynamic-slice_bitcast_fusion.2), channel_id=1, source_target_pairs={{0,4},{1,5},{2,6},{3,7},{8,12},{9,13},{10,14},{11,15},{16,20},{17,... | collective-permute-start | bytes 589832 | tf_op jit(solution)/shard_map/ppermute | solution.py:633
  26.2 113.6 %all-gather.6.cloned.1.call-start = ((), (), s32[]{:S(2)}) async-start(), calls=%async_computation.6 | async-start | bytes 5308416 | tf_op jit(solution)/shard_map/all_gather | solution.py:727
  26.3 13.0 %collective-permute-start = (bf16[128,768]{1,0:T(8,128)(2,1)S(1)}, bf16[128,768]{1,0:T(8,128)(2,1)S(1)}, u32[]{:S(2)}, u32[]{:S(2)}) collective-permute-start(bf16[128,768]{1,0:T(8,128)(2,1)S(1)} %dynamic-slice_bitcast_fusion.2), channel_id=1, source_target_pairs={{0,6},{1,7},{8,14},{9,15},{16,22},{17,23},{24,30},{25,31}} | collective-permute-start | bytes 589832 | tf_op jit(solution)/shard_map/ppermute | solution.py:633
  33.7 13.2 %collective-permute-start.3 = (bf16[128,768]{1,0:T(8,128)(2,1)S(1)}, bf16[128,768]{1,0:T(8,128)(2,1)S(1)}, u32[]{:S(2)}, u32[]{:S(2)}) collective-permute-start(bf16[128,768]{1,0:T(8,128)(2,1)S(1)} %dynamic-slice_bitcast_fusion.2), channel_id=1, source_target_pairs={{0,2},{1,3},{2,4},{3,5},{4,6},{5,7},{8,10},{9,11},{10,12},{11,13},... | collective-permute-start | bytes 589832 | tf_op jit(solution)/shard_map/ppermute | solution.py:633
  35.0 22.7 %collective-permute-start.4 = (bf16[128,768]{1,0:T(8,128)(2,1)S(1)}, bf16[128,768]{1,0:T(8,128)(2,1)S(1)}, u32[]{:S(2)}, u32[]{:S(2)}) collective-permute-start(bf16[128,768]{1,0:T(8,128)(2,1)S(1)} %dynamic-slice_bitcast_fusion.2), channel_id=1, source_target_pairs={{2,0},{3,1},{4,2},{5,3},{6,4},{7,5},{10,8},{11,9},{12,10},{13,11},... | collective-permute-start | bytes 589832 | tf_op jit(solution)/shard_map/ppermute | solution.py:633
  36.3 21.4 %collective-permute-start.5 = (bf16[128,768]{1,0:T(8,128)(2,1)S(1)}, bf16[128,768]{1,0:T(8,128)(2,1)S(1)}, u32[]{:S(2)}, u32[]{:S(2)}) collective-permute-start(bf16[128,768]{1,0:T(8,128)(2,1)S(1)} %dynamic-slice_bitcast_fusion.2), channel_id=1, source_target_pairs={{6,0},{7,1},{14,8},{15,9},{22,16},{23,17},{30,24},{31,25}} | collective-permute-start | bytes 589832 | tf_op jit(solution)/shard_map/ppermute | solution.py:633
  57.8 7.2 %collective-permute-start.8 = (bf16[1,3,128,384]{3,2,0,1:T(8,128)(2,1)S(1)}, bf16[1,3,128,384]{3,2,0,1:T(8,128)(2,1)S(1)}, u32[]{:S(2)}, u32[]{:S(2)}) collective-permute-start(bf16[1,3,128,384]{3,2,0,1:T(8,128)(2,1)S(1)} %get-tuple-element.137), channel_id=1, source_target_pairs={{0,16},{8,24},{16,0},{24,8},{1,17},{9,25},{17,1},{25,9},{2,18},{10... | collective-permute-start | bytes 884744 | tf_op jit(solution)/shard_map/ppermute | solution.py:641
  60.3 237.3 %reduce-scatter.3.cloned.1.call-start = ((), (), s32[]{:S(2)}) async-start(), calls=%async_computation.7 | async-start | bytes 10616832 | tf_op jit(solution)/shard_map/reduce_scatter | solution.py:761
  60.4 9.9 %collective-permute-start.6 = (bf16[1,3,128,384]{3,2,1,0:T(8,128)(2,1)S(1)}, bf16[1,3,128,384]{3,2,1,0:T(8,128)(2,1)S(1)}, u32[]{:S(2)}, u32[]{:S(2)}) collective-permute-start(bf16[1,3,128,384]{3,2,1,0:T(8,128)(2,1)S(1)} %get-tuple-element.136), channel_id=1, source_target_pairs={{0,8},{8,0},{16,24},{24,16},{1,9},{9,1},{17,25},{25,17},{2,10},{10... | collective-permute-start | bytes 884744 | tf_op jit(solution)/shard_map/ppermute | solution.py:641
  65.1 14.1 %collective-permute-start.9 = (bf16[2,3,128,384]{3,2,0,1:T(8,128)(2,1)S(1)}, bf16[2,3,128,384]{3,2,0,1:T(8,128)(2,1)S(1)}, u32[]{:S(2)}, u32[]{:S(2)}) collective-permute-start(bf16[2,3,128,384]{3,2,0,1:T(8,128)(2,1)S(1)} %pad_maximum_fusion.3), channel_id=1, source_target_pairs={{0,8},{8,0},{16,24},{24,16},{1,9},{9,1},{17,25},{25,17},{2,10},{10... | collective-permute-start | bytes 1769480 | tf_op jit(solution)/shard_map/ppermute | solution.py:641
  70.4 9.9 %collective-permute-start.7 = (bf16[2,3,128,384]{3,2,1,0:T(8,128)(2,1)S(1)}, bf16[2,3,128,384]{3,2,1,0:T(8,128)(2,1)S(1)}, u32[]{:S(2)}, u32[]{:S(2)}) collective-permute-start(bf16[2,3,128,384]{3,2,1,0:T(8,128)(2,1)S(1)} %pad_maximum_fusion.2), channel_id=1, source_target_pairs={{0,16},{8,24},{16,0},{24,8},{1,17},{9,25},{17,1},{25,9},{2,18},{10... | collective-permute-start | bytes 1769480 | tf_op jit(solution)/shard_map/ppermute | solution.py:641
  80.5 1.1 copy-start.2
  82.1 5.9 %copy-start = (bf16[4,4,128,768]{3,2,1,0:T(8,128)(2,1)}, bf16[4,4,128,768]{3,2,1,0:T(8,128)(2,1)S(1)}, u32[]{:S(2)}) copy-start(bf16[4,4,128,768]{3,2,1,0:T(8,128)(2,1)S(1)} %select_select_fusion.refs_3_.refs_5_.refs_7_.refs_9_.w_q_ref.w_k_ref.w_v_ref.refs_8_.refs_10_.refs_12_.refs_14_) | copy-start | bytes 9437188
  82.1 5.9 %collective-permute-start.10 = (bf16[4,4,128,768]{3,2,1,0:T(8,128)(2,1)S(1)}, bf16[4,4,128,768]{3,2,1,0:T(8,128)(2,1)}, u32[]{:S(2)}, u32[]{:S(2)}) collective-permute-start(bf16[4,4,128,768]{3,2,1,0:T(8,128)(2,1)S(1)} %select_select_fusion.refs_3_.refs_5_.refs_7_.refs_9_.w_q_ref.w_k_ref.w_v_ref.refs_8_.refs_, ...), channel_id=1, source_target_pairs={{0,1},{1,0},{2,3},{3,2},{4,5},{5,4},{6,7},{7,6},{8,9},{9,8},{10,11... | collective-permute-start | bytes 9437192 | tf_op jit(solution)/shard_map/ppermute | solution.py:622
  270.0 5.9 %collective-permute-start.11 = (bf16[4,4,128,768]{3,2,1,0:T(8,128)(2,1)}, bf16[4,4,128,768]{3,2,1,0:T(8,128)(2,1)S(1)}, u32[]{:S(2)}, u32[]{:S(2)}) collective-permute-start(bf16[4,4,128,768]{3,2,1,0:T(8,128)(2,1)} %get-tuple-element.80), channel_id=1, source_target_pairs={{0,1},{1,0},{2,3},{3,2},{4,5},{5,4},{6,7},{7,6},{8,9},{9,8},{10,11... | collective-permute-start | bytes 9437192 | tf_op jit(solution)/shard_map/ppermute | solution.py:622
  280.5 46.8 %all-to-all-start = ((bf16[4,4,128,768]{3,2,1,0:T(8,128)(2,1)}), bf16[4,4,128,768]{3,2,1,0:T(8,128)(2,1)S(1)}, u32[]{:S(2)}, u32[]{:S(2)}) async-start(bf16[4,4,128,768]{3,2,1,0:T(8,128)(2,1)} %add_convert_fusion), calls=%async_computation | async-start | bytes 6291456 | tf_op jit(solution)/shard_map/all_to_all | solution.py:637
  284.2 53.6 %reduce-scatter.5.cloned.1.call-start = ((), (), s32[]{:S(2)}) async-start(), calls=%async_computation.8 | async-start | bytes 1474560 | tf_op jit(solution)/shard_map/reduce_scatter | solution.py:781
  328.8 23.4 %all-to-all-start.1 = ((bf16[4,128,768]{2,1,0:T(8,128)(2,1)}), bf16[4,128,768]{2,1,0:T(8,128)(2,1)S(1)}, u32[]{:S(2)}, u32[]{:S(2)}) async-start(bf16[4,128,768]{2,1,0:T(8,128)(2,1)} %reduce_sum.24), calls=%async_computation.1 | async-start | bytes 1572864 | tf_op jit(solution)/shard_map/all_to_all | solution.py:628
  332.4 41.8 %all-gather.8.cloned.1.call-start = ((), (), s32[]{:S(2)}) async-start(), calls=%async_computation.9 | async-start | bytes 1474560 | tf_op jit(solution)/shard_map/all_gather | solution.py:784
  353.3 19.0 %all-to-all-start.2 = ((bf16[4,112,768]{2,1,0:T(8,128)(2,1)}), bf16[4,112,768]{2,1,0:T(8,128)(2,1)S(1)}, u32[]{:S(2)}, u32[]{:S(2)}) async-start(bf16[4,112,768]{2,1,0:T(8,128)(2,1)} %broadcast_in_dim.50), calls=%async_computation.2 | async-start | bytes 1376256 | tf_op jit(solution)/shard_map/all_to_all | solution.py:637
Sparse Core Ops, SparseCore 0:
  26.4 61.9 all-gather.3
  90.0 49.7 all-gather.5
  199.2 98.2 reduce-scatter.2
  300.3 37.4 reduce-scatter.4
  339.5 33.1 all-gather.7
